TPU v7x, 128 devices: a whole 4x4x4 slice. The times are simulated.
128 devices in a mesh: rows: 128 (over y, x, z, core).
Axes of the slice: x: 4, y: 4, z: 4, core: 2. Of those that a mesh axis runs over, the one named last changes fastest.
Arguments:
- features: bfloat16 [16384, 256], P('rows'), may hold values from -6 to 6
- tile_values: bfloat16 [128, 16, 512, 512], P('rows'), may hold values from -0.0625 to 0.0625
- tile_col: int32 [128, 16], P('rows'), may hold values from 0 to 31, as said below
- tile_count: int32 [128], P('rows'), may hold values from 4 to 16, as said below
- weight: bfloat16 [256, 256], replicated, may hold values from -0.375 to 0.375
- bias: float32 [256], replicated, may hold values from -3 to 3
- cotangent: bfloat16 [65536, 256], P('rows'), may hold values from -6 to 6
Outputs:
- activation: bfloat16 [65536, 256], P('rows')
- grad_weight: float32 [256, 256], replicated
- grad_bias: float32 [256], replicated
- grad_features: float32 [16384, 256], P('rows')
Inputs may be any that keep to these rules, and one draw needn't show every extreme that they name: `tile_count`: each row block uses between 4 and 16 slots, and some row block uses all 16. `tile_col`: the 16 tile columns of one row block are distinct.
All inputs are finite; a program needn't handle non-finite values.
Results may differ from a plain program's by a relative error of at most 0.011.
Values may be sent and summed in bfloat16 or wider, within the bound.
No kernel may reach another device: no remote copies, remote signals or barrier semaphores. Data moves between devices by JAX's collectives and lax.ppermute only.
A program may use at most 128 MiB of HBM per device.

v0:
```python
import jax
import jax.numpy as jnp
from jax import lax
from jax.sharding import PartitionSpec as P


def elu_grad(pre):
    return jnp.where(pre > 0, 1.0, jnp.exp(jnp.minimum(pre, 0.0)))


def on_device(features, tile_values, tile_col, tile_count, weight, bias, cotangent):
    slots = tile_values.shape[1]
    tile = tile_values.shape[2]
    width = features.shape[1]
    gathered = lax.all_gather(features, "rows", axis=0, tiled=True)
    ctiles = gathered.shape[0] // tile
    blocks = gathered.reshape(ctiles, tile, width)
    values = tile_values[0]
    cols = tile_col[0]
    count = tile_count[0]
    slot_ids = jnp.arange(slots, dtype=jnp.int32)
    col_ids = jnp.arange(ctiles, dtype=jnp.int32)
    live = slot_ids < count
    chosen = jnp.where(live[:, None, None], blocks[cols], jnp.zeros((), jnp.bfloat16))
    agg = jnp.einsum("sij,sjh->ih", values, chosen, preferred_element_type=jnp.float32)
    agg = agg.astype(jnp.bfloat16)
    pre = jnp.dot(agg, weight, preferred_element_type=jnp.float32) + bias
    activation = jax.nn.elu(pre).astype(jnp.bfloat16)
    grad_pre = (cotangent.astype(jnp.float32) * elu_grad(pre)).astype(jnp.bfloat16)
    local_weight = lax.dot_general(
        agg, grad_pre, (((0,), (0,)), ((), ())), preferred_element_type=jnp.float32
    )
    local_bias = jnp.sum(grad_pre.astype(jnp.float32), axis=0)
    total_weight, total_bias = lax.psum((local_weight, local_bias), "rows")
    scale = (tile * lax.axis_size("rows")) ** (-0.5)
    grad_weight = total_weight * scale
    grad_bias = total_bias * scale
    live_f = (slot_ids < count).astype(jnp.float32)
    onehot = (cols[:, None] == col_ids[None, :]).astype(jnp.float32) * live_f[:, None]
    parts = jnp.einsum("sij,ih->sjh", values, grad_pre, preferred_element_type=jnp.float32)
    column_terms = jnp.einsum("sc,sjh->cjh", onehot, parts)
    column_terms = column_terms.reshape(ctiles * tile, width)
    back = lax.psum_scatter(column_terms, "rows", scatter_dimension=0, tiled=True)
    back = back.astype(jnp.bfloat16)
    grad_features = lax.dot_general(
        back, weight, (((1,), (1,)), ((), ())), preferred_element_type=jnp.float32
    )
    return (activation, grad_weight, grad_bias, grad_features)


def solution(mesh):
    in_specs = (
        P("rows", None),
        P("rows", None, None, None),
        P("rows", None),
        P("rows"),
        P(),
        P(),
        P("rows", None),
    )
    out_specs = (P("rows", None), P(), P(), P("rows", None))
    return jax.shard_map(
        on_device, mesh=mesh, in_specs=in_specs, out_specs=out_specs, check_vma=False
    )
```

profile of v0, /device:TPU:1, one launch (start us, length us, event | category | flops | bytes accessed | tf_op | source)
XLA Modules:
  0.0 906.0 jit_solution(17339060379736557651)
XLA Ops:
  7.2 0.0 copy-start
  7.2 0.0 all-gather.2.cloned.1.call-start
  7.2 0.7 all-gather.2.cloned.1.call-update
  7.9 0.0 all-reduce.2.cloned.1.call-start
  8.6 0.0 copy-start.3
  8.6 14.9 %copy.14 = bf16[16,512,512]{1,0,2:T(8,128)(2,1)} copy(bf16[16,512,512]{2,1,0:T(8,128)(2,1)} %bitcast.34) | data formatting | bytes 16777216 | tf_op jit(solution)/shard_map/squeeze | solution.py:18
  23.5 0.0 copy-done.3
  23.6 61.2 %all-gather.2.cloned.1.call-done = bf16[16384,256]{1,0:T(8,128)(2,1)} async-done(((bf16[128,256]{1,0:T(8,128)(2,1)}), bf16[16384,256]{1,0:T(8,128)(2,1)}) %all-gather.2.cloned.1.call-update) | async-done | bytes 8388624 | tf_op jit(solution)/shard_map/all_gather | solution.py:15
  84.8 6.1 gather_fusion
  90.9 0.0 copy-start.1
  90.9 0.0 copy-start.2
  90.9 7.7 fusion.11
  98.7 0.0 copy-done
  98.7 0.0 copy-done.1
  98.7 0.0 copy-done.2
  98.7 1.2 convert_reduce_fusion
  99.9 0.9 fusion.33
  100.8 0.0 all-reduce.2.cloned.1.call-update
  100.9 0.0 reduce-scatter.2.cloned.1.call-start
  100.9 12.5 %fusion = f32[32,512,256]{2,0,1:T(8,128)} fusion(bf16[16,512,512]{1,0,2:T(8,128)(2,1)} %copy.14, bf16[512,256]{1,0:T(8,128)(2,1)S(1)} %get-tuple-element.5, bf16[16]{0:T(256)(128)(2,1)S(1)} %fusion.31, s32[16]{0:T(128)S(1)} %bitcast.36), kind=kOutput, calls=%fused_computation.1 | convolution fusion | flops 2281702400 | bytes 25428064 | tf_op jit(solution)/shard_map/sc,sjh->cjh/dot_general | solution.py:41
  113.4 15.8 %copy.12 = f32[32,512,256]{2,1,0:T(8,128)} copy(f32[32,512,256]{2,0,1:T(8,128)} %fusion) | data formatting | bytes 33554432 | tf_op jit(solution)/shard_map/sc,sjh->cjh/dot_general | solution.py:41
  129.3 0.0 reduce-scatter.2.cloned.1.call-update
  129.3 63.0 %psum.15 = f32[256]{0:T(256)S(1)} all-reduce(f32[256]{0:T(256)S(1)} %get-tuple-element.4), channel_id=1, replica_groups=mesh['rows'=128] {'rows'}, use_global_device_ids=true, to_apply=%region_2.3 | all-reduce | flops 256 | bytes 2048 | tf_op jit(solution)/shard_map/psum | solution.py:34
  192.3 0.6 broadcast_multiply_fusion.1
  192.8 46.8 %all-reduce.2.cloned.1.call-done = f32[256,256]{1,0:T(8,128)} async-done(((f32[256,256]{1,0:T(8,128)}), f32[256,256]{1,0:T(8,128)}) %all-reduce.2.cloned.1.call-update) | async-done | bytes 262160 | tf_op jit(solution)/shard_map/psum | solution.py:34
  239.7 1.7 broadcast_multiply_fusion
  241.3 656.3 %reduce-scatter.2.cloned.1.call-done = f32[128,256]{1,0:T(8,128)} async-done(((f32[16384,256]{1,0:T(8,128)}), f32[128,256]{1,0:T(8,128)}) %reduce-scatter.2.cloned.1.call-update) | async-done | bytes 131088 | tf_op jit(solution)/shard_map/reduce_scatter | solution.py:43
  897.7 1.8 fusion.20
  (4 shorter events, 0.0 us)
Async XLA Ops:
  7.2 91.5 %copy-start = (bf16[256,256]{1,0:T(8,128)(2,1)S(1)}, bf16[256,256]{1,0:T(8,128)(2,1)}, u32[]{:S(2)}) copy-start(bf16[256,256]{1,0:T(8,128)(2,1)} %param.11) | copy-start | bytes 393220
  7.2 77.6 %all-gather.2.cloned.1.call-start = ((), (), s32[]{:S(2)}) async-start(), calls=%async_computation.1 | async-start | bytes 8454144 | tf_op jit(solution)/shard_map/all_gather | solution.py:15
  7.9 231.8 %all-reduce.2.cloned.1.call-start = ((), (), s32[]{:S(2)}) async-start(), calls=%async_computation.2 | async-start | bytes 524288 | tf_op jit(solution)/shard_map/psum | solution.py:34
  8.6 14.9 %copy-start.3 = (s32[1,16]{1,0:T(1,128)S(1)}, s32[1,16]{1,0:T(1,128)}, u32[]{:S(2)}) copy-start(s32[1,16]{1,0:T(1,128)} %param.9) | copy-start | bytes 196
  90.9 7.8 copy-start.1
  90.9 7.8 copy-start.2
  100.9 796.8 %reduce-scatter.2.cloned.1.call-start = ((), (), s32[]{:S(2)}) async-start(), calls=%async_computation.3 | async-start | bytes 16908288 | tf_op jit(solution)/shard_map/reduce_scatter | solution.py:43
Sparse Core Ops, SparseCore 0:
  11.0 73.7 all-gather.1
  101.0 138.6 all-reduce.1
  242.1 655.5 reduce-scatter.1
where the time goes:
time: 913 us; the launch traced here: 906 us
  waiting for transfers between devices  765 us (84%)
  blocking collectives  63 us (7%)
  local copies, waits for them, and re-layouts  36.9 us (4%)
  matrix products  24.1 us (3%)
  between operations  14.5 us (2%)
    reduce_scatter x1, waiting for transfers between devices, on_device(): lax.psum_scatter(column_terms, 'rows', scatter_dimension=0, tiled=True)  656 us
    psum x1, blocking collectives, on_device(): total_weight, total_bias = lax.psum((local_weight, local_bias), 'rows')  63 us
    all_gather x1, waiting for transfers between devices, on_device(): gathered = lax.all_gather(features, 'rows', axis=0, tiled=True)  61.2 us
    psum x1, waiting for transfers between devices, on_device(): total_weight, total_bias = lax.psum((local_weight, local_bias), 'rows')  46.8 us
  transfers between devices with their start and end apart: 3, of which 3 were waited for; matrix products, arithmetic and copies ran while one was open for 5% of the time, Pallas kernels for 0%

commit v1 on v0

v1 whole, which is shorter than its diff:
```python
import functools

import jax
import jax.numpy as jnp
import numpy as np
from jax import lax
from jax.experimental import pallas as pl
from jax.experimental.pallas import tpu as pltpu
from jax.sharding import PartitionSpec as P

AXIS = "rows"
SIZES = (4, 4, 4, 2)
Y, X, Z = 0, 1, 2
ORDERS = ((X, Y, Z), (Y, Z, X))
BF16 = jnp.bfloat16
F32 = jnp.float32
EXTRA = 272


def pairs(move):
    out = []
    for i in range(128):
        to = move([int(v) for v in np.unravel_index(i, SIZES)])
        to = [t % n for t, n in zip(to, SIZES)]
        out.append((i, int(np.ravel_multi_index(to, SIZES))))
    return out


def hop(x, phase, k):
    def move(at):
        at[ORDERS[at[3]][phase]] += k
        return at

    return lax.ppermute(x, AXIS, pairs(move))


def swap(x):
    def move(at):
        at[3] += 1
        return at

    return lax.ppermute(x, AXIS, pairs(move))


def dot(a, b, dims):
    return lax.dot_general(a, b, (dims, ((), ())), preferred_element_type=F32)


def split3(v):
    hi = v.astype(BF16)
    rest = v - hi.astype(F32)
    mid = rest.astype(BF16)
    low = (rest - mid.astype(F32)).astype(BF16)
    return hi, mid, low


def kernel(
    s_ref, a_hbm, mine, theirs, w_hbm, b_hbm, cot_hbm,
    act_hbm, rm_hbm, rt_hbm, em_hbm, et_hbm,
    a_buf, x_buf, acc, w_v, b_v, cot_v, act_v, g_t, out_buf, extra, zero, flags,
    sem_a, sem_x, sem_in, sem_o, sem_e, sem_act,
):
    count = s_ref[16]
    me = (s_ref[17], s_ref[18], s_ref[19])
    core = s_ref[20]

    def place(t, zlo, cc, sign):
        there = (lax.shift_right_logical(t, 3), lax.shift_right_logical(t, 1) & 3, (t & 1) * 2 + zlo)
        k = [((me[i] - there[i]) * sign) & 3 for i in range(3)]
        o = ORDERS[cc]
        return k[o[2]], k[o[1]] * 4 + k[o[0]]

    inputs = ((w_hbm, w_v), (b_hbm, b_v), (cot_hbm, cot_v))

    def load(s, carry):
        t = s_ref[s]
        for j in range(4):
            cc = j % 2
            k3, k21 = place(t, j // 2, cc, 1)
            to = x_buf.at[s, pl.ds(j * 128, 128)]

            @pl.when(core == cc)
            def _():
                pltpu.make_async_copy(mine.at[k3 * 16 + k21], to, sem_x.at[s, j]).start()

            @pl.when(core != cc)
            def _():
                pltpu.make_async_copy(theirs.at[k3 * 16 + k21], to, sem_x.at[s, j]).start()

        pltpu.make_async_copy(a_hbm.at[s], a_buf.at[s], sem_a.at[s]).start()
        return carry

    lax.fori_loop(0, count, load, 0)
    for i, (src, dst) in enumerate(inputs):
        pltpu.make_async_copy(src, dst, sem_in.at[i]).start()

    def send(src, t, j):
        cc = j % 2
        k3, k21 = place(t, j // 2, cc, -1)
        rows = pl.ds(k21 * 256, 256)

        @pl.when(core == cc)
        def _():
            pltpu.make_async_copy(src, rm_hbm.at[k3, rows], sem_o.at[t, j]).start()

        @pl.when(core != cc)
        def _():
            pltpu.make_async_copy(src, rt_hbm.at[k3, rows], sem_o.at[t, j]).start()

    zero[...] = jnp.zeros_like(zero)
    for t in range(32):
        flags[t] = 0

    def mark(s, carry):
        flags[s_ref[s]] = 1
        return carry

    lax.fori_loop(0, count, mark, 0)

    def clear(t, carry):
        @pl.when(flags[t] == 0)
        def _():
            for j in range(4):
                send(zero, t, j)

        return carry

    lax.fori_loop(0, 32, clear, 0)

    acc[...] = jnp.zeros_like(acc)

    def forward(s, carry):
        pltpu.make_async_copy(a_hbm.at[s], a_buf.at[s], sem_a.at[s]).wait()
        for j in range(4):
            to = x_buf.at[s, pl.ds(j * 128, 128)]
            pltpu.make_async_copy(mine.at[0], to, sem_x.at[s, j]).wait()
        acc[...] += dot(a_buf[s], x_buf[s], ((1,), (0,)))
        return carry

    lax.fori_loop(0, count, forward, 0)
    for i, (src, dst) in enumerate(inputs):
        pltpu.make_async_copy(src, dst, sem_in.at[i]).wait()

    agg = acc[...].astype(BF16)
    pre = dot(agg, w_v[...], ((1,), (0,))) + b_v[...]
    low = jnp.exp(jnp.minimum(pre, 0.0))
    act_v[...] = jnp.where(pre > 0, pre, low - 1.0).astype(BF16)
    act_copy = pltpu.make_async_copy(act_v, act_hbm, sem_act)
    act_copy.start()
    grad = (cot_v[...].astype(F32) * low).astype(BF16)
    g_t[...] = grad.astype(F32).T.astype(BF16)
    dw = dot(agg, grad, ((0,), (0,)))
    db = jnp.sum(grad.astype(F32), axis=0, keepdims=True)
    for h in range(2):
        half = slice(h * 128, h * 128 + 128)
        extra[h, :256, :] = dw[:, half].astype(BF16)
        row = lax.broadcasted_iota(jnp.int32, (16, 128), 0)
        hi, mid, low3 = [p.astype(F32) for p in split3(db[:, half])]
        parts = jnp.where(row == 0, hi, jnp.where(row == 1, mid, jnp.where(row == 2, low3, 0.0)))
        extra[h, 256:, :] = parts.astype(BF16)
    pltpu.make_async_copy(extra.at[core], em_hbm, sem_e.at[0]).start()
    pltpu.make_async_copy(extra.at[1 - core], et_hbm, sem_e.at[1]).start()

    def backward(s, carry):
        part = dot(g_t[...], a_buf[s], ((1,), (0,))).astype(BF16)
        for j in range(4):
            out_buf[s, j] = part[:, j * 128 : j * 128 + 128]
        for j in range(4):
            send(out_buf.at[s, j], s_ref[s], j)
        return carry

    lax.fori_loop(0, count, backward, 0)

    def finish(t, carry):
        for j in range(4):
            pltpu.make_async_copy(zero, rm_hbm.at[0, pl.ds(0, 256)], sem_o.at[t, j]).wait()
        return carry

    lax.fori_loop(0, 32, finish, 0)
    pltpu.make_async_copy(extra.at[0], em_hbm, sem_e.at[0]).wait()
    pltpu.make_async_copy(extra.at[1], et_hbm, sem_e.at[1]).wait()
    act_copy.wait()


def local(scalars, values, mine, theirs, weight, bias, cotangent):
    anywhere = pl.BlockSpec(memory_space=pl.ANY)
    return pl.pallas_call(
        kernel,
        out_shape=(
            jax.ShapeDtypeStruct((512, 256), BF16),
            jax.ShapeDtypeStruct((4, 4096, 128), BF16),
            jax.ShapeDtypeStruct((4, 4096, 128), BF16),
            jax.ShapeDtypeStruct((EXTRA, 128), BF16),
            jax.ShapeDtypeStruct((EXTRA, 128), BF16),
        ),
        in_specs=[pl.BlockSpec(memory_space=pltpu.SMEM)] + [anywhere] * 6,
        out_specs=(anywhere,) * 5,
        scratch_shapes=[
            pltpu.VMEM((16, 512, 512), BF16),
            pltpu.VMEM((16, 512, 256), BF16),
            pltpu.VMEM((512, 256), F32),
            pltpu.VMEM((256, 256), BF16),
            pltpu.VMEM((1, 256), F32),
            pltpu.VMEM((512, 256), BF16),
            pltpu.VMEM((512, 256), BF16),
            pltpu.VMEM((256, 512), BF16),
            pltpu.VMEM((16, 4, 256, 128), BF16),
            pltpu.VMEM((2, EXTRA, 128), BF16),
            pltpu.VMEM((256, 128), BF16),
            pltpu.SMEM((32,), jnp.int32),
            pltpu.SemaphoreType.DMA((16,)),
            pltpu.SemaphoreType.DMA((16, 4)),
            pltpu.SemaphoreType.DMA((3,)),
            pltpu.SemaphoreType.DMA((32, 4)),
            pltpu.SemaphoreType.DMA((2,)),
            pltpu.SemaphoreType.DMA,
        ],
        compiler_params=pltpu.CompilerParams(vmem_limit_bytes=28 * 1024 * 1024),
        cost_estimate=pl.CostEstimate(
            flops=2 * 2 * 16 * 512 * 512 * 256, bytes_accessed=32 * 2**20, transcendentals=512 * 256
        ),
        name="layer",
    )(scalars, values, mine, theirs, weight, bias, cotangent)


def add_up(parts):
    total = parts[0].astype(F32)
    for part in parts[1:]:
        total = total + part.astype(F32)
    return total


def exact_rows(total):
    db = total[256] + total[257] + total[258]
    hi = lax.reduce_precision(db, 8, 7)
    mid = lax.reduce_precision(db - hi, 8, 7)
    low = db - hi - mid
    row = lax.broadcasted_iota(jnp.int32, (16, 128), 0)
    bias = jnp.where(row == 0, hi, jnp.where(row == 1, mid, jnp.where(row == 2, low, 0.0)))
    return jnp.concatenate([total[:256], bias]).astype(BF16)


def on_device(features, tile_values, tile_col, tile_count, weight, bias, cotangent):
    me = lax.axis_index(AXIS)
    core = me & 1
    coords = jnp.stack([me >> 5, (me >> 3) & 3, (me >> 1) & 3, core]).astype(jnp.int32)
    scalars = jnp.concatenate([tile_col[0], tile_count, coords])

    held = features[None]
    for phase in range(2):
        held = jnp.concatenate([held] + [hop(held, phase, k) for k in (1, 2, 3)])
    got = [held] + [hop(held, 2, k) for k in (1, 2, 3)]
    mine = jnp.concatenate(got)
    theirs = jnp.concatenate([swap(g) for g in got])

    activation, r_mine, r_theirs, e_mine, e_theirs = local(
        scalars, tile_values[0], mine, theirs, weight, bias[None], cotangent
    )

    ride = exact_rows(add_up([e_mine, swap(e_theirs)]))
    terms = [None] * 4
    for k in (1, 3, 2, 0):
        body = add_up([r_mine[k], swap(r_theirs[k])]).astype(BF16)
        terms[k] = jnp.concatenate([body, ride])
    total = add_up([terms[0]] + [hop(terms[k], 2, k) for k in (1, 3, 2)])
    for phase in (1, 0):
        ride = exact_rows(total[-EXTRA:])
        rows = (total.shape[0] - EXTRA) // 4
        body = total[:-EXTRA].astype(BF16)
        terms = [jnp.concatenate([body[k * rows : k * rows + rows], ride]) for k in range(4)]
        total = add_up([terms[0]] + [hop(terms[k], phase, k) for k in (1, 3, 2)])
    back = total[:256].astype(BF16)
    grad_features = dot(back, weight, ((0,), (1,)))

    scale = 65536 ** (-0.5)
    own = total[256:]
    own_dw = own[:256] * scale
    own_db = ((own[256] + own[257]) + own[258]) * scale
    own = jnp.concatenate([own_dw, jnp.broadcast_to(own_db, (8, 128))])
    other = swap(own)
    first = jnp.where(core == 0, own, other)
    second = jnp.where(core == 0, other, own)
    both = jnp.concatenate([first, second], axis=1)
    return activation, both[:256], both[256], grad_features


def solution(mesh):
    in_specs = (
        P("rows", None),
        P("rows", None, None, None),
        P("rows", None),
        P("rows"),
        P(),
        P(),
        P("rows", None),
    )
    out_specs = (P("rows", None), P(), P(), P("rows", None))
    return jax.shard_map(
        on_device, mesh=mesh, in_specs=in_specs, out_specs=out_specs, check_vma=False
    )
```

time: 913 us -> 159 us (0.17)
  waiting for transfers between devices: 765 us -> 62.8 us
  blocking collectives: 63 us -> 0 us
  starting transfers between devices: 0.12 us -> 43.4 us
  Pallas kernels: 0 us -> 29.3 us
  local copies, waits for them, and re-layouts: 36.9 us -> 13 us
  matrix products: 24.1 us -> 0.85 us
  between operations: 14.5 us -> 1.61 us
    reduce_scatter x1 -> x0, waiting for transfers between devices: 656 us -> none  [on_device(): lax.psum_scatter(column_terms, 'rows', scatter_dimension=0, tiled=True)]
    psum x1 -> x0, blocking collectives: 63 us -> none  [on_device(): total_weight, total_bias = lax.psum((local_weight, local_bias), 'rows')]
    ppermute x0 -> x28, waiting for transfers between devices: none -> 62.8 us  [the longest x18 56.5 us: hop(): return lax.ppermute(x, AXIS, pairs(move))]
    all_gather x1 -> x0, waiting for transfers between devices: 61.2 us -> none  [on_device(): gathered = lax.all_gather(features, 'rows', axis=0, tiled=True)]
    psum x1 -> x0, waiting for transfers between devices: 46.8 us -> none  [on_device(): total_weight, total_bias = lax.psum((local_weight, local_bias), 'rows')]
    ppermute x0 -> x28, starting transfers between devices: none -> 43.4 us  [the longest x18 27.6 us: hop(): return lax.ppermute(x, AXIS, pairs(move))]
    pallas_call x0 -> x1, Pallas kernels: none -> 29.3 us  [local(): pl.pallas_call(kernel, out_shape=(jax.ShapeDtypeStruct((512, 256), BF16),...]
    dot_general x5 -> x1, matrix products: 24.1 us -> 0.85 us  [dot(): return lax.dot_general(a, b, (dims, ((), ())), preferred_element_type=F32)]
  transfers between devices with their start and end apart: 3 -> 28, of which waited for: 3 -> 13; matrix products, arithmetic and copies ran while one was open for 5% -> 6% of each run, Pallas kernels for 0% -> 0%
where the time goes in v1:
time: 159 us; the launch traced here: 158 us
  waiting for transfers between devices  62.8 us (39%)
  starting transfers between devices  43.4 us (27%)
  Pallas kernels  29.3 us (18%)
  local copies, waits for them, and re-layouts  13 us (8%)
  other arithmetic  7.29 us (5%)
  between operations  1.61 us (1%)
    ppermute x18, waiting for transfers between devices, hop(): return lax.ppermute(x, AXIS, pairs(move))  56.5 us
    pallas_call x1, Pallas kernels, local(): pl.pallas_call(kernel, out_shape=(jax.ShapeDtypeStruct((512, 256), BF16),...  29.3 us
    ppermute x18, starting transfers between devices, hop(): return lax.ppermute(x, AXIS, pairs(move))  27.6 us
    ppermute x10, starting transfers between devices, swap(): return lax.ppermute(x, AXIS, pairs(move))  15.8 us
    unnamed x18, local copies, waits for them, and re-layouts  10.6 us
    ppermute x10, waiting for transfers between devices, swap(): return lax.ppermute(x, AXIS, pairs(move))  6.29 us
  transfers between devices with their start and end apart: 28, of which 13 were waited for; matrix products, arithmetic and copies ran while one was open for 6% of the time, Pallas kernels for 0%

profile of v1, /device:TPU:1, one launch (start us, length us, event | category | flops | bytes accessed | tf_op | source)
XLA Modules:
  0.0 158.2 jit_solution(4068135128741934121)
XLA Ops:
  0.6 2.2 %collective-permute-start = (bf16[1,128,256]{2,1,0:T(8,128)(2,1)}, bf16[1,128,256]{2,1,0:T(8,128)(2,1)S(1)}, u32[]{:S(2)}, u32[]{:S(2)}) collective-permute-start(bf16[1,128,256]{2,1,0:T(8,128)(2,1)} %bitcast.45), channel_id=1, source_target_pairs={{0,8},{1,33},{2,10},{3,35},{4,12},{5,37},{6,14},{7,39},{8,16},{9,4... | collective-permute-start | bytes 196616 | tf_op jit(solution)/shard_map/ppermute | solution.py:34
  2.8 2.6 %collective-permute-start.1 = (bf16[1,128,256]{2,1,0:T(8,128)(2,1)}, bf16[1,128,256]{2,1,0:T(8,128)(2,1)S(1)}, u32[]{:S(2)}, u32[]{:S(2)}) collective-permute-start(bf16[1,128,256]{2,1,0:T(8,128)(2,1)} %bitcast.46), channel_id=1, source_target_pairs={{0,16},{1,65},{2,18},{3,67},{4,20},{5,69},{6,22},{7,71},{8,24},{9,... | collective-permute-start | bytes 196616 | tf_op jit(solution)/shard_map/ppermute | solution.py:34
  5.5 1.1 collective-permute-start.2
  6.5 1.5 constant_dynamic-update-slice_fusion.6
  10.0 1.7 %collective-permute-start.3 = (bf16[4,128,256]{2,1,0:T(8,128)(2,1)S(1)}, bf16[4,128,256]{2,1,0:T(8,128)(2,1)S(1)}, u32[]{:S(2)}, u32[]{:S(2)}) collective-permute-start(bf16[4,128,256]{2,1,0:T(8,128)(2,1)S(1)} %pad_maximum_fusion.20), channel_id=1, source_target_pairs={{0,32},{1,3},{2,34},{3,5},{4,36},{5,7},{6,38},{7,1},{8,40},{9,11},... | collective-permute-start | bytes 786440 | tf_op jit(solution)/shard_map/ppermute | solution.py:34
  11.7 3.3 %collective-permute-start.4 = (bf16[4,128,256]{2,1,0:T(8,128)(2,1)S(1)}, bf16[4,128,256]{2,1,0:T(8,128)(2,1)S(1)}, u32[]{:S(2)}, u32[]{:S(2)}) collective-permute-start(bf16[4,128,256]{2,1,0:T(8,128)(2,1)S(1)} %pad_maximum_fusion.20), channel_id=1, source_target_pairs={{0,64},{1,5},{2,66},{3,7},{4,68},{5,1},{6,70},{7,3},{8,72},{9,13},... | collective-permute-start | bytes 786440 | tf_op jit(solution)/shard_map/ppermute | solution.py:34
  18.7 3.2 %collective-permute-done.4 = bf16[4,128,256]{2,1,0:T(8,128)(2,1)S(1)} collective-permute-done((bf16[4,128,256]{2,1,0:T(8,128)(2,1)S(1)}, bf16[4,128,256]{2,1,0:T(8,128)(2,1)S(1)}, u32[]{:S(2)}, u32[]{:S(2)}) %collective-permute-start.4) | collective-permute-done | bytes 262176 | tf_op jit(solution)/shard_map/ppermute | solution.py:34
  23.5 1.2 collective-permute-start.6
  24.7 2.2 %collective-permute-start.7 = (bf16[16,128,256]{2,1,0:T(8,128)(2,1)}, bf16[16,128,256]{2,1,0:T(8,128)(2,1)S(1)}, u32[]{:S(2)}, u32[]{:S(2)}) collective-permute-start(bf16[16,128,256]{2,1,0:T(8,128)(2,1)} %get-tuple-element.41), channel_id=1, source_target_pairs={{0,4},{1,17},{2,6},{3,19},{4,0},{5,21},{6,2},{7,23},{8,12},{9,25},... | collective-permute-start | bytes 3145736 | tf_op jit(solution)/shard_map/ppermute | solution.py:34
  26.8 1.3 collective-permute-start.8
  28.1 3.5 %collective-permute-start.9 = (bf16[16,128,256]{2,1,0:T(8,128)(2,1)}, bf16[16,128,256]{2,1,0:T(8,128)(2,1)}, u32[]{:S(2)}, u32[]{:S(2)}) collective-permute-start(bf16[16,128,256]{2,1,0:T(8,128)(2,1)} %get-tuple-element.41), channel_id=1, source_target_pairs={{0,1},{1,0},{2,3},{3,2},{4,5},{5,4},{6,7},{7,6},{8,9},{9,8},{10,11... | collective-permute-start | bytes 3145736 | tf_op jit(solution)/shard_map/ppermute | solution.py:42
  31.6 7.2 %collective-permute-done.6 = bf16[16,128,256]{2,1,0:T(8,128)(2,1)S(1)} collective-permute-done((bf16[16,128,256]{2,1,0:T(8,128)(2,1)}, bf16[16,128,256]{2,1,0:T(8,128)(2,1)S(1)}, u32[]{:S(2)}, u32[]{:S(2)}) %collective-permute-start.6) | collective-permute-done | bytes 1048608 | tf_op jit(solution)/shard_map/ppermute | solution.py:34
  38.8 3.3 %collective-permute-start.10 = (bf16[16,128,256]{2,1,0:T(8,128)(2,1)S(1)}, bf16[16,128,256]{2,1,0:T(8,128)(2,1)}, u32[]{:S(2)}, u32[]{:S(2)}) collective-permute-start(bf16[16,128,256]{2,1,0:T(8,128)(2,1)S(1)} %collective-permute-done.6), channel_id=1, source_target_pairs={{0,1},{1,0},{2,3},{3,2},{4,5},{5,4},{6,7},{7,6},{8,9},{9,8},{10,11... | collective-permute-start | bytes 3145736 | tf_op jit(solution)/shard_map/ppermute | solution.py:42
  42.2 8.6 %collective-permute-done.7 = bf16[16,128,256]{2,1,0:T(8,128)(2,1)S(1)} collective-permute-done((bf16[16,128,256]{2,1,0:T(8,128)(2,1)}, bf16[16,128,256]{2,1,0:T(8,128)(2,1)S(1)}, u32[]{:S(2)}, u32[]{:S(2)}) %collective-permute-start.7) | collective-permute-done | bytes 1048608 | tf_op jit(solution)/shard_map/ppermute | solution.py:34
  50.8 4.1 %collective-permute-start.11 = (bf16[16,128,256]{2,1,0:T(8,128)(2,1)S(1)}, bf16[16,128,256]{2,1,0:T(8,128)(2,1)}, u32[]{:S(2)}, u32[]{:S(2)}) collective-permute-start(bf16[16,128,256]{2,1,0:T(8,128)(2,1)S(1)} %collective-permute-done.7), channel_id=1, source_target_pairs={{0,1},{1,0},{2,3},{3,2},{4,5},{5,4},{6,7},{7,6},{8,9},{9,8},{10,11... | collective-permute-start | bytes 3145736 | tf_op jit(solution)/shard_map/ppermute | solution.py:42
  56.7 1.1 constant_dynamic-update-slice_fusion.8
  58.8 2.5 %pad_maximum_fusion.theirs = bf16[64,128,256]{2,1,0:T(8,128)(2,1)S(1)} fusion(bf16[16,128,256]{2,1,0:T(8,128)(2,1)} %collective-permute-done.12, bf16[16,128,256]{2,1,0:T(8,128)(2,1)} %collective-permute-done.11, bf16[16,128,256]{2,1,0:T(8,128)(2,1)} %collective-permute-done.10, bf16[16,128,256]{2,1,0:T(8,128)(2,1)} %collective-permute-done.9), kind=kLoop, calls=%fused_computation | loop fusion | flops 6291456 | bytes 8388608 | tf_op jit(solution)/shard_map/concatenate | solution.py:254
  61.3 3.4 %copy-done = bf16[1,16,512,512]{3,2,1,0:T(8,128)(2,1)S(1)} copy-done((bf16[1,16,512,512]{3,2,1,0:T(8,128)(2,1)S(1)}, bf16[1,16,512,512]{3,2,1,0:T(8,128)(2,1)}, u32[]{:S(2)}) %copy-start) | copy-done | bytes 8388632
  64.7 29.3 %layer.1 = (bf16[512,256]{1,0:T(8,128)(2,1)}, bf16[4,4096,128]{2,1,0:T(8,128)(2,1)S(1)}, bf16[4,4096,128]{2,1,0:T(8,128)(2,1)S(1)}, bf16[272,128]{1,0:T(8,128)(2,1)S(1)}, bf16[272,128]{1,0:T(8,128)(2,1)S(1)}) custom-call(s32[21]{0:T(128)S(1)} %concatenate.77.s_ref, bf16[16,512,512]{2,1,0:T(8,128)(2,1)S(1)} %bitcast.43, ...), custom_call_target="tpu_custom_call" | custom-call | flops 4294967296 | bytes 33554432 | tf_op jit(solution)/shard_map/layer/pallas_call | solution.py:187
  95.5 6.1 %collective-permute-done.14 = bf16[272,128]{1,0:T(8,128)(2,1)S(1)} collective-permute-done((bf16[272,128]{1,0:T(8,128)(2,1)S(1)}, bf16[272,128]{1,0:T(8,128)(2,1)S(1)}, u32[]{:S(2)}, u32[]{:S(2)}) %collective-permute-start.14) | collective-permute-done | bytes 69664 | tf_op jit(solution)/shard_map/ppermute | solution.py:42
  101.8 1.1 fusion.3
  103.6 2.3 %collective-permute-start.18 = (bf16[4368,128]{1,0:T(8,128)(2,1)S(1)}, bf16[4368,128]{1,0:T(8,128)(2,1)S(1)}, u32[]{:S(2)}, u32[]{:S(2)}) collective-permute-start(bf16[4368,128]{1,0:T(8,128)(2,1)S(1)} %get-tuple-element.52), channel_id=1, source_target_pairs={{0,6},{1,25},{2,0},{3,27},{4,2},{5,29},{6,4},{7,31},{8,14},{9,1},{... | collective-permute-start | bytes 3354632 | tf_op jit(solution)/shard_map/ppermute | solution.py:34
  105.9 25.2 %collective-permute-done.16 = bf16[4368,128]{1,0:T(8,128)(2,1)S(1)} collective-permute-done((bf16[4368,128]{1,0:T(8,128)(2,1)S(1)}, bf16[4368,128]{1,0:T(8,128)(2,1)S(1)}, u32[]{:S(2)}, u32[]{:S(2)}) %collective-permute-start.16) | collective-permute-done | bytes 1118240 | tf_op jit(solution)/shard_map/ppermute | solution.py:34
  132.3 2.7 %collective-permute-start.22 = (bf16[1296,128]{1,0:T(8,128)(2,1)S(1)}, bf16[1296,128]{1,0:T(8,128)(2,1)S(1)}, u32[]{:S(2)}, u32[]{:S(2)}) collective-permute-start(bf16[1296,128]{1,0:T(8,128)(2,1)S(1)} %get-tuple-element.63), channel_id=1, source_target_pairs={{0,96},{1,7},{2,98},{3,1},{4,100},{5,3},{6,102},{7,5},{8,104},{9,1... | collective-permute-start | bytes 995336 | tf_op jit(solution)/shard_map/ppermute | solution.py:34
  134.9 1.6 %collective-permute-start.23 = (bf16[1296,128]{1,0:T(8,128)(2,1)S(1)}, bf16[1296,128]{1,0:T(8,128)(2,1)S(1)}, u32[]{:S(2)}, u32[]{:S(2)}) collective-permute-start(bf16[1296,128]{1,0:T(8,128)(2,1)S(1)} %get-tuple-element.50), channel_id=1, source_target_pairs={{0,64},{1,5},{2,66},{3,7},{4,68},{5,1},{6,70},{7,3},{8,72},{9,13},... | collective-permute-start | bytes 995336 | tf_op jit(solution)/shard_map/ppermute | solution.py:34
  136.5 3.2 %collective-permute-done.21 = bf16[1296,128]{1,0:T(8,128)(2,1)S(1)} collective-permute-done((bf16[1296,128]{1,0:T(8,128)(2,1)S(1)}, bf16[1296,128]{1,0:T(8,128)(2,1)S(1)}, u32[]{:S(2)}, u32[]{:S(2)}) %collective-permute-start.21) | collective-permute-done | bytes 331808 | tf_op jit(solution)/shard_map/ppermute | solution.py:34
  139.7 2.8 %collective-permute-done.22 = bf16[1296,128]{1,0:T(8,128)(2,1)S(1)} collective-permute-done((bf16[1296,128]{1,0:T(8,128)(2,1)S(1)}, bf16[1296,128]{1,0:T(8,128)(2,1)S(1)}, u32[]{:S(2)}, u32[]{:S(2)}) %collective-permute-start.22) | collective-permute-done | bytes 331808 | tf_op jit(solution)/shard_map/ppermute | solution.py:34
  144.6 2.1 %collective-permute-start.25 = (bf16[528,128]{1,0:T(8,128)(2,1)S(1)}, bf16[528,128]{1,0:T(8,128)(2,1)S(1)}, u32[]{:S(2)}, u32[]{:S(2)}) collective-permute-start(bf16[528,128]{1,0:T(8,128)(2,1)S(1)} %get-tuple-element.62), channel_id=1, source_target_pairs={{0,24},{1,97},{2,26},{3,99},{4,28},{5,101},{6,30},{7,103},{8,0},{9... | collective-permute-start | bytes 405512 | tf_op jit(solution)/shard_map/ppermute | solution.py:34
  146.7 1.1 collective-permute-start.26
  147.8 1.2 collective-permute-done.24
  149.1 3.0 %collective-permute-done.26 = bf16[528,128]{1,0:T(8,128)(2,1)S(1)} collective-permute-done((bf16[528,128]{1,0:T(8,128)(2,1)S(1)}, bf16[528,128]{1,0:T(8,128)(2,1)S(1)}, u32[]{:S(2)}, u32[]{:S(2)}) %collective-permute-start.26) | collective-permute-done | bytes 135200 | tf_op jit(solution)/shard_map/ppermute | solution.py:34
  152.2 3.6 %collective-permute-start.27 = (f32[264,128]{1,0:T(8,128)S(1)}, f32[264,128]{1,0:T(8,128)S(1)}, u32[]{:S(2)}, u32[]{:S(2)}) collective-permute-start(f32[264,128]{1,0:T(8,128)S(1)} %pad_maximum_fusion.24), channel_id=1, source_target_pairs={{0,1},{1,0},{2,3},{3,2},{4,5},{5,4},{6,7},{7,6},{8,9},{9,8},{10,11... | collective-permute-start | bytes 405512 | tf_op jit(solution)/shard_map/ppermute | solution.py:42
  (82 shorter events, 17.3 us)
Async XLA Ops:
  0.6 54.9 %copy-start.4 = (s32[1,16]{1,0:T(1,128)S(1)}, s32[1,16]{1,0:T(1,128)}, u32[]{:S(2)}) copy-start(s32[1,16]{1,0:T(1,128)} %param.9) | copy-start | bytes 196
  0.6 7.4 %collective-permute-start = (bf16[1,128,256]{2,1,0:T(8,128)(2,1)}, bf16[1,128,256]{2,1,0:T(8,128)(2,1)S(1)}, u32[]{:S(2)}, u32[]{:S(2)}) collective-permute-start(bf16[1,128,256]{2,1,0:T(8,128)(2,1)} %bitcast.45), channel_id=1, source_target_pairs={{0,8},{1,33},{2,10},{3,35},{4,12},{5,37},{6,14},{7,39},{8,16},{9,4... | collective-permute-start | bytes 196616 | tf_op jit(solution)/shard_map/ppermute | solution.py:34
  2.8 5.2 %collective-permute-start.1 = (bf16[1,128,256]{2,1,0:T(8,128)(2,1)}, bf16[1,128,256]{2,1,0:T(8,128)(2,1)S(1)}, u32[]{:S(2)}, u32[]{:S(2)}) collective-permute-start(bf16[1,128,256]{2,1,0:T(8,128)(2,1)} %bitcast.46), channel_id=1, source_target_pairs={{0,16},{1,65},{2,18},{3,67},{4,20},{5,69},{6,22},{7,71},{8,24},{9,... | collective-permute-start | bytes 196616 | tf_op jit(solution)/shard_map/ppermute | solution.py:34
  5.5 3.6 %collective-permute-start.2 = (bf16[1,128,256]{2,1,0:T(8,128)(2,1)}, bf16[1,128,256]{2,1,0:T(8,128)(2,1)S(1)}, u32[]{:S(2)}, u32[]{:S(2)}) collective-permute-start(bf16[1,128,256]{2,1,0:T(8,128)(2,1)} %bitcast.47), channel_id=1, source_target_pairs={{0,24},{1,97},{2,26},{3,99},{4,28},{5,101},{6,30},{7,103},{8,0},{9... | collective-permute-start | bytes 196616 | tf_op jit(solution)/shard_map/ppermute | solution.py:34
  10.0 7.9 %collective-permute-start.3 = (bf16[4,128,256]{2,1,0:T(8,128)(2,1)S(1)}, bf16[4,128,256]{2,1,0:T(8,128)(2,1)S(1)}, u32[]{:S(2)}, u32[]{:S(2)}) collective-permute-start(bf16[4,128,256]{2,1,0:T(8,128)(2,1)S(1)} %pad_maximum_fusion.20), channel_id=1, source_target_pairs={{0,32},{1,3},{2,34},{3,5},{4,36},{5,7},{6,38},{7,1},{8,40},{9,11},... | collective-permute-start | bytes 786440 | tf_op jit(solution)/shard_map/ppermute | solution.py:34
  11.7 10.2 %collective-permute-start.4 = (bf16[4,128,256]{2,1,0:T(8,128)(2,1)S(1)}, bf16[4,128,256]{2,1,0:T(8,128)(2,1)S(1)}, u32[]{:S(2)}, u32[]{:S(2)}) collective-permute-start(bf16[4,128,256]{2,1,0:T(8,128)(2,1)S(1)} %pad_maximum_fusion.20), channel_id=1, source_target_pairs={{0,64},{1,5},{2,66},{3,7},{4,68},{5,1},{6,70},{7,3},{8,72},{9,13},... | collective-permute-start | bytes 786440 | tf_op jit(solution)/shard_map/ppermute | solution.py:34
  15.0 7.7 %collective-permute-start.5 = (bf16[4,128,256]{2,1,0:T(8,128)(2,1)S(1)}, bf16[4,128,256]{2,1,0:T(8,128)(2,1)S(1)}, u32[]{:S(2)}, u32[]{:S(2)}) collective-permute-start(bf16[4,128,256]{2,1,0:T(8,128)(2,1)S(1)} %pad_maximum_fusion.20), channel_id=1, source_target_pairs={{0,96},{1,7},{2,98},{3,1},{4,100},{5,3},{6,102},{7,5},{8,104},{9,1... | collective-permute-start | bytes 786440 | tf_op jit(solution)/shard_map/ppermute | solution.py:34
  23.5 15.4 %collective-permute-start.6 = (bf16[16,128,256]{2,1,0:T(8,128)(2,1)}, bf16[16,128,256]{2,1,0:T(8,128)(2,1)S(1)}, u32[]{:S(2)}, u32[]{:S(2)}) collective-permute-start(bf16[16,128,256]{2,1,0:T(8,128)(2,1)} %get-tuple-element.41), channel_id=1, source_target_pairs={{0,2},{1,9},{2,4},{3,11},{4,6},{5,13},{6,0},{7,15},{8,10},{9,17},{... | collective-permute-start | bytes 3145736 | tf_op jit(solution)/shard_map/ppermute | solution.py:34
  24.7 26.1 %collective-permute-start.7 = (bf16[16,128,256]{2,1,0:T(8,128)(2,1)}, bf16[16,128,256]{2,1,0:T(8,128)(2,1)S(1)}, u32[]{:S(2)}, u32[]{:S(2)}) collective-permute-start(bf16[16,128,256]{2,1,0:T(8,128)(2,1)} %get-tuple-element.41), channel_id=1, source_target_pairs={{0,4},{1,17},{2,6},{3,19},{4,0},{5,21},{6,2},{7,23},{8,12},{9,25},... | collective-permute-start | bytes 3145736 | tf_op jit(solution)/shard_map/ppermute | solution.py:34
  26.8 28.0 %collective-permute-start.8 = (bf16[16,128,256]{2,1,0:T(8,128)(2,1)}, bf16[16,128,256]{2,1,0:T(8,128)(2,1)S(1)}, u32[]{:S(2)}, u32[]{:S(2)}) collective-permute-start(bf16[16,128,256]{2,1,0:T(8,128)(2,1)} %get-tuple-element.41), channel_id=1, source_target_pairs={{0,6},{1,25},{2,0},{3,27},{4,2},{5,29},{6,4},{7,31},{8,14},{9,1},{... | collective-permute-start | bytes 3145736 | tf_op jit(solution)/shard_map/ppermute | solution.py:34
  28.1 30.7 %collective-permute-start.9 = (bf16[16,128,256]{2,1,0:T(8,128)(2,1)}, bf16[16,128,256]{2,1,0:T(8,128)(2,1)}, u32[]{:S(2)}, u32[]{:S(2)}) collective-permute-start(bf16[16,128,256]{2,1,0:T(8,128)(2,1)} %get-tuple-element.41), channel_id=1, source_target_pairs={{0,1},{1,0},{2,3},{3,2},{4,5},{5,4},{6,7},{7,6},{8,9},{9,8},{10,11... | collective-permute-start | bytes 3145736 | tf_op jit(solution)/shard_map/ppermute | solution.py:42
  38.8 19.9 %collective-permute-start.10 = (bf16[16,128,256]{2,1,0:T(8,128)(2,1)S(1)}, bf16[16,128,256]{2,1,0:T(8,128)(2,1)}, u32[]{:S(2)}, u32[]{:S(2)}) collective-permute-start(bf16[16,128,256]{2,1,0:T(8,128)(2,1)S(1)} %collective-permute-done.6), channel_id=1, source_target_pairs={{0,1},{1,0},{2,3},{3,2},{4,5},{5,4},{6,7},{7,6},{8,9},{9,8},{10,11... | collective-permute-start | bytes 3145736 | tf_op jit(solution)/shard_map/ppermute | solution.py:42
  50.8 8.0 %collective-permute-start.11 = (bf16[16,128,256]{2,1,0:T(8,128)(2,1)S(1)}, bf16[16,128,256]{2,1,0:T(8,128)(2,1)}, u32[]{:S(2)}, u32[]{:S(2)}) collective-permute-start(bf16[16,128,256]{2,1,0:T(8,128)(2,1)S(1)} %collective-permute-done.7), channel_id=1, source_target_pairs={{0,1},{1,0},{2,3},{3,2},{4,5},{5,4},{6,7},{7,6},{8,9},{9,8},{10,11... | collective-permute-start | bytes 3145736 | tf_op jit(solution)/shard_map/ppermute | solution.py:42
  54.9 3.9 %collective-permute-start.12 = (bf16[16,128,256]{2,1,0:T(8,128)(2,1)S(1)}, bf16[16,128,256]{2,1,0:T(8,128)(2,1)}, u32[]{:S(2)}, u32[]{:S(2)}) collective-permute-start(bf16[16,128,256]{2,1,0:T(8,128)(2,1)S(1)} %collective-permute-done.8), channel_id=1, source_target_pairs={{0,1},{1,0},{2,3},{3,2},{4,5},{5,4},{6,7},{7,6},{8,9},{9,8},{10,11... | collective-permute-start | bytes 3145736 | tf_op jit(solution)/shard_map/ppermute | solution.py:42
  58.8 2.6 %copy-start.2 = (bf16[512,256]{1,0:T(8,128)(2,1)S(1)}, bf16[512,256]{1,0:T(8,128)(2,1)}, u32[]{:S(2)}) copy-start(bf16[512,256]{1,0:T(8,128)(2,1)} %cot_hbm.1) | copy-start | bytes 786436
  58.8 2.6 %copy-start.3 = (f32[256]{0:T(256)S(1)}, f32[256]{0:T(256)}, u32[]{:S(2)}) copy-start(f32[256]{0:T(256)} %param.12) | copy-start | bytes 3076
  61.3 3.4 %copy-start = (bf16[1,16,512,512]{3,2,1,0:T(8,128)(2,1)S(1)}, bf16[1,16,512,512]{3,2,1,0:T(8,128)(2,1)}, u32[]{:S(2)}) copy-start(bf16[1,16,512,512]{3,2,1,0:T(8,128)(2,1)} %param.8) | copy-start | bytes 25165828
  94.3 7.5 %collective-permute-start.13 = (bf16[4096,128]{1,0:T(8,128)(2,1)S(1)}, bf16[4096,128]{1,0:T(8,128)(2,1)S(1)}, u32[]{:S(2)}, u32[]{:S(2)}) collective-permute-start(bf16[4096,128]{1,0:T(8,128)(2,1)S(1)} %get-tuple-element.28), channel_id=1, source_target_pairs={{0,1},{1,0},{2,3},{3,2},{4,5},{5,4},{6,7},{7,6},{8,9},{9,8},{10,11... | collective-permute-start | bytes 3145736 | tf_op jit(solution)/shard_map/ppermute | solution.py:42
  94.4 7.4 %collective-permute-start.15 = (bf16[4096,128]{1,0:T(8,128)(2,1)S(1)}, bf16[4096,128]{1,0:T(8,128)(2,1)S(1)}, u32[]{:S(2)}, u32[]{:S(2)}) collective-permute-start(bf16[4096,128]{1,0:T(8,128)(2,1)S(1)} %get-tuple-element.31), channel_id=1, source_target_pairs={{0,1},{1,0},{2,3},{3,2},{4,5},{5,4},{6,7},{7,6},{8,9},{9,8},{10,11... | collective-permute-start | bytes 3145736 | tf_op jit(solution)/shard_map/ppermute | solution.py:42
  94.9 6.9 %collective-permute-start.17 = (bf16[4096,128]{1,0:T(8,128)(2,1)S(1)}, bf16[4096,128]{1,0:T(8,128)(2,1)S(1)}, u32[]{:S(2)}, u32[]{:S(2)}) collective-permute-start(bf16[4096,128]{1,0:T(8,128)(2,1)S(1)} %get-tuple-element.30), channel_id=1, source_target_pairs={{0,1},{1,0},{2,3},{3,2},{4,5},{5,4},{6,7},{7,6},{8,9},{9,8},{10,11... | collective-permute-start | bytes 3145736 | tf_op jit(solution)/shard_map/ppermute | solution.py:42
  95.0 6.8 %collective-permute-start.19 = (bf16[4096,128]{1,0:T(8,128)(2,1)S(1)}, bf16[4096,128]{1,0:T(8,128)(2,1)S(1)}, u32[]{:S(2)}, u32[]{:S(2)}) collective-permute-start(bf16[4096,128]{1,0:T(8,128)(2,1)S(1)} %get-tuple-element.29), channel_id=1, source_target_pairs={{0,1},{1,0},{2,3},{3,2},{4,5},{5,4},{6,7},{7,6},{8,9},{9,8},{10,11... | collective-permute-start | bytes 3145736 | tf_op jit(solution)/shard_map/ppermute | solution.py:42
  95.4 6.2 %collective-permute-start.14 = (bf16[272,128]{1,0:T(8,128)(2,1)S(1)}, bf16[272,128]{1,0:T(8,128)(2,1)S(1)}, u32[]{:S(2)}, u32[]{:S(2)}) collective-permute-start(bf16[272,128]{1,0:T(8,128)(2,1)S(1)} %get-tuple-element.13), channel_id=1, source_target_pairs={{0,1},{1,0},{2,3},{3,2},{4,5},{5,4},{6,7},{7,6},{8,9},{9,8},{10,11... | collective-permute-start | bytes 208904 | tf_op jit(solution)/shard_map/ppermute | solution.py:42
  103.1 28.0 %collective-permute-start.16 = (bf16[4368,128]{1,0:T(8,128)(2,1)S(1)}, bf16[4368,128]{1,0:T(8,128)(2,1)S(1)}, u32[]{:S(2)}, u32[]{:S(2)}) collective-permute-start(bf16[4368,128]{1,0:T(8,128)(2,1)S(1)} %get-tuple-element.51), channel_id=1, source_target_pairs={{0,2},{1,9},{2,4},{3,11},{4,6},{5,13},{6,0},{7,15},{8,10},{9,17},{... | collective-permute-start | bytes 3354632 | tf_op jit(solution)/shard_map/ppermute | solution.py:34
  103.6 27.5 %collective-permute-start.18 = (bf16[4368,128]{1,0:T(8,128)(2,1)S(1)}, bf16[4368,128]{1,0:T(8,128)(2,1)S(1)}, u32[]{:S(2)}, u32[]{:S(2)}) collective-permute-start(bf16[4368,128]{1,0:T(8,128)(2,1)S(1)} %get-tuple-element.52), channel_id=1, source_target_pairs={{0,6},{1,25},{2,0},{3,27},{4,2},{5,29},{6,4},{7,31},{8,14},{9,1},{... | collective-permute-start | bytes 3354632 | tf_op jit(solution)/shard_map/ppermute | solution.py:34
  105.9 25.2 %collective-permute-start.20 = (bf16[4368,128]{1,0:T(8,128)(2,1)S(1)}, bf16[4368,128]{1,0:T(8,128)(2,1)S(1)}, u32[]{:S(2)}, u32[]{:S(2)}) collective-permute-start(bf16[4368,128]{1,0:T(8,128)(2,1)S(1)} %get-tuple-element.53), channel_id=1, source_target_pairs={{0,4},{1,17},{2,6},{3,19},{4,0},{5,21},{6,2},{7,23},{8,12},{9,25},... | collective-permute-start | bytes 3354632 | tf_op jit(solution)/shard_map/ppermute | solution.py:34
  132.0 7.7 %collective-permute-start.21 = (bf16[1296,128]{1,0:T(8,128)(2,1)S(1)}, bf16[1296,128]{1,0:T(8,128)(2,1)S(1)}, u32[]{:S(2)}, u32[]{:S(2)}) collective-permute-start(bf16[1296,128]{1,0:T(8,128)(2,1)S(1)} %get-tuple-element.49), channel_id=1, source_target_pairs={{0,32},{1,3},{2,34},{3,5},{4,36},{5,7},{6,38},{7,1},{8,40},{9,11},... | collective-permute-start | bytes 995336 | tf_op jit(solution)/shard_map/ppermute | solution.py:34
  132.3 10.3 %collective-permute-start.22 = (bf16[1296,128]{1,0:T(8,128)(2,1)S(1)}, bf16[1296,128]{1,0:T(8,128)(2,1)S(1)}, u32[]{:S(2)}, u32[]{:S(2)}) collective-permute-start(bf16[1296,128]{1,0:T(8,128)(2,1)S(1)} %get-tuple-element.63), channel_id=1, source_target_pairs={{0,96},{1,7},{2,98},{3,1},{4,100},{5,3},{6,102},{7,5},{8,104},{9,1... | collective-permute-start | bytes 995336 | tf_op jit(solution)/shard_map/ppermute | solution.py:34
  134.9 8.5 %collective-permute-start.23 = (bf16[1296,128]{1,0:T(8,128)(2,1)S(1)}, bf16[1296,128]{1,0:T(8,128)(2,1)S(1)}, u32[]{:S(2)}, u32[]{:S(2)}) collective-permute-start(bf16[1296,128]{1,0:T(8,128)(2,1)S(1)} %get-tuple-element.50), channel_id=1, source_target_pairs={{0,64},{1,5},{2,66},{3,7},{4,68},{5,1},{6,70},{7,3},{8,72},{9,13},... | collective-permute-start | bytes 995336 | tf_op jit(solution)/shard_map/ppermute | solution.py:34
  143.8 5.3 %collective-permute-start.24 = (bf16[528,128]{1,0:T(8,128)(2,1)S(1)}, bf16[528,128]{1,0:T(8,128)(2,1)S(1)}, u32[]{:S(2)}, u32[]{:S(2)}) collective-permute-start(bf16[528,128]{1,0:T(8,128)(2,1)S(1)} %get-tuple-element.47), channel_id=1, source_target_pairs={{0,8},{1,33},{2,10},{3,35},{4,12},{5,37},{6,14},{7,39},{8,16},{9,4... | collective-permute-start | bytes 405512 | tf_op jit(solution)/shard_map/ppermute | solution.py:34
  144.6 4.5 %collective-permute-start.25 = (bf16[528,128]{1,0:T(8,128)(2,1)S(1)}, bf16[528,128]{1,0:T(8,128)(2,1)S(1)}, u32[]{:S(2)}, u32[]{:S(2)}) collective-permute-start(bf16[528,128]{1,0:T(8,128)(2,1)S(1)} %get-tuple-element.62), channel_id=1, source_target_pairs={{0,24},{1,97},{2,26},{3,99},{4,28},{5,101},{6,30},{7,103},{8,0},{9... | collective-permute-start | bytes 405512 | tf_op jit(solution)/shard_map/ppermute | solution.py:34
  146.7 5.4 %collective-permute-start.26 = (bf16[528,128]{1,0:T(8,128)(2,1)S(1)}, bf16[528,128]{1,0:T(8,128)(2,1)S(1)}, u32[]{:S(2)}, u32[]{:S(2)}) collective-permute-start(bf16[528,128]{1,0:T(8,128)(2,1)S(1)} %get-tuple-element.48), channel_id=1, source_target_pairs={{0,16},{1,65},{2,18},{3,67},{4,20},{5,69},{6,22},{7,71},{8,24},{9,... | collective-permute-start | bytes 405512 | tf_op jit(solution)/shard_map/ppermute | solution.py:34
  152.2 4.6 %collective-permute-start.27 = (f32[264,128]{1,0:T(8,128)S(1)}, f32[264,128]{1,0:T(8,128)S(1)}, u32[]{:S(2)}, u32[]{:S(2)}) collective-permute-start(f32[264,128]{1,0:T(8,128)S(1)} %pad_maximum_fusion.24), channel_id=1, source_target_pairs={{0,1},{1,0},{2,3},{3,2},{4,5},{5,4},{6,7},{7,6},{8,9},{9,8},{10,11... | collective-permute-start | bytes 405512 | tf_op jit(solution)/shard_map/ppermute | solution.py:42
  (1 other events, 2.5 us)

commit v2 on v0

v2 whole, which is shorter than its diff:
```python
import functools

import jax
import jax.numpy as jnp
import numpy as np
from jax import lax
from jax.experimental import pallas as pl
from jax.experimental.pallas import tpu as pltpu
from jax.sharding import PartitionSpec as P

AXIS = "rows"
SIZES = (4, 4, 4, 2)
Y, X, Z = 0, 1, 2
ORDERS = ((X, Y, Z), (Y, Z, X))
BF16 = jnp.bfloat16
F32 = jnp.float32
GROUP = 8
STARTS = (0, 8, 16, 56, 24, 48, 32, 40)
EXTRA = 272


def pairs(move):
    out = []
    for i in range(128):
        to = move([int(v) for v in np.unravel_index(i, SIZES)])
        to = [t % n for t, n in zip(to, SIZES)]
        out.append((i, int(np.ravel_multi_index(to, SIZES))))
    return out


def hop(x, phase, k):
    def move(at):
        at[ORDERS[at[3]][phase]] += k
        return at

    return lax.ppermute(x, AXIS, pairs(move))


def swap(x):
    def move(at):
        at[3] += 1
        return at

    return lax.ppermute(x, AXIS, pairs(move))


def dot(a, b, dims):
    return lax.dot_general(a, b, (dims, ((), ())), preferred_element_type=F32)


def cut_in_kernel(v):
    return v.astype(BF16).astype(F32)


def cut(v):
    return lax.reduce_precision(v, 8, 7)


def split3(v, cut):
    hi = cut(v)
    mid = cut(v - hi)
    return hi, mid, (v - hi) - mid


def load_kernel(a_hbm, a_ref, sem):
    copies = [
        pltpu.make_async_copy(a_hbm.at[s], a_ref.at[:, pl.ds(s * 512, 512)], sem.at[s])
        for s in range(16)
    ]
    for copy in copies:
        copy.start()
    for copy in copies:
        copy.wait()


def load(values):
    return pl.pallas_call(
        load_kernel,
        out_shape=pltpu.VMEM((512, 8192), BF16),
        in_specs=[pl.BlockSpec(memory_space=pltpu.HBM)],
        out_specs=pl.BlockSpec(memory_space=pltpu.VMEM),
        scratch_shapes=[pltpu.SemaphoreType.DMA((16,))],
        compiler_params=pltpu.CompilerParams(vmem_limit_bytes=1024 * 1024),
        cost_estimate=pl.CostEstimate(flops=0, bytes_accessed=2 * 8 * 2**20, transcendentals=0),
        name="load",
    )(pltpu.with_memory_space_constraint(values, pltpu.HBM))


def kernel(
    col_ref, count_ref, a_ref, w_ref, b_ref, cot_ref, *rest,
):
    blocks, (act_ref, r_ref, e_ref, g_buf, x_buf, acc, g_t) = rest[:16], rest[16:]
    count = count_ref[0]
    index = lax.axis_index(AXIS)
    me = (index >> 5, (index >> 3) & 3, (index >> 1) & 3)
    core = index & 1

    def place(t, zlo, cc, sign):
        there = (lax.shift_right_logical(t, 3), lax.shift_right_logical(t, 1) & 3, (t & 1) * 2 + zlo)
        k = [((me[i] - there[i]) * sign) & 3 for i in range(3)]
        o = ORDERS[cc]
        return k[o[2]], k[o[1]] * 4 + k[o[0]]

    for side in range(2):
        for ref, start in zip(blocks[side * 8 : side * 8 + 8], STARTS):
            g_buf[side, start : start + ref.shape[0]] = ref[...]
    r_ref[...] = jnp.zeros_like(r_ref)
    acc[...] = jnp.zeros_like(acc)

    def forward(g, carry):
        for q in range(GROUP):
            s = g * GROUP + q
            t = col_ref[0, s]
            live = s < count
            for j in range(4):
                cc = j % 2
                k3, k21 = place(t, j // 2, cc, 1)
                at = k3 * 16 + k21
                piece = g_buf[jnp.where(core == cc, 0, 1), at]
                rows = slice(q * 512 + j * 128, q * 512 + j * 128 + 128)
                x_buf[rows] = jnp.where(live, piece, jnp.zeros_like(piece))
        columns = pl.ds(pl.multiple_of(g * (GROUP * 512), GROUP * 512), GROUP * 512)
        acc[...] += dot(a_ref[:, columns], x_buf[...], ((1,), (0,)))
        return carry

    lax.fori_loop(0, 16 // GROUP, forward, 0)

    agg = acc[...].astype(BF16)
    pre = dot(agg, w_ref[...], ((1,), (0,))) + b_ref[...]
    low = jnp.exp(jnp.minimum(pre, 0.0))
    act_ref[...] = jnp.where(pre > 0, pre, low - 1.0).astype(BF16)
    grad = (cot_ref[...].astype(F32) * low).astype(BF16)
    g_t[...] = grad.astype(F32).T.astype(BF16)
    dw = dot(agg, grad, ((0,), (0,)))
    db = jnp.sum(grad.astype(F32), axis=0, keepdims=True)
    for h in range(2):
        half = slice(h * 128, h * 128 + 128)
        side = jnp.where(core == h, 0, 1)
        e_ref[side, :256, :] = dw[:, half].astype(BF16)
        row = lax.broadcasted_iota(jnp.int32, (16, 128), 0)
        hi, mid, low3 = split3(db[:, half], cut_in_kernel)
        parts = jnp.where(row == 0, hi, jnp.where(row == 1, mid, jnp.where(row == 2, low3, 0.0)))
        e_ref[side, 256:, :] = parts.astype(BF16)

    def backward(g, carry):
        for q in range(GROUP):
            s = g * GROUP + q
            t = col_ref[0, s]
            columns = pl.ds(pl.multiple_of(s * 512, 512), 512)
            part = dot(g_t[...], a_ref[:, columns], ((1,), (0,)))
            part = jnp.where(s < count, part, 0.0).astype(BF16)
            for j in range(4):
                cc = j % 2
                k3, k21 = place(t, j // 2, cc, -1)
                side = jnp.where(core == cc, 0, 1)
                rows = pl.ds(pl.multiple_of(k21 * 256, 256), 256)
                r_ref[side * 4 + k3, rows] = part[:, j * 128 : j * 128 + 128]
        return carry

    lax.fori_loop(0, 16 // GROUP, backward, 0)


def local(cols, count, values, weight, bias, cotangent, blocks):
    vmem = pl.BlockSpec(memory_space=pltpu.VMEM)
    return pl.pallas_call(
        kernel,
        out_shape=(
            pltpu.VMEM((512, 256), BF16),
            pltpu.VMEM((8, 4096, 128), BF16),
            pltpu.VMEM((2, EXTRA, 128), BF16),
        ),
        in_specs=[pl.BlockSpec(memory_space=pltpu.SMEM)] * 2 + [vmem] * 20,
        out_specs=(vmem,) * 3,
        scratch_shapes=[
            pltpu.VMEM((2, 64, 128, 256), BF16),
            pltpu.VMEM((GROUP * 512, 256), BF16),
            pltpu.VMEM((512, 256), F32),
            pltpu.VMEM((256, 512), BF16),
        ],
        compiler_params=pltpu.CompilerParams(vmem_limit_bytes=18 * 1024 * 1024),
        cost_estimate=pl.CostEstimate(
            flops=2 * 2 * 16 * 512 * 512 * 256, bytes_accessed=8 * 2**20, transcendentals=512 * 256
        ),
        name="layer",
    )(cols, count, values, weight, bias, cotangent, *blocks)


def in_vmem(name, body, outs, *ins):
    vmem = pl.BlockSpec(memory_space=pltpu.VMEM)
    size = sum(int(np.prod(o.shape)) * 2 for o in (*outs, *ins))
    return pl.pallas_call(
        body,
        out_shape=tuple(pltpu.VMEM(o.shape, o.dtype) for o in outs),
        in_specs=[vmem] * len(ins),
        out_specs=(vmem,) * len(outs),
        compiler_params=pltpu.CompilerParams(vmem_limit_bytes=4 * 1024 * 1024),
        cost_estimate=pl.CostEstimate(flops=0, bytes_accessed=size // 4, transcendentals=0),
        name=name,
    )(*ins)


def like(*shape):
    return jax.ShapeDtypeStruct(shape, BF16)


def join(parts, pieces=1):
    rows = sum(p.shape[0] for p in parts) // pieces

    def body(*refs):
        at = 0
        for ref in refs[: len(parts)]:
            for i in range(ref.shape[0]):
                refs[len(parts) + at // rows][at % rows] = ref[i]
                at += 1

    outs = [like(rows, *parts[0].shape[1:])] * pieces
    return in_vmem("join", body, outs, *parts)


def add_up(parts):
    total = parts[0].astype(F32)
    for part in parts[1:]:
        total = total + part.astype(F32)
    return total


def widened(*refs):
    total = refs[0].astype(F32)
    for ref in refs[1:]:
        total = total + ref.astype(F32)
    return total


def exact_rows(total, cut):
    db = total[256:257] + total[257:258] + total[258:259]
    row = lax.broadcasted_iota(jnp.int32, (16, 128), 0)
    hi, mid, low = split3(db, cut)
    bias = jnp.where(row == 0, hi, jnp.where(row == 1, mid, jnp.where(row == 2, low, 0.0)))
    return total[:256].astype(BF16), bias.astype(BF16)


def put_extra(ref, at, total):
    top, bias = exact_rows(total, cut_in_kernel)
    ref[at : at + 256] = top
    ref[at + 256 : at + EXTRA] = bias


def first_terms(a, b, ea, eb, o1, o2, ride):
    put_extra(ride, 0, widened(ea[...], eb[...]))
    o1[:2048] = widened(a[:2048], b[:2048]).astype(BF16)
    o2[:2048] = widened(a[2048:], b[2048:]).astype(BF16)
    o1[2048:] = ride[...]
    o2[2048:] = ride[...]


def direct_terms(a, b, o):
    o[...] = widened(a[...], b[...]).astype(BF16)


def passed_terms(a, b, got, o):
    o[:2048] = widened(a[...], b[...], got[:2048]).astype(BF16)
    if o.shape[0] > 2048:
        o[2048:] = got[2048:]


def on_device(features, tile_values, tile_col, tile_count, weight, bias, cotangent):
    core = lax.axis_index(AXIS) & 1

    values = load(tile_values[0])
    held = features[None]
    held = join([held] + [hop(held, 0, k) for k in (1, 2, 3)])[0]
    held, values = lax.optimization_barrier((held, values))
    h1, h2 = join([held] + [hop(held, 1, k) for k in (1, 2, 3)], 2)
    a1, b2 = hop(h1, 2, 1), hop(h2, 2, 3)
    a2, b1 = hop(h2, 2, 1), hop(h1, 2, 3)
    c1, c2 = hop(a1, 2, 1), hop(b2, 2, 3)
    mine = [h1, h2, a1, b2, a2, b1, c1, c2]
    theirs = [swap(g) for g in mine]

    activation, r_all, e_all = local(
        tile_col, tile_count, values, weight, bias[None], cotangent, mine + theirs
    )

    o1, o2, ride = in_vmem(
        "first_terms", first_terms, [like(2048 + EXTRA, 128)] * 2 + [like(EXTRA, 128)],
        r_all[2], swap(r_all[6]), e_all[0], swap(e_all[1]),
    )
    o1, o2, r_all = lax.optimization_barrier((o1, o2, r_all))
    via1, via3 = hop(o1, 2, 1), hop(o2, 2, 3)
    t1, t3 = swap(r_all[5]), swap(r_all[7])
    half = [like(2048, 128)]
    d1 = in_vmem("direct_terms", direct_terms, half, r_all[1, 2048:], t1[2048:])[0]
    d3 = in_vmem("direct_terms", direct_terms, half, r_all[3, :2048], t3[:2048])[0]
    d1, d3 = hop(d1, 2, 1), hop(d3, 2, 3)
    t0 = swap(r_all[4])
    p1 = in_vmem("passed_terms", passed_terms, [like(2048 + EXTRA, 128)], r_all[1, :2048], t1[:2048], via1)[0]
    p3 = in_vmem("passed_terms", passed_terms, half, r_all[3, 2048:], t3[2048:], via3[:2048])[0]
    p1, p3 = hop(p1, 2, 1), hop(p3, 2, 3)

    total = jnp.concatenate([
        add_up([r_all[0, :2048], t0[:2048], d3, p1[:2048]]),
        add_up([r_all[0, 2048:], t0[2048:], d1, p3]),
        add_up([ride, via1[2048:], via3[2048:], p1[2048:]]),
    ])
    for phase in (1, 0):
        ride = jnp.concatenate(exact_rows(total[-EXTRA:], cut))
        rows = (total.shape[0] - EXTRA) // 4
        body = total[:-EXTRA].astype(BF16)
        terms = [jnp.concatenate([body[k * rows : k * rows + rows], ride]) for k in range(4)]
        own = jnp.concatenate([total[:rows], total[-EXTRA:]])
        total = add_up([own] + [hop(terms[k], phase, k) for k in (1, 3, 2)])
    back = total[:256].astype(BF16)
    grad_features = dot(back, weight, ((0,), (1,)))

    scale = 65536 ** (-0.5)
    own = total[256:]
    own_dw = own[:256] * scale
    own_db = ((own[256] + own[257]) + own[258]) * scale
    own = jnp.concatenate([own_dw, jnp.broadcast_to(own_db, (8, 128))])
    other = swap(own)
    first = jnp.where(core == 0, own, other)
    second = jnp.where(core == 0, other, own)
    both = jnp.concatenate([first, second], axis=1)
    return activation, both[:256], both[256], grad_features


def solution(mesh):
    in_specs = (
        P("rows", None),
        P("rows", None, None, None),
        P("rows", None),
        P("rows"),
        P(),
        P(),
        P("rows", None),
    )
    out_specs = (P("rows", None), P(), P(), P("rows", None))
    return jax.shard_map(
        on_device, mesh=mesh, in_specs=in_specs, out_specs=out_specs, check_vma=False
    )
```

time: 913 us -> 121 us (0.13)
  waiting for transfers between devices: 765 us -> 45 us
  blocking collectives: 63 us -> 0 us
  starting transfers between devices: 0.12 us -> 56.5 us
  local copies, waits for them, and re-layouts: 36.9 us -> 1.54 us
  matrix products: 24.1 us -> 0.86 us
  between operations: 14.5 us -> 1.67 us
  Pallas kernels: 0 us -> 12.8 us
    reduce_scatter x1 -> x0, waiting for transfers between devices: 656 us -> none  [on_device(): lax.psum_scatter(column_terms, 'rows', scatter_dimension=0, tiled=True)]
    psum x1 -> x0, blocking collectives: 63 us -> none  [on_device(): total_weight, total_bias = lax.psum((local_weight, local_bias), 'rows')]
    all_gather x1 -> x0, waiting for transfers between devices: 61.2 us -> none  [on_device(): gathered = lax.all_gather(features, 'rows', axis=0, tiled=True)]
    ppermute x0 -> x38, starting transfers between devices: none -> 56.5 us  [the longest x24 31.7 us: hop(): return lax.ppermute(x, AXIS, pairs(move))]
    psum x1 -> x0, waiting for transfers between devices: 46.8 us -> none  [on_device(): total_weight, total_bias = lax.psum((local_weight, local_bias), 'rows')]
    ppermute x0 -> x38, waiting for transfers between devices: none -> 45 us  [the longest x24 41.3 us: hop(): return lax.ppermute(x, AXIS, pairs(move))]
    dot_general x5 -> x1, matrix products: 24.1 us -> 0.86 us  [dot(): return lax.dot_general(a, b, (dims, ((), ())), preferred_element_type=F32)]
    dot_general x1 -> x0, local copies, waits for them, and re-layouts: 15.8 us -> none  [on_device(): column_terms = jnp.einsum('sc,sjh->cjh', onehot, parts)]
  transfers between devices with their start and end apart: 3 -> 38, of which waited for: 3 -> 19; matrix products, arithmetic and copies ran while one was open for 5% -> 2% of each run, Pallas kernels for 0% -> 3%
where the time goes in v2:
time: 121 us
  starting transfers between devices  56.5 us (47%)
  waiting for transfers between devices  45 us (37%)
  Pallas kernels  12.8 us (11%)
  other arithmetic  2.42 us (2%)
  between operations  1.67 us (1%)
  local copies, waits for them, and re-layouts  1.54 us (1%)
    ppermute x24, waiting for transfers between devices, hop(): return lax.ppermute(x, AXIS, pairs(move))  41.3 us
    ppermute x24, starting transfers between devices, hop(): return lax.ppermute(x, AXIS, pairs(move))  31.7 us
    ppermute x14, starting transfers between devices, swap(): return lax.ppermute(x, AXIS, pairs(move))  24.8 us
    pallas_call x1, Pallas kernels, local(): pl.pallas_call(kernel, out_shape=(pltpu.VMEM((512, 256), BF16), pltpu.VME...  7.99 us
    ppermute x14, waiting for transfers between devices, swap(): return lax.ppermute(x, AXIS, pairs(move))  3.74 us
    pallas_call x1, Pallas kernels, load(): pl.pallas_call(load_kernel, out_shape=pltpu.VMEM((512, 8192), BF16), in_s...  3.56 us
  transfers between devices with their start and end apart: 38, of which 19 were waited for; matrix products, arithmetic and copies ran while one was open for 2% of the time, Pallas kernels for 3%

profile of v2, /device:TPU:1, one launch (start us, length us, event | category | flops | bytes accessed | tf_op | source)
XLA Modules:
  0.0 120.8 jit_solution(10869066760806327608)
XLA Ops:
  0.6 2.2 %collective-permute-start = (bf16[1,128,256]{2,1,0:T(8,128)(2,1)}, bf16[1,128,256]{2,1,0:T(8,128)(2,1)S(1)}, u32[]{:S(2)}, u32[]{:S(2)}) collective-permute-start(bf16[1,128,256]{2,1,0:T(8,128)(2,1)} %bitcast.47), channel_id=1, source_target_pairs={{0,8},{1,33},{2,10},{3,35},{4,12},{5,37},{6,14},{7,39},{8,16},{9,4... | collective-permute-start | bytes 196616 | tf_op jit(solution)/shard_map/ppermute | solution.py:36
  2.8 2.6 %collective-permute-start.1 = (bf16[1,128,256]{2,1,0:T(8,128)(2,1)}, bf16[1,128,256]{2,1,0:T(8,128)(2,1)S(1)}, u32[]{:S(2)}, u32[]{:S(2)}) collective-permute-start(bf16[1,128,256]{2,1,0:T(8,128)(2,1)} %bitcast.48), channel_id=1, source_target_pairs={{0,16},{1,65},{2,18},{3,67},{4,20},{5,69},{6,22},{7,71},{8,24},{9,... | collective-permute-start | bytes 196616 | tf_op jit(solution)/shard_map/ppermute | solution.py:36
  6.5 3.6 %load.1.a_ref = bf16[512,8192]{1,0:T(8,128)(2,1)S(1)} custom-call(bf16[16,512,512]{2,1,0:T(8,128)(2,1)} %bitcast.52), custom_call_target="tpu_custom_call" | custom-call | bytes 16777216 | tf_op jit(solution)/shard_map/load/pallas_call | solution.py:77
  10.2 1.7 %collective-permute-start.3 = (bf16[4,128,256]{2,1,0:T(8,128)(2,1)S(1)}, bf16[4,128,256]{2,1,0:T(8,128)(2,1)S(1)}, u32[]{:S(2)}, u32[]{:S(2)}) collective-permute-start(bf16[4,128,256]{2,1,0:T(8,128)(2,1)S(1)} %join.2.refs_0_), channel_id=1, source_target_pairs={{0,32},{1,3},{2,34},{3,5},{4,36},{5,7},{6,38},{7,1},{8,40},{9,11},... | collective-permute-start | bytes 786440 | tf_op jit(solution)/shard_map/ppermute | solution.py:36
  11.9 3.3 %collective-permute-start.4 = (bf16[4,128,256]{2,1,0:T(8,128)(2,1)S(1)}, bf16[4,128,256]{2,1,0:T(8,128)(2,1)S(1)}, u32[]{:S(2)}, u32[]{:S(2)}) collective-permute-start(bf16[4,128,256]{2,1,0:T(8,128)(2,1)S(1)} %join.2.refs_0_), channel_id=1, source_target_pairs={{0,64},{1,5},{2,66},{3,7},{4,68},{5,1},{6,70},{7,3},{8,72},{9,13},... | collective-permute-start | bytes 786440 | tf_op jit(solution)/shard_map/ppermute | solution.py:36
  15.9 2.1 %collective-permute-done.3.refs_1_ = bf16[4,128,256]{2,1,0:T(8,128)(2,1)S(1)} collective-permute-done((bf16[4,128,256]{2,1,0:T(8,128)(2,1)S(1)}, bf16[4,128,256]{2,1,0:T(8,128)(2,1)S(1)}, u32[]{:S(2)}, u32[]{:S(2)}) %collective-permute-start.3) | collective-permute-done | bytes 262176 | tf_op jit(solution)/shard_map/ppermute | solution.py:36
  18.1 4.0 %collective-permute-done.4.refs_2_ = bf16[4,128,256]{2,1,0:T(8,128)(2,1)S(1)} collective-permute-done((bf16[4,128,256]{2,1,0:T(8,128)(2,1)S(1)}, bf16[4,128,256]{2,1,0:T(8,128)(2,1)S(1)}, u32[]{:S(2)}, u32[]{:S(2)}) %collective-permute-start.4) | collective-permute-done | bytes 262176 | tf_op jit(solution)/shard_map/ppermute | solution.py:36
  23.3 1.6 %collective-permute-start.7 = (bf16[8,128,256]{2,1,0:T(8,128)(2,1)S(1)}, bf16[8,128,256]{2,1,0:T(8,128)(2,1)S(1)}, u32[]{:S(2)}, u32[]{:S(2)}) collective-permute-start(bf16[8,128,256]{2,1,0:T(8,128)(2,1)S(1)} %get-tuple-element.20.rest_1_), channel_id=1, source_target_pairs={{0,6},{1,25},{2,0},{3,27},{4,2},{5,29},{6,4},{7,31},{8,14},{9,1},{... | collective-permute-start | bytes 1572872 | tf_op jit(solution)/shard_map/ppermute | solution.py:36
  24.9 2.7 %collective-permute-start.9 = (bf16[8,128,256]{2,1,0:T(8,128)(2,1)S(1)}, bf16[8,128,256]{2,1,0:T(8,128)(2,1)S(1)}, u32[]{:S(2)}, u32[]{:S(2)}) collective-permute-start(bf16[8,128,256]{2,1,0:T(8,128)(2,1)S(1)} %get-tuple-element.19.rest_0_), channel_id=1, source_target_pairs={{0,6},{1,25},{2,0},{3,27},{4,2},{5,29},{6,4},{7,31},{8,14},{9,1},{... | collective-permute-start | bytes 1572872 | tf_op jit(solution)/shard_map/ppermute | solution.py:36
  27.5 3.2 %collective-permute-start.12 = (bf16[8,128,256]{2,1,0:T(8,128)(2,1)S(1)}, bf16[8,128,256]{2,1,0:T(8,128)(2,1)S(1)}, u32[]{:S(2)}, u32[]{:S(2)}) collective-permute-start(bf16[8,128,256]{2,1,0:T(8,128)(2,1)S(1)} %get-tuple-element.19.rest_0_), channel_id=1, source_target_pairs={{0,1},{1,0},{2,3},{3,2},{4,5},{5,4},{6,7},{7,6},{8,9},{9,8},{10,11... | collective-permute-start | bytes 1572872 | tf_op jit(solution)/shard_map/ppermute | solution.py:44
  31.7 2.8 %collective-permute-start.13 = (bf16[8,128,256]{2,1,0:T(8,128)(2,1)S(1)}, bf16[8,128,256]{2,1,0:T(8,128)(2,1)S(1)}, u32[]{:S(2)}, u32[]{:S(2)}) collective-permute-start(bf16[8,128,256]{2,1,0:T(8,128)(2,1)S(1)} %get-tuple-element.20.rest_1_), channel_id=1, source_target_pairs={{0,1},{1,0},{2,3},{3,2},{4,5},{5,4},{6,7},{7,6},{8,9},{9,8},{10,11... | collective-permute-start | bytes 1572872 | tf_op jit(solution)/shard_map/ppermute | solution.py:44
  34.9 2.5 %collective-permute-done.8.rest_4_ = bf16[8,128,256]{2,1,0:T(8,128)(2,1)S(1)} collective-permute-done((bf16[8,128,256]{2,1,0:T(8,128)(2,1)S(1)}, bf16[8,128,256]{2,1,0:T(8,128)(2,1)S(1)}, u32[]{:S(2)}, u32[]{:S(2)}) %collective-permute-start.8) | collective-permute-done | bytes 524320 | tf_op jit(solution)/shard_map/ppermute | solution.py:36
  38.6 3.6 %collective-permute-start.14 = (bf16[8,128,256]{2,1,0:T(8,128)(2,1)S(1)}, bf16[8,128,256]{2,1,0:T(8,128)(2,1)S(1)}, u32[]{:S(2)}, u32[]{:S(2)}) collective-permute-start(bf16[8,128,256]{2,1,0:T(8,128)(2,1)S(1)} %collective-permute-done.6.rest_2_), channel_id=1, source_target_pairs={{0,1},{1,0},{2,3},{3,2},{4,5},{5,4},{6,7},{7,6},{8,9},{9,8},{10,11... | collective-permute-start | bytes 1572872 | tf_op jit(solution)/shard_map/ppermute | solution.py:44
  42.7 1.4 %collective-permute-done.10.rest_6_ = bf16[8,128,256]{2,1,0:T(8,128)(2,1)S(1)} collective-permute-done((bf16[8,128,256]{2,1,0:T(8,128)(2,1)S(1)}, bf16[8,128,256]{2,1,0:T(8,128)(2,1)S(1)}, u32[]{:S(2)}, u32[]{:S(2)}) %collective-permute-start.10) | collective-permute-done | bytes 524320 | tf_op jit(solution)/shard_map/ppermute | solution.py:36
  44.1 1.7 %collective-permute-start.17 = (bf16[8,128,256]{2,1,0:T(8,128)(2,1)S(1)}, bf16[8,128,256]{2,1,0:T(8,128)(2,1)S(1)}, u32[]{:S(2)}, u32[]{:S(2)}) collective-permute-start(bf16[8,128,256]{2,1,0:T(8,128)(2,1)S(1)} %collective-permute-done.9.rest_5_), channel_id=1, source_target_pairs={{0,1},{1,0},{2,3},{3,2},{4,5},{5,4},{6,7},{7,6},{8,9},{9,8},{10,11... | collective-permute-start | bytes 1572872 | tf_op jit(solution)/shard_map/ppermute | solution.py:44
  45.8 3.6 %collective-permute-start.18 = (bf16[8,128,256]{2,1,0:T(8,128)(2,1)S(1)}, bf16[8,128,256]{2,1,0:T(8,128)(2,1)S(1)}, u32[]{:S(2)}, u32[]{:S(2)}) collective-permute-start(bf16[8,128,256]{2,1,0:T(8,128)(2,1)S(1)} %collective-permute-done.10.rest_6_), channel_id=1, source_target_pairs={{0,1},{1,0},{2,3},{3,2},{4,5},{5,4},{6,7},{7,6},{8,9},{9,8},{10,11... | collective-permute-start | bytes 1572872 | tf_op jit(solution)/shard_map/ppermute | solution.py:44
  51.7 8.0 %layer.1 = (bf16[512,256]{1,0:T(8,128)(2,1)S(1)}, bf16[8,4096,128]{2,1,0:T(8,128)(2,1)S(1)}, bf16[2,272,128]{2,1,0:T(8,128)(2,1)S(1)}) custom-call(s32[1,16]{1,0:T(1,128)S(1)} %copy-done.4, s32[1]{0:T(128)S(6)} %copy.12.count_ref, bf16[512,8192]{1,0:T(8,128)(2,1)S(1)} %load.1.a_ref, bf16[256,256]{1,0:T(8,128)(2,1)S(1)} %copy-done, f32[1,256]{1,0:T(1,128)S(1)} %bitcast.51, ...), custom_call_target="tpu_custom_call" | custom-call | flops 4294967296 | bytes 8388608 | tf_op jit(solution)/shard_map/layer/pallas_call | solution.py:165
  60.7 2.0 %collective-permute-done.21.eb = bf16[272,128]{1,0:T(8,128)(2,1)S(1)} collective-permute-done((bf16[272,128]{1,0:T(8,128)(2,1)S(1)}, bf16[272,128]{1,0:T(8,128)(2,1)S(1)}, u32[]{:S(2)}, u32[]{:S(2)}) %collective-permute-start.21) | collective-permute-done | bytes 69664 | tf_op jit(solution)/shard_map/ppermute | solution.py:44
  64.0 1.8 %collective-permute-start.28 = (bf16[2320,128]{1,0:T(8,128)(2,1)S(1)}, bf16[2320,128]{1,0:T(8,128)(2,1)S(1)}, u32[]{:S(2)}, u32[]{:S(2)}) collective-permute-start(bf16[2320,128]{1,0:T(8,128)(2,1)S(1)} %get-tuple-element.29), channel_id=1, source_target_pairs={{0,6},{1,25},{2,0},{3,27},{4,2},{5,29},{6,4},{7,31},{8,14},{9,1},{... | collective-permute-start | bytes 1781768 | tf_op jit(solution)/shard_map/ppermute | solution.py:36
  65.9 1.9 %collective-permute-start.22 = (bf16[4096,128]{1,0:T(8,128)(2,1)S(1)}, bf16[4096,128]{1,0:T(8,128)(2,1)S(1)}, u32[]{:S(2)}, u32[]{:S(2)}) collective-permute-start(bf16[4096,128]{1,0:T(8,128)(2,1)S(1)} %get-tuple-element.42), channel_id=1, source_target_pairs={{0,1},{1,0},{2,3},{3,2},{4,5},{5,4},{6,7},{7,6},{8,9},{9,8},{10,11... | collective-permute-start | bytes 3145736 | tf_op jit(solution)/shard_map/ppermute | solution.py:44
  67.8 5.2 %collective-permute-done.28 = bf16[2320,128]{1,0:T(8,128)(2,1)S(1)} collective-permute-done((bf16[2320,128]{1,0:T(8,128)(2,1)S(1)}, bf16[2320,128]{1,0:T(8,128)(2,1)S(1)}, u32[]{:S(2)}, u32[]{:S(2)}) %collective-permute-start.28) | collective-permute-done | bytes 593952 | tf_op jit(solution)/shard_map/ppermute | solution.py:36
  73.7 2.4 %collective-permute-done.26.got = bf16[2320,128]{1,0:T(8,128)(2,1)S(1)} collective-permute-done((bf16[2320,128]{1,0:T(8,128)(2,1)S(1)}, bf16[2320,128]{1,0:T(8,128)(2,1)S(1)}, u32[]{:S(2)}, u32[]{:S(2)}) %collective-permute-start.26) | collective-permute-done | bytes 593952 | tf_op jit(solution)/shard_map/ppermute | solution.py:36
  76.6 2.7 %collective-permute-start.31 = (bf16[2048,128]{1,0:T(8,128)(2,1)S(1)}, bf16[2048,128]{1,0:T(8,128)(2,1)S(1)}, u32[]{:S(2)}, u32[]{:S(2)}) collective-permute-start(bf16[2048,128]{1,0:T(8,128)(2,1)S(1)} %passed_terms.3), channel_id=1, source_target_pairs={{0,6},{1,25},{2,0},{3,27},{4,2},{5,29},{6,4},{7,31},{8,14},{9,1},{... | collective-permute-start | bytes 1572872 | tf_op jit(solution)/shard_map/ppermute | solution.py:36
  79.6 10.0 %collective-permute-done.27 = bf16[2320,128]{1,0:T(8,128)(2,1)S(1)} collective-permute-done((bf16[2320,128]{1,0:T(8,128)(2,1)S(1)}, bf16[2320,128]{1,0:T(8,128)(2,1)S(1)}, u32[]{:S(2)}, u32[]{:S(2)}) %collective-permute-start.27) | collective-permute-done | bytes 593952 | tf_op jit(solution)/shard_map/ppermute | solution.py:36
  89.7 1.4 %collective-permute-done.24 = bf16[2048,128]{1,0:T(8,128)(2,1)S(1)} collective-permute-done((bf16[2048,128]{1,0:T(8,128)(2,1)S(1)}, bf16[2048,128]{1,0:T(8,128)(2,1)S(1)}, u32[]{:S(2)}, u32[]{:S(2)}) %collective-permute-start.24) | collective-permute-done | bytes 524320 | tf_op jit(solution)/shard_map/ppermute | solution.py:36
  91.9 2.7 %collective-permute-start.32 = (bf16[1296,128]{1,0:T(8,128)(2,1)S(1)}, bf16[1296,128]{1,0:T(8,128)(2,1)S(1)}, u32[]{:S(2)}, u32[]{:S(2)}) collective-permute-start(bf16[1296,128]{1,0:T(8,128)(2,1)S(1)} %get-tuple-element.63), channel_id=1, source_target_pairs={{0,96},{1,7},{2,98},{3,1},{4,100},{5,3},{6,102},{7,5},{8,104},{9,1... | collective-permute-start | bytes 995336 | tf_op jit(solution)/shard_map/ppermute | solution.py:36
  95.8 3.3 %collective-permute-done.29 = bf16[1296,128]{1,0:T(8,128)(2,1)S(1)} collective-permute-done((bf16[1296,128]{1,0:T(8,128)(2,1)S(1)}, bf16[1296,128]{1,0:T(8,128)(2,1)S(1)}, u32[]{:S(2)}, u32[]{:S(2)}) %collective-permute-start.29) | collective-permute-done | bytes 331808 | tf_op jit(solution)/shard_map/ppermute | solution.py:36
  99.1 3.2 %collective-permute-done.32 = bf16[1296,128]{1,0:T(8,128)(2,1)S(1)} collective-permute-done((bf16[1296,128]{1,0:T(8,128)(2,1)S(1)}, bf16[1296,128]{1,0:T(8,128)(2,1)S(1)}, u32[]{:S(2)}, u32[]{:S(2)}) %collective-permute-start.32) | collective-permute-done | bytes 331808 | tf_op jit(solution)/shard_map/ppermute | solution.py:36
  102.3 1.5 %collective-permute-done.33 = bf16[1296,128]{1,0:T(8,128)(2,1)S(1)} collective-permute-done((bf16[1296,128]{1,0:T(8,128)(2,1)S(1)}, bf16[1296,128]{1,0:T(8,128)(2,1)S(1)}, u32[]{:S(2)}, u32[]{:S(2)}) %collective-permute-start.33) | collective-permute-done | bytes 331808 | tf_op jit(solution)/shard_map/ppermute | solution.py:36
  104.2 1.4 %collective-permute-start.34 = (bf16[528,128]{1,0:T(8,128)(2,1)S(1)}, bf16[528,128]{1,0:T(8,128)(2,1)S(1)}, u32[]{:S(2)}, u32[]{:S(2)}) collective-permute-start(bf16[528,128]{1,0:T(8,128)(2,1)S(1)} %get-tuple-element.60), channel_id=1, source_target_pairs={{0,8},{1,33},{2,10},{3,35},{4,12},{5,37},{6,14},{7,39},{8,16},{9,4... | collective-permute-start | bytes 405512 | tf_op jit(solution)/shard_map/ppermute | solution.py:36
  109.5 2.8 %collective-permute-done.36 = bf16[528,128]{1,0:T(8,128)(2,1)S(1)} collective-permute-done((bf16[528,128]{1,0:T(8,128)(2,1)S(1)}, bf16[528,128]{1,0:T(8,128)(2,1)S(1)}, u32[]{:S(2)}, u32[]{:S(2)}) %collective-permute-start.36) | collective-permute-done | bytes 135200 | tf_op jit(solution)/shard_map/ppermute | solution.py:36
  112.4 6.1 %collective-permute-start.37 = (f32[264,128]{1,0:T(8,128)S(1)}, f32[264,128]{1,0:T(8,128)S(1)}, u32[]{:S(2)}, u32[]{:S(2)}) collective-permute-start(f32[264,128]{1,0:T(8,128)S(1)} %pad_maximum_fusion.11), channel_id=1, source_target_pairs={{0,1},{1,0},{2,3},{3,2},{4,5},{5,4},{6,7},{7,6},{8,9},{9,8},{10,11... | collective-permute-start | bytes 405512 | tf_op jit(solution)/shard_map/ppermute | solution.py:44
  (101 shorter events, 20.2 us)
Async XLA Ops:
  0.6 9.5 %collective-permute-start = (bf16[1,128,256]{2,1,0:T(8,128)(2,1)}, bf16[1,128,256]{2,1,0:T(8,128)(2,1)S(1)}, u32[]{:S(2)}, u32[]{:S(2)}) collective-permute-start(bf16[1,128,256]{2,1,0:T(8,128)(2,1)} %bitcast.47), channel_id=1, source_target_pairs={{0,8},{1,33},{2,10},{3,35},{4,12},{5,37},{6,14},{7,39},{8,16},{9,4... | collective-permute-start | bytes 196616 | tf_op jit(solution)/shard_map/ppermute | solution.py:36
  2.8 7.3 %collective-permute-start.1 = (bf16[1,128,256]{2,1,0:T(8,128)(2,1)}, bf16[1,128,256]{2,1,0:T(8,128)(2,1)S(1)}, u32[]{:S(2)}, u32[]{:S(2)}) collective-permute-start(bf16[1,128,256]{2,1,0:T(8,128)(2,1)} %bitcast.48), channel_id=1, source_target_pairs={{0,16},{1,65},{2,18},{3,67},{4,20},{5,69},{6,22},{7,71},{8,24},{9,... | collective-permute-start | bytes 196616 | tf_op jit(solution)/shard_map/ppermute | solution.py:36
  10.2 7.9 %collective-permute-start.3 = (bf16[4,128,256]{2,1,0:T(8,128)(2,1)S(1)}, bf16[4,128,256]{2,1,0:T(8,128)(2,1)S(1)}, u32[]{:S(2)}, u32[]{:S(2)}) collective-permute-start(bf16[4,128,256]{2,1,0:T(8,128)(2,1)S(1)} %join.2.refs_0_), channel_id=1, source_target_pairs={{0,32},{1,3},{2,34},{3,5},{4,36},{5,7},{6,38},{7,1},{8,40},{9,11},... | collective-permute-start | bytes 786440 | tf_op jit(solution)/shard_map/ppermute | solution.py:36
  11.9 10.2 %collective-permute-start.4 = (bf16[4,128,256]{2,1,0:T(8,128)(2,1)S(1)}, bf16[4,128,256]{2,1,0:T(8,128)(2,1)S(1)}, u32[]{:S(2)}, u32[]{:S(2)}) collective-permute-start(bf16[4,128,256]{2,1,0:T(8,128)(2,1)S(1)} %join.2.refs_0_), channel_id=1, source_target_pairs={{0,64},{1,5},{2,66},{3,7},{4,68},{5,1},{6,70},{7,3},{8,72},{9,13},... | collective-permute-start | bytes 786440 | tf_op jit(solution)/shard_map/ppermute | solution.py:36
  15.2 6.9 %collective-permute-start.5 = (bf16[4,128,256]{2,1,0:T(8,128)(2,1)S(1)}, bf16[4,128,256]{2,1,0:T(8,128)(2,1)S(1)}, u32[]{:S(2)}, u32[]{:S(2)}) collective-permute-start(bf16[4,128,256]{2,1,0:T(8,128)(2,1)S(1)} %join.2.refs_0_), channel_id=1, source_target_pairs={{0,96},{1,7},{2,98},{3,1},{4,100},{5,3},{6,102},{7,5},{8,104},{9,1... | collective-permute-start | bytes 786440 | tf_op jit(solution)/shard_map/ppermute | solution.py:36
  22.1 9.6 %collective-permute-start.6 = (bf16[8,128,256]{2,1,0:T(8,128)(2,1)S(1)}, bf16[8,128,256]{2,1,0:T(8,128)(2,1)S(1)}, u32[]{:S(2)}, u32[]{:S(2)}) collective-permute-start(bf16[8,128,256]{2,1,0:T(8,128)(2,1)S(1)} %get-tuple-element.19.rest_0_), channel_id=1, source_target_pairs={{0,2},{1,9},{2,4},{3,11},{4,6},{5,13},{6,0},{7,15},{8,10},{9,17},{... | collective-permute-start | bytes 1572872 | tf_op jit(solution)/shard_map/ppermute | solution.py:36
  23.3 11.3 %collective-permute-start.7 = (bf16[8,128,256]{2,1,0:T(8,128)(2,1)S(1)}, bf16[8,128,256]{2,1,0:T(8,128)(2,1)S(1)}, u32[]{:S(2)}, u32[]{:S(2)}) collective-permute-start(bf16[8,128,256]{2,1,0:T(8,128)(2,1)S(1)} %get-tuple-element.20.rest_1_), channel_id=1, source_target_pairs={{0,6},{1,25},{2,0},{3,27},{4,2},{5,29},{6,4},{7,31},{8,14},{9,1},{... | collective-permute-start | bytes 1572872 | tf_op jit(solution)/shard_map/ppermute | solution.py:36
  24.9 12.5 %collective-permute-start.8 = (bf16[8,128,256]{2,1,0:T(8,128)(2,1)S(1)}, bf16[8,128,256]{2,1,0:T(8,128)(2,1)S(1)}, u32[]{:S(2)}, u32[]{:S(2)}) collective-permute-start(bf16[8,128,256]{2,1,0:T(8,128)(2,1)S(1)} %get-tuple-element.20.rest_1_), channel_id=1, source_target_pairs={{0,2},{1,9},{2,4},{3,11},{4,6},{5,13},{6,0},{7,15},{8,10},{9,17},{... | collective-permute-start | bytes 1572872 | tf_op jit(solution)/shard_map/ppermute | solution.py:36
  24.9 13.7 %collective-permute-start.9 = (bf16[8,128,256]{2,1,0:T(8,128)(2,1)S(1)}, bf16[8,128,256]{2,1,0:T(8,128)(2,1)S(1)}, u32[]{:S(2)}, u32[]{:S(2)}) collective-permute-start(bf16[8,128,256]{2,1,0:T(8,128)(2,1)S(1)} %get-tuple-element.19.rest_0_), channel_id=1, source_target_pairs={{0,6},{1,25},{2,0},{3,27},{4,2},{5,29},{6,4},{7,31},{8,14},{9,1},{... | collective-permute-start | bytes 1572872 | tf_op jit(solution)/shard_map/ppermute | solution.py:36
  27.5 14.7 %collective-permute-start.12 = (bf16[8,128,256]{2,1,0:T(8,128)(2,1)S(1)}, bf16[8,128,256]{2,1,0:T(8,128)(2,1)S(1)}, u32[]{:S(2)}, u32[]{:S(2)}) collective-permute-start(bf16[8,128,256]{2,1,0:T(8,128)(2,1)S(1)} %get-tuple-element.19.rest_0_), channel_id=1, source_target_pairs={{0,1},{1,0},{2,3},{3,2},{4,5},{5,4},{6,7},{7,6},{8,9},{9,8},{10,11... | collective-permute-start | bytes 1572872 | tf_op jit(solution)/shard_map/ppermute | solution.py:44
  31.7 10.6 %collective-permute-start.13 = (bf16[8,128,256]{2,1,0:T(8,128)(2,1)S(1)}, bf16[8,128,256]{2,1,0:T(8,128)(2,1)S(1)}, u32[]{:S(2)}, u32[]{:S(2)}) collective-permute-start(bf16[8,128,256]{2,1,0:T(8,128)(2,1)S(1)} %get-tuple-element.20.rest_1_), channel_id=1, source_target_pairs={{0,1},{1,0},{2,3},{3,2},{4,5},{5,4},{6,7},{7,6},{8,9},{9,8},{10,11... | collective-permute-start | bytes 1572872 | tf_op jit(solution)/shard_map/ppermute | solution.py:44
  34.6 9.5 %collective-permute-start.10 = (bf16[8,128,256]{2,1,0:T(8,128)(2,1)S(1)}, bf16[8,128,256]{2,1,0:T(8,128)(2,1)S(1)}, u32[]{:S(2)}, u32[]{:S(2)}) collective-permute-start(bf16[8,128,256]{2,1,0:T(8,128)(2,1)S(1)} %collective-permute-done.6.rest_2_), channel_id=1, source_target_pairs={{0,2},{1,9},{2,4},{3,11},{4,6},{5,13},{6,0},{7,15},{8,10},{9,17},{... | collective-permute-start | bytes 1572872 | tf_op jit(solution)/shard_map/ppermute | solution.py:36
  37.3 8.5 %collective-permute-start.11 = (bf16[8,128,256]{2,1,0:T(8,128)(2,1)S(1)}, bf16[8,128,256]{2,1,0:T(8,128)(2,1)S(1)}, u32[]{:S(2)}, u32[]{:S(2)}) collective-permute-start(bf16[8,128,256]{2,1,0:T(8,128)(2,1)S(1)} %collective-permute-done.7.rest_3_), channel_id=1, source_target_pairs={{0,6},{1,25},{2,0},{3,27},{4,2},{5,29},{6,4},{7,31},{8,14},{9,1},{... | collective-permute-start | bytes 1572872 | tf_op jit(solution)/shard_map/ppermute | solution.py:36
  38.6 10.7 %collective-permute-start.14 = (bf16[8,128,256]{2,1,0:T(8,128)(2,1)S(1)}, bf16[8,128,256]{2,1,0:T(8,128)(2,1)S(1)}, u32[]{:S(2)}, u32[]{:S(2)}) collective-permute-start(bf16[8,128,256]{2,1,0:T(8,128)(2,1)S(1)} %collective-permute-done.6.rest_2_), channel_id=1, source_target_pairs={{0,1},{1,0},{2,3},{3,2},{4,5},{5,4},{6,7},{7,6},{8,9},{9,8},{10,11... | collective-permute-start | bytes 1572872 | tf_op jit(solution)/shard_map/ppermute | solution.py:44
  42.2 7.8 %collective-permute-start.15 = (bf16[8,128,256]{2,1,0:T(8,128)(2,1)S(1)}, bf16[8,128,256]{2,1,0:T(8,128)(2,1)S(1)}, u32[]{:S(2)}, u32[]{:S(2)}) collective-permute-start(bf16[8,128,256]{2,1,0:T(8,128)(2,1)S(1)} %collective-permute-done.7.rest_3_), channel_id=1, source_target_pairs={{0,1},{1,0},{2,3},{3,2},{4,5},{5,4},{6,7},{7,6},{8,9},{9,8},{10,11... | collective-permute-start | bytes 1572872 | tf_op jit(solution)/shard_map/ppermute | solution.py:44
  42.3 7.7 %collective-permute-start.16 = (bf16[8,128,256]{2,1,0:T(8,128)(2,1)S(1)}, bf16[8,128,256]{2,1,0:T(8,128)(2,1)S(1)}, u32[]{:S(2)}, u32[]{:S(2)}) collective-permute-start(bf16[8,128,256]{2,1,0:T(8,128)(2,1)S(1)} %collective-permute-done.8.rest_4_), channel_id=1, source_target_pairs={{0,1},{1,0},{2,3},{3,2},{4,5},{5,4},{6,7},{7,6},{8,9},{9,8},{10,11... | collective-permute-start | bytes 1572872 | tf_op jit(solution)/shard_map/ppermute | solution.py:44
  44.1 5.9 %collective-permute-start.17 = (bf16[8,128,256]{2,1,0:T(8,128)(2,1)S(1)}, bf16[8,128,256]{2,1,0:T(8,128)(2,1)S(1)}, u32[]{:S(2)}, u32[]{:S(2)}) collective-permute-start(bf16[8,128,256]{2,1,0:T(8,128)(2,1)S(1)} %collective-permute-done.9.rest_5_), channel_id=1, source_target_pairs={{0,1},{1,0},{2,3},{3,2},{4,5},{5,4},{6,7},{7,6},{8,9},{9,8},{10,11... | collective-permute-start | bytes 1572872 | tf_op jit(solution)/shard_map/ppermute | solution.py:44
  63.4 9.7 %collective-permute-start.25 = (bf16[4096,128]{1,0:T(8,128)(2,1)S(1)}, bf16[4096,128]{1,0:T(8,128)(2,1)S(1)}, u32[]{:S(2)}, u32[]{:S(2)}) collective-permute-start(bf16[4096,128]{1,0:T(8,128)(2,1)S(1)} %get-tuple-element.43), channel_id=1, source_target_pairs={{0,1},{1,0},{2,3},{3,2},{4,5},{5,4},{6,7},{7,6},{8,9},{9,8},{10,11... | collective-permute-start | bytes 3145736 | tf_op jit(solution)/shard_map/ppermute | solution.py:44
  63.9 12.5 %collective-permute-start.23 = (bf16[4096,128]{1,0:T(8,128)(2,1)S(1)}, bf16[4096,128]{1,0:T(8,128)(2,1)S(1)}, u32[]{:S(2)}, u32[]{:S(2)}) collective-permute-start(bf16[4096,128]{1,0:T(8,128)(2,1)S(1)} %get-tuple-element.44), channel_id=1, source_target_pairs={{0,1},{1,0},{2,3},{3,2},{4,5},{5,4},{6,7},{7,6},{8,9},{9,8},{10,11... | collective-permute-start | bytes 3145736 | tf_op jit(solution)/shard_map/ppermute | solution.py:44
  64.0 9.1 %collective-permute-start.28 = (bf16[2320,128]{1,0:T(8,128)(2,1)S(1)}, bf16[2320,128]{1,0:T(8,128)(2,1)S(1)}, u32[]{:S(2)}, u32[]{:S(2)}) collective-permute-start(bf16[2320,128]{1,0:T(8,128)(2,1)S(1)} %get-tuple-element.29), channel_id=1, source_target_pairs={{0,6},{1,25},{2,0},{3,27},{4,2},{5,29},{6,4},{7,31},{8,14},{9,1},{... | collective-permute-start | bytes 1781768 | tf_op jit(solution)/shard_map/ppermute | solution.py:36
  65.8 10.3 %collective-permute-start.26 = (bf16[2320,128]{1,0:T(8,128)(2,1)S(1)}, bf16[2320,128]{1,0:T(8,128)(2,1)S(1)}, u32[]{:S(2)}, u32[]{:S(2)}) collective-permute-start(bf16[2320,128]{1,0:T(8,128)(2,1)S(1)} %get-tuple-element.27), channel_id=1, source_target_pairs={{0,2},{1,9},{2,4},{3,11},{4,6},{5,13},{6,0},{7,15},{8,10},{9,17},{... | collective-permute-start | bytes 1781768 | tf_op jit(solution)/shard_map/ppermute | solution.py:36
  65.9 23.8 %collective-permute-start.22 = (bf16[4096,128]{1,0:T(8,128)(2,1)S(1)}, bf16[4096,128]{1,0:T(8,128)(2,1)S(1)}, u32[]{:S(2)}, u32[]{:S(2)}) collective-permute-start(bf16[4096,128]{1,0:T(8,128)(2,1)S(1)} %get-tuple-element.42), channel_id=1, source_target_pairs={{0,1},{1,0},{2,3},{3,2},{4,5},{5,4},{6,7},{7,6},{8,9},{9,8},{10,11... | collective-permute-start | bytes 3145736 | tf_op jit(solution)/shard_map/ppermute | solution.py:44
  73.3 16.4 %collective-permute-start.30 = (bf16[2048,128]{1,0:T(8,128)(2,1)S(1)}, bf16[2048,128]{1,0:T(8,128)(2,1)S(1)}, u32[]{:S(2)}, u32[]{:S(2)}) collective-permute-start(bf16[2048,128]{1,0:T(8,128)(2,1)S(1)} %direct_terms.3), channel_id=1, source_target_pairs={{0,2},{1,9},{2,4},{3,11},{4,6},{5,13},{6,0},{7,15},{8,10},{9,17},{... | collective-permute-start | bytes 1572872 | tf_op jit(solution)/shard_map/ppermute | solution.py:36
  76.3 13.4 %collective-permute-start.27 = (bf16[2320,128]{1,0:T(8,128)(2,1)S(1)}, bf16[2320,128]{1,0:T(8,128)(2,1)S(1)}, u32[]{:S(2)}, u32[]{:S(2)}) collective-permute-start(bf16[2320,128]{1,0:T(8,128)(2,1)S(1)} %passed_terms.2), channel_id=1, source_target_pairs={{0,2},{1,9},{2,4},{3,11},{4,6},{5,13},{6,0},{7,15},{8,10},{9,17},{... | collective-permute-start | bytes 1781768 | tf_op jit(solution)/shard_map/ppermute | solution.py:36
  76.6 13.1 %collective-permute-start.31 = (bf16[2048,128]{1,0:T(8,128)(2,1)S(1)}, bf16[2048,128]{1,0:T(8,128)(2,1)S(1)}, u32[]{:S(2)}, u32[]{:S(2)}) collective-permute-start(bf16[2048,128]{1,0:T(8,128)(2,1)S(1)} %passed_terms.3), channel_id=1, source_target_pairs={{0,6},{1,25},{2,0},{3,27},{4,2},{5,29},{6,4},{7,31},{8,14},{9,1},{... | collective-permute-start | bytes 1572872 | tf_op jit(solution)/shard_map/ppermute | solution.py:36
  79.5 11.6 %collective-permute-start.24 = (bf16[2048,128]{1,0:T(8,128)(2,1)S(1)}, bf16[2048,128]{1,0:T(8,128)(2,1)S(1)}, u32[]{:S(2)}, u32[]{:S(2)}) collective-permute-start(bf16[2048,128]{1,0:T(8,128)(2,1)S(1)} %direct_terms.2), channel_id=1, source_target_pairs={{0,6},{1,25},{2,0},{3,27},{4,2},{5,29},{6,4},{7,31},{8,14},{9,1},{... | collective-permute-start | bytes 1572872 | tf_op jit(solution)/shard_map/ppermute | solution.py:36
  91.9 7.2 %collective-permute-start.29 = (bf16[1296,128]{1,0:T(8,128)(2,1)S(1)}, bf16[1296,128]{1,0:T(8,128)(2,1)S(1)}, u32[]{:S(2)}, u32[]{:S(2)}) collective-permute-start(bf16[1296,128]{1,0:T(8,128)(2,1)S(1)} %get-tuple-element.62), channel_id=1, source_target_pairs={{0,32},{1,3},{2,34},{3,5},{4,36},{5,7},{6,38},{7,1},{8,40},{9,11},... | collective-permute-start | bytes 995336 | tf_op jit(solution)/shard_map/ppermute | solution.py:36
  91.9 10.3 %collective-permute-start.32 = (bf16[1296,128]{1,0:T(8,128)(2,1)S(1)}, bf16[1296,128]{1,0:T(8,128)(2,1)S(1)}, u32[]{:S(2)}, u32[]{:S(2)}) collective-permute-start(bf16[1296,128]{1,0:T(8,128)(2,1)S(1)} %get-tuple-element.63), channel_id=1, source_target_pairs={{0,96},{1,7},{2,98},{3,1},{4,100},{5,3},{6,102},{7,5},{8,104},{9,1... | collective-permute-start | bytes 995336 | tf_op jit(solution)/shard_map/ppermute | solution.py:36
  94.7 9.2 %collective-permute-start.33 = (bf16[1296,128]{1,0:T(8,128)(2,1)S(1)}, bf16[1296,128]{1,0:T(8,128)(2,1)S(1)}, u32[]{:S(2)}, u32[]{:S(2)}) collective-permute-start(bf16[1296,128]{1,0:T(8,128)(2,1)S(1)} %get-tuple-element.64), channel_id=1, source_target_pairs={{0,64},{1,5},{2,66},{3,7},{4,68},{5,1},{6,70},{7,3},{8,72},{9,13},... | collective-permute-start | bytes 995336 | tf_op jit(solution)/shard_map/ppermute | solution.py:36
  104.2 5.1 %collective-permute-start.34 = (bf16[528,128]{1,0:T(8,128)(2,1)S(1)}, bf16[528,128]{1,0:T(8,128)(2,1)S(1)}, u32[]{:S(2)}, u32[]{:S(2)}) collective-permute-start(bf16[528,128]{1,0:T(8,128)(2,1)S(1)} %get-tuple-element.60), channel_id=1, source_target_pairs={{0,8},{1,33},{2,10},{3,35},{4,12},{5,37},{6,14},{7,39},{8,16},{9,4... | collective-permute-start | bytes 405512 | tf_op jit(solution)/shard_map/ppermute | solution.py:36
  106.9 5.4 %collective-permute-start.36 = (bf16[528,128]{1,0:T(8,128)(2,1)S(1)}, bf16[528,128]{1,0:T(8,128)(2,1)S(1)}, u32[]{:S(2)}, u32[]{:S(2)}) collective-permute-start(bf16[528,128]{1,0:T(8,128)(2,1)S(1)} %get-tuple-element.61), channel_id=1, source_target_pairs={{0,16},{1,65},{2,18},{3,67},{4,20},{5,69},{6,22},{7,71},{8,24},{9,... | collective-permute-start | bytes 405512 | tf_op jit(solution)/shard_map/ppermute | solution.py:36
  112.4 7.1 %collective-permute-start.37 = (f32[264,128]{1,0:T(8,128)S(1)}, f32[264,128]{1,0:T(8,128)S(1)}, u32[]{:S(2)}, u32[]{:S(2)}) collective-permute-start(f32[264,128]{1,0:T(8,128)S(1)} %pad_maximum_fusion.11), channel_id=1, source_target_pairs={{0,1},{1,0},{2,3},{3,2},{4,5},{5,4},{6,7},{7,6},{8,9},{9,8},{10,11... | collective-permute-start | bytes 405512 | tf_op jit(solution)/shard_map/ppermute | solution.py:44
  (11 other events, 205.3 us)

commit v3 on v2

v3 whole, which is shorter than its diff:
```python
import functools

import jax
import jax.numpy as jnp
import numpy as np
from jax import lax
from jax.experimental import pallas as pl
from jax.experimental.pallas import tpu as pltpu
from jax.sharding import PartitionSpec as P

AXIS = "rows"
SIZES = (4, 4, 4, 2)
Y, X, Z = 0, 1, 2
PLANES = ((Y, Z), (Y, X))
LINE = (X, Z)
STEPS = ((Y, Z), (X, Y))
BF16 = jnp.bfloat16
F32 = jnp.float32
GROUP = 8
STARTS = ((0,), (16, 56), (24, 48), (32,), (40,))
DB = 16


def device(at):
    return int(np.ravel_multi_index([t % n for t, n in zip(at, SIZES)], SIZES))


def groups(axes):
    out = {}
    for i in range(128):
        at = [int(v) for v in np.unravel_index(i, SIZES)]
        own = axes[at[3]]
        key = tuple(-1 if a in own else at[a] for a in range(4))
        out.setdefault(key, []).append((tuple(at[a] for a in own), i))
    return [[i for _, i in sorted(members)] for _, members in sorted(out.items())]


def exchange(x, axes):
    return lax.all_to_all(
        x, AXIS, split_axis=0, concat_axis=0, tiled=True, axis_index_groups=groups(axes)
    )


def pairs(move):
    return [(i, device(move([int(v) for v in np.unravel_index(i, SIZES)]))) for i in range(128)]


def hop(x, axes, k):
    def move(at):
        at[axes[at[3]]] += k
        return at

    return lax.ppermute(x, AXIS, pairs(move))


def around(x, axes):
    return [hop(x, axes, k) for k in (3, 2, 1)]


def swap(x):
    def move(at):
        at[3] += 1
        return at

    return lax.ppermute(x, AXIS, pairs(move))


def dot(a, b, dims):
    return lax.dot_general(a, b, (dims, ((), ())), preferred_element_type=F32)


def load_kernel(a_hbm, a_ref, sem):
    copies = [
        pltpu.make_async_copy(a_hbm.at[s], a_ref.at[:, pl.ds(s * 512, 512)], sem.at[s])
        for s in range(16)
    ]
    for copy in copies:
        copy.start()
    for copy in copies:
        copy.wait()


def load(values):
    return pl.pallas_call(
        load_kernel,
        out_shape=pltpu.VMEM((512, 8192), BF16),
        in_specs=[pl.BlockSpec(memory_space=pltpu.HBM)],
        out_specs=pl.BlockSpec(memory_space=pltpu.VMEM),
        scratch_shapes=[pltpu.SemaphoreType.DMA((16,))],
        compiler_params=pltpu.CompilerParams(vmem_limit_bytes=1024 * 1024),
        cost_estimate=pl.CostEstimate(flops=0, bytes_accessed=2 * 8 * 2**20, transcendentals=0),
        name="load",
    )(pltpu.with_memory_space_constraint(values, pltpu.HBM))


def kernel(
    col_ref, count_ref, a_ref, w_ref, b_ref, cot_ref, *rest,
):
    blocks, (act_ref, r_ref, e_ref, g_buf, x_buf, acc, g_t) = rest[:10], rest[10:]
    count = count_ref[0]
    index = lax.axis_index(AXIS)
    me = (index >> 5, (index >> 3) & 3, (index >> 1) & 3)
    core = index & 1

    def there(t, zlo):
        return lax.shift_right_logical(t, 3), lax.shift_right_logical(t, 1) & 3, (t & 1) * 2 + zlo

    def source(t, zlo, cc):
        at = there(t, zlo)
        away = [(at[i] - me[i]) & 3 for i in range(3)]
        first, second = STEPS[cc]
        return (-away[LINE[cc]] & 3) * 16 + away[second] * 4 + away[first]

    def target(t, zlo, cc):
        at = there(t, zlo)
        away = [(at[i] - me[i]) & 3 for i in range(3)]
        first, second = STEPS[cc]
        return away[LINE[cc]], away[second] * 4 + away[first]

    for side in range(2):
        for ref, starts in zip(blocks[side * 5 : side * 5 + 5], STARTS):
            length = ref.shape[0] // len(starts)
            for i, start in enumerate(starts):
                g_buf[side, start : start + length] = ref[i * length : i * length + length]
    r_ref[...] = jnp.zeros_like(r_ref)
    acc[...] = jnp.zeros_like(acc)

    def forward(g, carry):
        for q in range(GROUP):
            s = g * GROUP + q
            t = col_ref[0, s]
            live = s < count
            for j in range(4):
                cc = j % 2
                at = source(t, j // 2, cc)
                piece = g_buf[jnp.where(core == cc, 0, 1), at]
                rows = slice(q * 512 + j * 128, q * 512 + j * 128 + 128)
                x_buf[rows] = jnp.where(live, piece, jnp.zeros_like(piece))
        columns = pl.ds(pl.multiple_of(g * (GROUP * 512), GROUP * 512), GROUP * 512)
        acc[...] += dot(a_ref[:, columns], x_buf[...], ((1,), (0,)))
        return carry

    lax.fori_loop(0, 16 // GROUP, forward, 0)

    agg = acc[...].astype(BF16)
    pre = dot(agg, w_ref[...], ((1,), (0,))) + b_ref[...]
    low = jnp.exp(jnp.minimum(pre, 0.0))
    act_ref[...] = jnp.where(pre > 0, pre, low - 1.0).astype(BF16)
    grad = (cot_ref[...].astype(F32) * low).astype(BF16)
    g_t[...] = grad.astype(F32).T.astype(BF16)
    dw = dot(agg, grad, ((0,), (0,)))
    db = jnp.sum(grad.astype(F32), axis=0, keepdims=True)
    for h in range(2):
        half = slice(h * 128, h * 128 + 128)
        side = jnp.where(core == h, 0, 1)
        e_ref[side, :256] = dw[:, half]
        e_ref[side, 256:] = jnp.broadcast_to(db[:, half], (8, 128))

    def backward(g, carry):
        for q in range(GROUP):
            s = g * GROUP + q
            t = col_ref[0, s]
            columns = pl.ds(pl.multiple_of(s * 512, 512), 512)
            part = dot(g_t[...], a_ref[:, columns], ((1,), (0,)))
            part = jnp.where(s < count, part, 0.0).astype(BF16)
            for j in range(4):
                cc = j % 2
                k3, k21 = target(t, j // 2, cc)
                rows = pl.ds(pl.multiple_of(k21 * 256, 256), 256)
                other = jnp.where(k3 == 0, 7, jnp.where(k3 == 1, 5, jnp.where(k3 == 2, 4, 6)))
                r_ref[jnp.where(core == cc, k3, other), rows] = part[:, j * 128 : j * 128 + 128]
        return carry

    lax.fori_loop(0, 16 // GROUP, backward, 0)


def local(cols, count, values, weight, bias, cotangent, blocks):
    vmem = pl.BlockSpec(memory_space=pltpu.VMEM)
    return pl.pallas_call(
        kernel,
        out_shape=(
            pltpu.VMEM((512, 256), BF16),
            pltpu.VMEM((8, 4096, 128), BF16),
            pltpu.VMEM((2, 264, 128), F32),
        ),
        in_specs=[pl.BlockSpec(memory_space=pltpu.SMEM)] * 2 + [vmem] * 14,
        out_specs=(vmem,) * 3,
        scratch_shapes=[
            pltpu.VMEM((2, 64, 128, 256), BF16),
            pltpu.VMEM((GROUP * 512, 256), BF16),
            pltpu.VMEM((512, 256), F32),
            pltpu.VMEM((256, 512), BF16),
        ],
        compiler_params=pltpu.CompilerParams(vmem_limit_bytes=18 * 1024 * 1024),
        cost_estimate=pl.CostEstimate(
            flops=2 * 2 * 16 * 512 * 512 * 256, bytes_accessed=8 * 2**20, transcendentals=512 * 256
        ),
        name="layer",
    )(cols, count, values, weight, bias, cotangent, *blocks)


def in_vmem(name, body, outs, *ins, last=False):
    vmem = pl.BlockSpec(memory_space=pltpu.VMEM)
    size = sum(int(np.prod(o.shape)) * 2 for o in (*outs, *ins))
    return pl.pallas_call(
        body,
        out_shape=tuple(o if last else pltpu.VMEM(o.shape, o.dtype) for o in outs),
        in_specs=[vmem] * len(ins),
        out_specs=(vmem,) * len(outs),
        compiler_params=pltpu.CompilerParams(vmem_limit_bytes=4 * 1024 * 1024),
        cost_estimate=pl.CostEstimate(flops=0, bytes_accessed=size // 4, transcendentals=0),
        name=name,
    )(*ins)


def like(*shape, dtype=BF16):
    return jax.ShapeDtypeStruct(shape, dtype)


def widened(*parts):
    total = parts[0].astype(F32)
    for part in parts[1:]:
        total = total + part.astype(F32)
    return total


def join(*parts):
    def body(*refs):
        at = 0
        for ref in refs[:-1]:
            refs[-1][at : at + ref.shape[0]] = ref[...]
            at += ref.shape[0]

    rows = sum(p.shape[0] for p in parts)
    return in_vmem("join", body, [like(rows, *parts[0].shape[1:])], *parts)[0]


def halves(x, lower, upper):
    lower[...] = x[:8]
    upper[...] = x[8:]


def add_rows(o, start, *parts):
    o[start : start + 256] = widened(*[ref[at : at + 256] for ref, at in parts]).astype(BF16)


def split(v):
    hi = v.astype(BF16).astype(F32)
    return hi, v - hi


def first_terms(r, t, e, te, o1, o3, ride):
    total = e[0] + te[...]
    hi, low = split(total[256:])
    ride[:256] = total[:256].astype(BF16)
    ride[256:] = jnp.concatenate([hi, low]).astype(BF16)
    for at in range(0, 2048, 256):
        add_rows(o1, at, (r.at[2], at), (t, at))
        add_rows(o3, at, (r.at[2], at + 2048), (t, at + 2048))
    o1[2048:] = ride[...]
    o3[2048:] = ride[...]


def extra_pieces(e, te, via1, via3, far, o):
    total = e[0] + te[...]
    dw = total[:256] + widened(via1[2048:2304], via3[2048:2304], far[:256])
    db = total[256:] + widened(via1[2304:2312], via1[2312:], via3[2304:2312], via3[2312:], far[256:264], far[264:])
    for i in range(16):
        o[i, :DB] = dw[i * 16 : i * 16 + 16]
        o[i, DB:] = db


def second_terms(r, t, via1, via3, _pieces, p1, p3):
    for at in range(0, 2048, 256):
        up = at + 2048
        add_rows(p1, at, (r.at[1], at), (t.at[0], at), (via1, at))
        add_rows(p1, up, (r.at[1], up), (t.at[0], up))
        add_rows(p3, at, (r.at[3], at), (t.at[1], at))
        add_rows(p3, up, (r.at[3], up), (t.at[1], up), (via3, at))


def line_sum(r, t0, p1, p3, got, own, piece, m1, m2, m3):
    total = got[0]
    for i in range(1, 16):
        total = total + got[i]
    total = total * 65536 ** (-0.5)
    hi, low = split(total[DB:])
    piece[...] = jnp.concatenate([total[:DB], hi, low]).astype(BF16)
    for k, message in enumerate((None, m1, m2, m3)):
        for at in range(0, 1024, 256):
            rows = slice(k * 1024 + at, k * 1024 + at + 256)
            terms = widened(r[0, rows], t0[rows], p1[rows], p3[rows])
            if message is None:
                own[at : at + 256] = terms
            else:
                message[at : at + 256] = terms.astype(BF16)
        if message is not None:
            message[1024:] = piece[...]


def plane_sum(own, piece, g1, g2, g3, rest, pieces, n1, n2, n3):
    for i, ref in enumerate((piece, g1, g2, g3)):
        pieces[i * 32 : i * 32 + 32] = ref[-32:]
    for k, message in enumerate((None, n1, n2, n3)):
        rows = slice(k * 256, k * 256 + 256)
        terms = own[rows] + widened(g1[rows], g2[rows], g3[rows])
        if message is None:
            rest[...] = terms
        else:
            message[:256] = terms.astype(BF16)
            message[256:] = pieces[...]


def extra_half(pieces, h1, h2, h3, o):
    index = lax.axis_index(AXIS)
    at = (index >> 5, (index >> 3) & 3, (index >> 1) & 3)

    def choose(axes):
        return jnp.where((index & 1) == 0, at[axes[0]], at[axes[1]])

    first, second = (choose(axes) for axes in zip(*STEPS))
    flip = [STEPS[c] != PLANES[c] for c in range(2)]
    flip = jnp.where((index & 1) == 0, int(flip[0]), int(flip[1])) == 1
    for k1, (ref, base) in enumerate(((pieces, 0), (h1, 256), (h2, 256), (h3, 256))):
        for k2 in range(4):
            i, j = (first - k1) & 3, (second - k2) & 3
            place = jnp.where(flip, j * 4 + i, i * 4 + j)
            start = base + k2 * 32
            o[pl.ds(pl.multiple_of(place * 16, 16), 16)] = ref[start : start + DB].astype(F32)
    o[256:] = widened(pieces[DB : DB + 8], pieces[DB + 8 : DB + 16])


def extra_both(core, own, other, dw, db):
    here = core == 0
    first = jnp.where(here, own[...], other[...])
    second = jnp.where(here, other[...], own[...])
    dw[:, :128], dw[:, 128:] = first[:256], second[:256]
    db[:, :128], db[:, 128:] = first[256:257], second[256:257]


def finish(rest, h1, h2, h3, w, o):
    total = rest[...] + widened(h1[:256], h2[:256], h3[:256])
    o[...] = dot(total.T.astype(BF16), w[...], ((1,), (1,)))


def keep(x_ref, o_ref, sem):
    copy = pltpu.make_async_copy(x_ref, o_ref, sem)
    copy.start()
    copy.wait()


def to_output(x):
    return pl.pallas_call(
        keep,
        out_shape=like(*x.shape),
        in_specs=[pl.BlockSpec(memory_space=pltpu.VMEM)],
        out_specs=pl.BlockSpec(memory_space=pltpu.HBM),
        scratch_shapes=[pltpu.SemaphoreType.DMA],
        compiler_params=pltpu.CompilerParams(vmem_limit_bytes=1024 * 1024),
        name="to_output",
    )(x)


def on_device(features, tile_values, tile_col, tile_count, weight, bias, cotangent):
    values = load(tile_values[0])
    held = features[None]
    first, second = zip(*STEPS)
    held = join(held, *around(held, first))
    held, values = lax.optimization_barrier((held, values))
    held = join(held, *around(held, second))
    h1, h2 = in_vmem("halves", halves, [like(8, 128, 256)] * 2, held)
    a1, b2, a2, b1 = hop(h1, LINE, 1), hop(h2, LINE, 3), hop(h2, LINE, 1), hop(h1, LINE, 3)
    a1, b2, other = lax.optimization_barrier((a1, b2, held))
    c1, c2 = hop(a1, LINE, 1), hop(b2, LINE, 3)
    mine = [held, join(a1, b2), join(a2, b1), c1, c2]
    theirs = [swap(other)] + [swap(g) for g in mine[1:]]
    activation, r_all, e_all = local(
        tile_col, tile_count, values, weight, bias[None], cotangent, mine + theirs
    )

    some, whole = like(2048 + 272, 128), like(4096, 128)
    e_theirs = swap(e_all[1])
    o1, o3, ride = in_vmem(
        "first_terms", first_terms, [some, some, like(272, 128)],
        r_all, swap(r_all[4]), e_all, e_theirs,
    )
    o1, o3, ride, beside, activation = lax.optimization_barrier(
        (o1, o3, ride, r_all[5:7], activation)
    )
    via1, via3, far = hop(o1, LINE, 1), hop(o3, LINE, 3), hop(ride, LINE, 2)
    beside = swap(beside)
    activation = to_output(activation)
    pieces = in_vmem(
        "extra_pieces", extra_pieces, [like(16, 24, 128, dtype=F32)],
        e_all, e_theirs, via1, via3, far,
    )[0]
    p1, p3 = in_vmem(
        "second_terms", second_terms, [whole, whole], r_all, beside, via1, via3, pieces
    )
    p1, p3, pieces, activation, own = lax.optimization_barrier(
        (p1, p3, pieces, activation, r_all[7])
    )
    p1, p3 = hop(p1, LINE, 1), hop(p3, LINE, 3)
    pieces = exchange(pieces, PLANES)
    own, piece, *sent = in_vmem(
        "line_sum", line_sum, [like(1024, 128, dtype=F32), like(32, 128)] + [like(1056, 128)] * 3,
        r_all, swap(own), p1, p3, pieces,
    )
    got = [hop(m, second, k) for k, m in zip((1, 2, 3), sent)]
    rest, pieces, *sent = in_vmem(
        "plane_sum", plane_sum, [like(256, 128, dtype=F32), like(128, 128)] + [like(384, 128)] * 3,
        own, piece, *got,
    )
    got = [hop(m, first, k) for k, m in zip((1, 2, 3), sent)]
    own = in_vmem("extra_half", extra_half, [like(264, 128, dtype=F32)], pieces, *got)[0]
    other = swap(own)
    grad_features = in_vmem(
        "finish", finish, [like(128, 256, dtype=F32)], rest, *got, weight, last=True
    )[0]
    grad_weight, grad_bias = extras(own, other)
    return activation, grad_weight, grad_bias[0], grad_features


def extras(own, other):
    vmem = pl.BlockSpec(memory_space=pltpu.VMEM)

    def body(own, other, dw, db):
        extra_both(lax.axis_index(AXIS) & 1, own, other, dw, db)

    return pl.pallas_call(
        body,
        out_shape=(like(256, 256, dtype=F32), like(1, 256, dtype=F32)),
        in_specs=[vmem] * 2,
        out_specs=(vmem,) * 2,
        compiler_params=pltpu.CompilerParams(vmem_limit_bytes=4 * 1024 * 1024),
        name="extras",
    )(own, other)


def solution(mesh):
    in_specs = (
        P("rows", None),
        P("rows", None, None, None),
        P("rows", None),
        P("rows"),
        P(),
        P(),
        P("rows", None),
    )
    out_specs = (P("rows", None), P(), P(), P("rows", None))
    return jax.shard_map(
        on_device, mesh=mesh, in_specs=in_specs, out_specs=out_specs, check_vma=False
    )
```

time: 121 us -> 114 us (0.942)
  blocking collectives: 0 us -> 13.5 us
  waiting for transfers between devices: 45 us -> 33.8 us
  starting transfers between devices: 56.5 us -> 48.7 us
  Pallas kernels: 12.8 us -> 16.1 us
  other arithmetic: 2.42 us -> 0 us
  local copies, waits for them, and re-layouts: 1.54 us -> 0.3 us
    all_to_all x0 -> x1, blocking collectives: none -> 13.5 us  [exchange(): lax.all_to_all(x, AXIS, split_axis=0, concat_axis=0, tiled=True, axis_ind...]
    ppermute x24 -> x23, waiting for transfers between devices: 41.3 us -> 30.2 us  [hop(): return lax.ppermute(x, AXIS, pairs(move))]
    ppermute x14 -> x10, starting transfers between devices: 24.8 us -> 16.9 us  [swap(): return lax.ppermute(x, AXIS, pairs(move))]
    pallas_call x7 -> x14, Pallas kernels: 1.26 us -> 4.39 us  [the longest x12 2.95 us: in_vmem(): pl.pallas_call(body, out_shape=tuple((o if last else pltpu.VMEM(o.shape,...]
    concatenate x5 -> x0, other arithmetic: 1.4 us -> none  [the longest x2 1.28 us: on_device(): both = jnp.concatenate([first, second], axis=1)]
    ppermute x14 -> x10, waiting for transfers between devices: 3.74 us -> 3.59 us  [swap(): return lax.ppermute(x, AXIS, pairs(move))]
    ppermute x24 -> x23, starting transfers between devices: 31.7 us -> 31.8 us  [hop(): return lax.ppermute(x, AXIS, pairs(move))]
  transfers between devices with their start and end apart: 38 -> 33, of which waited for: 19 -> 15; matrix products, arithmetic and copies ran while one was open for 2% -> 0% of each run, Pallas kernels for 3% -> 5%
where the time goes in v3:
time: 114 us
  starting transfers between devices  48.7 us (43%)
  waiting for transfers between devices  33.8 us (30%)
  Pallas kernels  16.1 us (14%)
  blocking collectives  13.5 us (12%)
  between operations  1.5 us (1%)
    ppermute x23, starting transfers between devices, hop(): return lax.ppermute(x, AXIS, pairs(move))  31.8 us
    ppermute x23, waiting for transfers between devices, hop(): return lax.ppermute(x, AXIS, pairs(move))  30.2 us
    ppermute x10, starting transfers between devices, swap(): return lax.ppermute(x, AXIS, pairs(move))  16.9 us
    all_to_all x1, blocking collectives, exchange(): lax.all_to_all(x, AXIS, split_axis=0, concat_axis=0, tiled=True, axis_ind...  13.5 us
    pallas_call x1, Pallas kernels, local(): pl.pallas_call(kernel, out_shape=(pltpu.VMEM((512, 256), BF16), pltpu.VME...  8.15 us
    ppermute x10, waiting for transfers between devices, swap(): return lax.ppermute(x, AXIS, pairs(move))  3.59 us
    pallas_call x1, Pallas kernels, load(): pl.pallas_call(load_kernel, out_shape=pltpu.VMEM((512, 8192), BF16), in_s...  3.56 us
    pallas_call x12, Pallas kernels, in_vmem(): pl.pallas_call(body, out_shape=tuple((o if last else pltpu.VMEM(o.shape,...  2.95 us
  transfers between devices with their start and end apart: 33, of which 15 were waited for; matrix products, arithmetic and copies ran while one was open for 0% of the time, Pallas kernels for 5%

profile of v3, /device:TPU:1, one launch (start us, length us, event | category | flops | bytes accessed | tf_op | source)
XLA Modules:
  0.0 114.0 jit_solution(7028151351011314455)
XLA Ops:
  0.6 2.1 %collective-permute-start.2 = (bf16[1,128,256]{2,1,0:T(8,128)(2,1)}, bf16[1,128,256]{2,1,0:T(8,128)(2,1)S(1)}, u32[]{:S(2)}, u32[]{:S(2)}) collective-permute-start(bf16[1,128,256]{2,1,0:T(8,128)(2,1)} %bitcast.10), channel_id=1, source_target_pairs={{0,32},{1,9},{2,34},{3,11},{4,36},{5,13},{6,38},{7,15},{8,40},{9,1... | collective-permute-start | bytes 196616 | tf_op jit(solution)/shard_map/ppermute | solution.py:53
  2.7 2.5 %collective-permute-start.1 = (bf16[1,128,256]{2,1,0:T(8,128)(2,1)}, bf16[1,128,256]{2,1,0:T(8,128)(2,1)S(1)}, u32[]{:S(2)}, u32[]{:S(2)}) collective-permute-start(bf16[1,128,256]{2,1,0:T(8,128)(2,1)} %bitcast.11), channel_id=1, source_target_pairs={{0,64},{1,17},{2,66},{3,19},{4,68},{5,21},{6,70},{7,23},{8,72},{9,... | collective-permute-start | bytes 196616 | tf_op jit(solution)/shard_map/ppermute | solution.py:53
  6.4 3.6 %load.1.a_ref = bf16[512,8192]{1,0:T(8,128)(2,1)S(1)} custom-call(bf16[16,512,512]{2,1,0:T(8,128)(2,1)} %bitcast.15), custom_call_target="tpu_custom_call" | custom-call | bytes 16777216 | tf_op jit(solution)/shard_map/load/pallas_call | solution.py:84
  10.0 1.4 %collective-permute-start.5 = (bf16[4,128,256]{2,1,0:T(8,128)(2,1)S(1)}, bf16[4,128,256]{2,1,0:T(8,128)(2,1)S(1)}, u32[]{:S(2)}, u32[]{:S(2)}) collective-permute-start(bf16[4,128,256]{2,1,0:T(8,128)(2,1)S(1)} %join.4.refs_0_), channel_id=1, source_target_pairs={{0,2},{1,33},{2,4},{3,35},{4,6},{5,37},{6,0},{7,39},{8,10},{9,41},... | collective-permute-start | bytes 786440 | tf_op jit(solution)/shard_map/ppermute | solution.py:53
  11.4 2.6 %collective-permute-start.4 = (bf16[4,128,256]{2,1,0:T(8,128)(2,1)S(1)}, bf16[4,128,256]{2,1,0:T(8,128)(2,1)S(1)}, u32[]{:S(2)}, u32[]{:S(2)}) collective-permute-start(bf16[4,128,256]{2,1,0:T(8,128)(2,1)S(1)} %join.4.refs_0_), channel_id=1, source_target_pairs={{0,4},{1,65},{2,6},{3,67},{4,0},{5,69},{6,2},{7,71},{8,12},{9,73},... | collective-permute-start | bytes 786440 | tf_op jit(solution)/shard_map/ppermute | solution.py:53
  15.1 1.5 %collective-permute-done.5.refs_3_ = bf16[4,128,256]{2,1,0:T(8,128)(2,1)S(1)} collective-permute-done((bf16[4,128,256]{2,1,0:T(8,128)(2,1)S(1)}, bf16[4,128,256]{2,1,0:T(8,128)(2,1)S(1)}, u32[]{:S(2)}, u32[]{:S(2)}) %collective-permute-start.5) | collective-permute-done | bytes 262176 | tf_op jit(solution)/shard_map/ppermute | solution.py:53
  16.6 4.0 %collective-permute-done.4.refs_2_ = bf16[4,128,256]{2,1,0:T(8,128)(2,1)S(1)} collective-permute-done((bf16[4,128,256]{2,1,0:T(8,128)(2,1)S(1)}, bf16[4,128,256]{2,1,0:T(8,128)(2,1)S(1)}, u32[]{:S(2)}, u32[]{:S(2)}) %collective-permute-start.4) | collective-permute-done | bytes 262176 | tf_op jit(solution)/shard_map/ppermute | solution.py:53
  20.7 1.7 %collective-permute-start.6 = (bf16[8,128,256]{2,1,0:T(8,128)(2,1)S(1)}, bf16[8,128,256]{2,1,0:T(8,128)(2,1)S(1)}, u32[]{:S(2)}, u32[]{:S(2)}) collective-permute-start(bf16[8,128,256]{2,1,0:T(8,128)(2,1)S(1)} %get-tuple-element.43), channel_id=1, source_target_pairs={{0,8},{1,3},{2,10},{3,5},{4,12},{5,7},{6,14},{7,1},{8,16},{9,11},{... | collective-permute-start | bytes 1572872 | tf_op jit(solution)/shard_map/ppermute | solution.py:53
  22.4 2.2 %collective-permute-start.7 = (bf16[8,128,256]{2,1,0:T(8,128)(2,1)S(1)}, bf16[8,128,256]{2,1,0:T(8,128)(2,1)S(1)}, u32[]{:S(2)}, u32[]{:S(2)}) collective-permute-start(bf16[8,128,256]{2,1,0:T(8,128)(2,1)S(1)} %get-tuple-element.44), channel_id=1, source_target_pairs={{0,24},{1,7},{2,26},{3,1},{4,28},{5,3},{6,30},{7,5},{8,0},{9,15},{... | collective-permute-start | bytes 1572872 | tf_op jit(solution)/shard_map/ppermute | solution.py:53
  24.6 1.4 %collective-permute-start.9 = (bf16[8,128,256]{2,1,0:T(8,128)(2,1)S(1)}, bf16[8,128,256]{2,1,0:T(8,128)(2,1)S(1)}, u32[]{:S(2)}, u32[]{:S(2)}) collective-permute-start(bf16[8,128,256]{2,1,0:T(8,128)(2,1)S(1)} %get-tuple-element.43), channel_id=1, source_target_pairs={{0,24},{1,7},{2,26},{3,1},{4,28},{5,3},{6,30},{7,5},{8,0},{9,15},{... | collective-permute-start | bytes 1572872 | tf_op jit(solution)/shard_map/ppermute | solution.py:53
  26.1 5.3 %collective-permute-done.6.refs_0_ = bf16[8,128,256]{2,1,0:T(8,128)(2,1)S(1)} collective-permute-done((bf16[8,128,256]{2,1,0:T(8,128)(2,1)S(1)}, bf16[8,128,256]{2,1,0:T(8,128)(2,1)S(1)}, u32[]{:S(2)}, u32[]{:S(2)}) %collective-permute-start.6) | collective-permute-done | bytes 524320 | tf_op jit(solution)/shard_map/ppermute | solution.py:53
  32.4 1.8 %collective-permute-start.11 = (bf16[8,128,256]{2,1,0:T(8,128)(2,1)S(1)}, bf16[8,128,256]{2,1,0:T(8,128)(2,1)S(1)}, u32[]{:S(2)}, u32[]{:S(2)}) collective-permute-start(bf16[8,128,256]{2,1,0:T(8,128)(2,1)S(1)} %collective-permute-done.7.refs_1_), channel_id=1, source_target_pairs={{0,24},{1,7},{2,26},{3,1},{4,28},{5,3},{6,30},{7,5},{8,0},{9,15},{... | collective-permute-start | bytes 1572872 | tf_op jit(solution)/shard_map/ppermute | solution.py:53
  34.2 4.5 %collective-permute-start.13 = (bf16[16,128,256]{2,1,0:T(8,128)(2,1)S(1)}, bf16[16,128,256]{2,1,0:T(8,128)(2,1)S(1)}, u32[]{:S(2)}, u32[]{:S(2)}) collective-permute-start(bf16[16,128,256]{2,1,0:T(8,128)(2,1)S(1)} %join.6.rest_1_), channel_id=1, source_target_pairs={{0,1},{1,0},{2,3},{3,2},{4,5},{5,4},{6,7},{7,6},{8,9},{9,8},{10,11... | collective-permute-start | bytes 3145736 | tf_op jit(solution)/shard_map/ppermute | solution.py:65
  38.7 2.2 %collective-permute-start.12 = (bf16[16,128,256]{2,1,0:T(8,128)(2,1)S(1)}, bf16[16,128,256]{2,1,0:T(8,128)(2,1)S(1)}, u32[]{:S(2)}, u32[]{:S(2)}) collective-permute-start(bf16[16,128,256]{2,1,0:T(8,128)(2,1)S(1)} %join.5.x.rest_0_), channel_id=1, source_target_pairs={{0,1},{1,0},{2,3},{3,2},{4,5},{5,4},{6,7},{7,6},{8,9},{9,8},{10,11... | collective-permute-start | bytes 3145736 | tf_op jit(solution)/shard_map/ppermute | solution.py:65
  41.1 1.5 %collective-permute-done.10.rest_3_ = bf16[8,128,256]{2,1,0:T(8,128)(2,1)S(1)} collective-permute-done((bf16[8,128,256]{2,1,0:T(8,128)(2,1)S(1)}, bf16[8,128,256]{2,1,0:T(8,128)(2,1)S(1)}, u32[]{:S(2)}, u32[]{:S(2)}) %collective-permute-start.10) | collective-permute-done | bytes 524320 | tf_op jit(solution)/shard_map/ppermute | solution.py:53
  42.6 3.6 %collective-permute-start.15 = (bf16[8,128,256]{2,1,0:T(8,128)(2,1)S(1)}, bf16[8,128,256]{2,1,0:T(8,128)(2,1)S(1)}, u32[]{:S(2)}, u32[]{:S(2)}) collective-permute-start(bf16[8,128,256]{2,1,0:T(8,128)(2,1)S(1)} %collective-permute-done.10.rest_3_), channel_id=1, source_target_pairs={{0,1},{1,0},{2,3},{3,2},{4,5},{5,4},{6,7},{7,6},{8,9},{9,8},{10,11... | collective-permute-start | bytes 1572872 | tf_op jit(solution)/shard_map/ppermute | solution.py:65
  48.6 8.1 %layer.1 = (bf16[512,256]{1,0:T(8,128)(2,1)S(1)}, bf16[8,4096,128]{2,1,0:T(8,128)(2,1)S(1)}, f32[2,264,128]{2,1,0:T(8,128)S(1)}) custom-call(s32[1,16]{1,0:T(1,128)S(1)} %copy-done.4, s32[1]{0:T(128)S(6)} %copy.11.count_ref, bf16[512,8192]{1,0:T(8,128)(2,1)S(1)} %load.1.a_ref, bf16[256,256]{1,0:T(8,128)(2,1)S(1)} %copy-done, f32[1,256]{1,0:T(1,128)S(1)} %bitcast.14, ...), custom_call_target="tpu_custom_call" | custom-call | flops 4294967296 | bytes 8388608 | tf_op jit(solution)/shard_map/layer/pallas_call | solution.py:179
  57.7 2.1 %collective-permute-done.18.te = f32[264,128]{1,0:T(8,128)S(1)} collective-permute-done((f32[264,128]{1,0:T(8,128)S(1)}, f32[264,128]{1,0:T(8,128)S(1)}, u32[]{:S(2)}, u32[]{:S(2)}) %collective-permute-start.18) | collective-permute-done | bytes 135200 | tf_op jit(solution)/shard_map/ppermute | solution.py:65
  60.7 1.2 %collective-permute-start.20 = (bf16[2320,128]{1,0:T(8,128)(2,1)S(1)}, bf16[2320,128]{1,0:T(8,128)(2,1)S(1)}, u32[]{:S(2)}, u32[]{:S(2)}) collective-permute-start(bf16[2320,128]{1,0:T(8,128)(2,1)S(1)} %get-tuple-element.55), channel_id=1, source_target_pairs={{0,8},{1,3},{2,10},{3,5},{4,12},{5,7},{6,14},{7,1},{8,16},{9,11},{... | collective-permute-start | bytes 1781768 | tf_op jit(solution)/shard_map/ppermute | solution.py:53
  62.0 1.4 %collective-permute-start.21 = (bf16[2320,128]{1,0:T(8,128)(2,1)S(1)}, bf16[2320,128]{1,0:T(8,128)(2,1)S(1)}, u32[]{:S(2)}, u32[]{:S(2)}) collective-permute-start(bf16[2320,128]{1,0:T(8,128)(2,1)S(1)} %get-tuple-element.56), channel_id=1, source_target_pairs={{0,24},{1,7},{2,26},{3,1},{4,28},{5,3},{6,30},{7,5},{8,0},{9,15},{... | collective-permute-start | bytes 1781768 | tf_op jit(solution)/shard_map/ppermute | solution.py:53
  65.2 6.7 %collective-permute-done.22.far = bf16[272,128]{1,0:T(8,128)(2,1)S(1)} collective-permute-done((bf16[272,128]{1,0:T(8,128)(2,1)S(1)}, bf16[272,128]{1,0:T(8,128)(2,1)S(1)}, u32[]{:S(2)}, u32[]{:S(2)}) %collective-permute-start.22) | collective-permute-done | bytes 69664 | tf_op jit(solution)/shard_map/ppermute | solution.py:53
  72.6 1.7 %collective-permute-start.23 = (bf16[4096,128]{1,0:T(8,128)(2,1)S(1)}, bf16[4096,128]{1,0:T(8,128)(2,1)S(1)}, u32[]{:S(2)}, u32[]{:S(2)}) collective-permute-start(bf16[4096,128]{1,0:T(8,128)(2,1)S(1)} %get-tuple-element.62), channel_id=1, source_target_pairs={{0,1},{1,0},{2,3},{3,2},{4,5},{5,4},{6,7},{7,6},{8,9},{9,8},{10,11... | collective-permute-start | bytes 3145736 | tf_op jit(solution)/shard_map/ppermute | solution.py:65
  74.3 1.2 %collective-permute-start.24 = (bf16[4096,128]{1,0:T(8,128)(2,1)S(1)}, bf16[4096,128]{1,0:T(8,128)(2,1)S(1)}, u32[]{:S(2)}, u32[]{:S(2)}) collective-permute-start(bf16[4096,128]{1,0:T(8,128)(2,1)S(1)} %get-tuple-element.63), channel_id=1, source_target_pairs={{0,8},{1,3},{2,10},{3,5},{4,12},{5,7},{6,14},{7,1},{8,16},{9,11},{... | collective-permute-start | bytes 3145736 | tf_op jit(solution)/shard_map/ppermute | solution.py:53
  75.5 1.4 %collective-permute-start.25 = (bf16[4096,128]{1,0:T(8,128)(2,1)S(1)}, bf16[4096,128]{1,0:T(8,128)(2,1)S(1)}, u32[]{:S(2)}, u32[]{:S(2)}) collective-permute-start(bf16[4096,128]{1,0:T(8,128)(2,1)S(1)} %get-tuple-element.64), channel_id=1, source_target_pairs={{0,24},{1,7},{2,26},{3,1},{4,28},{5,3},{6,30},{7,5},{8,0},{9,15},{... | collective-permute-start | bytes 3145736 | tf_op jit(solution)/shard_map/ppermute | solution.py:53
  77.0 13.5 %all_to_all.5.got = f32[16,24,128]{2,1,0:T(8,128)S(1)} all-to-all(f32[16,24,128]{2,1,0:T(8,128)S(1)} %extra_pieces.1._pieces), channel_id=1, replica_groups={{1,9,17,25,33,41,49,57,65,73,81,89,97,105,113,121},{3,11,19,27,35,43,51..., dimensions={0} | all-to-all | bytes 393216 | tf_op jit(solution)/shard_map/all_to_all | solution.py:39
  91.6 2.6 %collective-permute-start.27 = (bf16[1056,128]{1,0:T(8,128)(2,1)S(1)}, bf16[1056,128]{1,0:T(8,128)(2,1)S(1)}, u32[]{:S(2)}, u32[]{:S(2)}) collective-permute-start(bf16[1056,128]{1,0:T(8,128)(2,1)S(1)} %get-tuple-element.69), channel_id=1, source_target_pairs={{0,4},{1,65},{2,6},{3,67},{4,0},{5,69},{6,2},{7,71},{8,12},{9,73},... | collective-permute-start | bytes 811016 | tf_op jit(solution)/shard_map/ppermute | solution.py:53
  94.2 3.9 %collective-permute-done.26.g1 = bf16[1056,128]{1,0:T(8,128)(2,1)S(1)} collective-permute-done((bf16[1056,128]{1,0:T(8,128)(2,1)S(1)}, bf16[1056,128]{1,0:T(8,128)(2,1)S(1)}, u32[]{:S(2)}, u32[]{:S(2)}) %collective-permute-start.26) | collective-permute-done | bytes 270368 | tf_op jit(solution)/shard_map/ppermute | solution.py:53
  98.1 3.2 %collective-permute-done.27.g2 = bf16[1056,128]{1,0:T(8,128)(2,1)S(1)} collective-permute-done((bf16[1056,128]{1,0:T(8,128)(2,1)S(1)}, bf16[1056,128]{1,0:T(8,128)(2,1)S(1)}, u32[]{:S(2)}, u32[]{:S(2)}) %collective-permute-start.27) | collective-permute-done | bytes 270368 | tf_op jit(solution)/shard_map/ppermute | solution.py:53
  102.7 2.5 %collective-permute-start.30 = (bf16[384,128]{1,0:T(8,128)(2,1)S(1)}, bf16[384,128]{1,0:T(8,128)(2,1)S(1)}, u32[]{:S(2)}, u32[]{:S(2)}) collective-permute-start(bf16[384,128]{1,0:T(8,128)(2,1)S(1)} %get-tuple-element.73), channel_id=1, source_target_pairs={{0,64},{1,17},{2,66},{3,19},{4,68},{5,21},{6,70},{7,23},{8,72},{9,... | collective-permute-start | bytes 294920 | tf_op jit(solution)/shard_map/ppermute | solution.py:53
  105.2 1.3 %collective-permute-done.29.h1 = bf16[384,128]{1,0:T(8,128)(2,1)S(1)} collective-permute-done((bf16[384,128]{1,0:T(8,128)(2,1)S(1)}, bf16[384,128]{1,0:T(8,128)(2,1)S(1)}, u32[]{:S(2)}, u32[]{:S(2)}) %collective-permute-start.29) | collective-permute-done | bytes 98336 | tf_op jit(solution)/shard_map/ppermute | solution.py:53
  106.5 1.8 %collective-permute-done.30.h2 = bf16[384,128]{1,0:T(8,128)(2,1)S(1)} collective-permute-done((bf16[384,128]{1,0:T(8,128)(2,1)S(1)}, bf16[384,128]{1,0:T(8,128)(2,1)S(1)}, u32[]{:S(2)}, u32[]{:S(2)}) %collective-permute-start.30) | collective-permute-done | bytes 98336 | tf_op jit(solution)/shard_map/ppermute | solution.py:53
  109.0 3.3 %collective-permute-start.32 = (f32[264,128]{1,0:T(8,128)S(1)}, f32[264,128]{1,0:T(8,128)S(1)}, u32[]{:S(2)}, u32[]{:S(2)}) collective-permute-start(f32[264,128]{1,0:T(8,128)S(1)} %extra_half.1.own), channel_id=1, source_target_pairs={{0,1},{1,0},{2,3},{3,2},{4,5},{5,4},{6,7},{7,6},{8,9},{9,8},{10,11... | collective-permute-start | bytes 405512 | tf_op jit(solution)/shard_map/ppermute | solution.py:65
  (64 shorter events, 14.7 us)
Async XLA Ops:
  0.6 9.3 %collective-permute-start.2 = (bf16[1,128,256]{2,1,0:T(8,128)(2,1)}, bf16[1,128,256]{2,1,0:T(8,128)(2,1)S(1)}, u32[]{:S(2)}, u32[]{:S(2)}) collective-permute-start(bf16[1,128,256]{2,1,0:T(8,128)(2,1)} %bitcast.10), channel_id=1, source_target_pairs={{0,32},{1,9},{2,34},{3,11},{4,36},{5,13},{6,38},{7,15},{8,40},{9,1... | collective-permute-start | bytes 196616 | tf_op jit(solution)/shard_map/ppermute | solution.py:53
  2.7 7.2 %collective-permute-start.1 = (bf16[1,128,256]{2,1,0:T(8,128)(2,1)}, bf16[1,128,256]{2,1,0:T(8,128)(2,1)S(1)}, u32[]{:S(2)}, u32[]{:S(2)}) collective-permute-start(bf16[1,128,256]{2,1,0:T(8,128)(2,1)} %bitcast.11), channel_id=1, source_target_pairs={{0,64},{1,17},{2,66},{3,19},{4,68},{5,21},{6,70},{7,23},{8,72},{9,... | collective-permute-start | bytes 196616 | tf_op jit(solution)/shard_map/ppermute | solution.py:53
  5.2 4.8 %collective-permute-start = (bf16[1,128,256]{2,1,0:T(8,128)(2,1)}, bf16[1,128,256]{2,1,0:T(8,128)(2,1)S(1)}, u32[]{:S(2)}, u32[]{:S(2)}) collective-permute-start(bf16[1,128,256]{2,1,0:T(8,128)(2,1)} %bitcast.12), channel_id=1, source_target_pairs={{0,96},{1,25},{2,98},{3,27},{4,100},{5,29},{6,102},{7,31},{8,104},... | collective-permute-start | bytes 196616 | tf_op jit(solution)/shard_map/ppermute | solution.py:53
  10.0 6.6 %collective-permute-start.5 = (bf16[4,128,256]{2,1,0:T(8,128)(2,1)S(1)}, bf16[4,128,256]{2,1,0:T(8,128)(2,1)S(1)}, u32[]{:S(2)}, u32[]{:S(2)}) collective-permute-start(bf16[4,128,256]{2,1,0:T(8,128)(2,1)S(1)} %join.4.refs_0_), channel_id=1, source_target_pairs={{0,2},{1,33},{2,4},{3,35},{4,6},{5,37},{6,0},{7,39},{8,10},{9,41},... | collective-permute-start | bytes 786440 | tf_op jit(solution)/shard_map/ppermute | solution.py:53
  11.4 9.2 %collective-permute-start.4 = (bf16[4,128,256]{2,1,0:T(8,128)(2,1)S(1)}, bf16[4,128,256]{2,1,0:T(8,128)(2,1)S(1)}, u32[]{:S(2)}, u32[]{:S(2)}) collective-permute-start(bf16[4,128,256]{2,1,0:T(8,128)(2,1)S(1)} %join.4.refs_0_), channel_id=1, source_target_pairs={{0,4},{1,65},{2,6},{3,67},{4,0},{5,69},{6,2},{7,71},{8,12},{9,73},... | collective-permute-start | bytes 786440 | tf_op jit(solution)/shard_map/ppermute | solution.py:53
  14.0 6.6 %collective-permute-start.3 = (bf16[4,128,256]{2,1,0:T(8,128)(2,1)S(1)}, bf16[4,128,256]{2,1,0:T(8,128)(2,1)S(1)}, u32[]{:S(2)}, u32[]{:S(2)}) collective-permute-start(bf16[4,128,256]{2,1,0:T(8,128)(2,1)S(1)} %join.4.refs_0_), channel_id=1, source_target_pairs={{0,6},{1,97},{2,0},{3,99},{4,2},{5,101},{6,4},{7,103},{8,14},{9,10... | collective-permute-start | bytes 786440 | tf_op jit(solution)/shard_map/ppermute | solution.py:53
  20.7 10.7 %collective-permute-start.6 = (bf16[8,128,256]{2,1,0:T(8,128)(2,1)S(1)}, bf16[8,128,256]{2,1,0:T(8,128)(2,1)S(1)}, u32[]{:S(2)}, u32[]{:S(2)}) collective-permute-start(bf16[8,128,256]{2,1,0:T(8,128)(2,1)S(1)} %get-tuple-element.43), channel_id=1, source_target_pairs={{0,8},{1,3},{2,10},{3,5},{4,12},{5,7},{6,14},{7,1},{8,16},{9,11},{... | collective-permute-start | bytes 1572872 | tf_op jit(solution)/shard_map/ppermute | solution.py:53
  22.4 9.0 %collective-permute-start.7 = (bf16[8,128,256]{2,1,0:T(8,128)(2,1)S(1)}, bf16[8,128,256]{2,1,0:T(8,128)(2,1)S(1)}, u32[]{:S(2)}, u32[]{:S(2)}) collective-permute-start(bf16[8,128,256]{2,1,0:T(8,128)(2,1)S(1)} %get-tuple-element.44), channel_id=1, source_target_pairs={{0,24},{1,7},{2,26},{3,1},{4,28},{5,3},{6,30},{7,5},{8,0},{9,15},{... | collective-permute-start | bytes 1572872 | tf_op jit(solution)/shard_map/ppermute | solution.py:53
  24.6 14.1 %collective-permute-start.9 = (bf16[8,128,256]{2,1,0:T(8,128)(2,1)S(1)}, bf16[8,128,256]{2,1,0:T(8,128)(2,1)S(1)}, u32[]{:S(2)}, u32[]{:S(2)}) collective-permute-start(bf16[8,128,256]{2,1,0:T(8,128)(2,1)S(1)} %get-tuple-element.43), channel_id=1, source_target_pairs={{0,24},{1,7},{2,26},{3,1},{4,28},{5,3},{6,30},{7,5},{8,0},{9,15},{... | collective-permute-start | bytes 1572872 | tf_op jit(solution)/shard_map/ppermute | solution.py:53
  26.0 14.9 %collective-permute-start.8 = (bf16[8,128,256]{2,1,0:T(8,128)(2,1)S(1)}, bf16[8,128,256]{2,1,0:T(8,128)(2,1)S(1)}, u32[]{:S(2)}, u32[]{:S(2)}) collective-permute-start(bf16[8,128,256]{2,1,0:T(8,128)(2,1)S(1)} %get-tuple-element.44), channel_id=1, source_target_pairs={{0,8},{1,3},{2,10},{3,5},{4,12},{5,7},{6,14},{7,1},{8,16},{9,11},{... | collective-permute-start | bytes 1572872 | tf_op jit(solution)/shard_map/ppermute | solution.py:53
  31.4 11.2 %collective-permute-start.10 = (bf16[8,128,256]{2,1,0:T(8,128)(2,1)S(1)}, bf16[8,128,256]{2,1,0:T(8,128)(2,1)S(1)}, u32[]{:S(2)}, u32[]{:S(2)}) collective-permute-start(bf16[8,128,256]{2,1,0:T(8,128)(2,1)S(1)} %collective-permute-done.6.refs_0_), channel_id=1, source_target_pairs={{0,8},{1,3},{2,10},{3,5},{4,12},{5,7},{6,14},{7,1},{8,16},{9,11},{... | collective-permute-start | bytes 1572872 | tf_op jit(solution)/shard_map/ppermute | solution.py:53
  32.4 13.9 %collective-permute-start.11 = (bf16[8,128,256]{2,1,0:T(8,128)(2,1)S(1)}, bf16[8,128,256]{2,1,0:T(8,128)(2,1)S(1)}, u32[]{:S(2)}, u32[]{:S(2)}) collective-permute-start(bf16[8,128,256]{2,1,0:T(8,128)(2,1)S(1)} %collective-permute-done.7.refs_1_), channel_id=1, source_target_pairs={{0,24},{1,7},{2,26},{3,1},{4,28},{5,3},{6,30},{7,5},{8,0},{9,15},{... | collective-permute-start | bytes 1572872 | tf_op jit(solution)/shard_map/ppermute | solution.py:53
  34.2 14.3 %collective-permute-start.13 = (bf16[16,128,256]{2,1,0:T(8,128)(2,1)S(1)}, bf16[16,128,256]{2,1,0:T(8,128)(2,1)S(1)}, u32[]{:S(2)}, u32[]{:S(2)}) collective-permute-start(bf16[16,128,256]{2,1,0:T(8,128)(2,1)S(1)} %join.6.rest_1_), channel_id=1, source_target_pairs={{0,1},{1,0},{2,3},{3,2},{4,5},{5,4},{6,7},{7,6},{8,9},{9,8},{10,11... | collective-permute-start | bytes 3145736 | tf_op jit(solution)/shard_map/ppermute | solution.py:65
  38.7 9.9 %collective-permute-start.12 = (bf16[16,128,256]{2,1,0:T(8,128)(2,1)S(1)}, bf16[16,128,256]{2,1,0:T(8,128)(2,1)S(1)}, u32[]{:S(2)}, u32[]{:S(2)}) collective-permute-start(bf16[16,128,256]{2,1,0:T(8,128)(2,1)S(1)} %join.5.x.rest_0_), channel_id=1, source_target_pairs={{0,1},{1,0},{2,3},{3,2},{4,5},{5,4},{6,7},{7,6},{8,9},{9,8},{10,11... | collective-permute-start | bytes 3145736 | tf_op jit(solution)/shard_map/ppermute | solution.py:65
  41.0 7.6 %collective-permute-start.14 = (bf16[16,128,256]{2,1,0:T(8,128)(2,1)S(1)}, bf16[16,128,256]{2,1,0:T(8,128)(2,1)S(1)}, u32[]{:S(2)}, u32[]{:S(2)}) collective-permute-start(bf16[16,128,256]{2,1,0:T(8,128)(2,1)S(1)} %join.7.rest_2_), channel_id=1, source_target_pairs={{0,1},{1,0},{2,3},{3,2},{4,5},{5,4},{6,7},{7,6},{8,9},{9,8},{10,11... | collective-permute-start | bytes 3145736 | tf_op jit(solution)/shard_map/ppermute | solution.py:65
  42.6 5.2 %collective-permute-start.15 = (bf16[8,128,256]{2,1,0:T(8,128)(2,1)S(1)}, bf16[8,128,256]{2,1,0:T(8,128)(2,1)S(1)}, u32[]{:S(2)}, u32[]{:S(2)}) collective-permute-start(bf16[8,128,256]{2,1,0:T(8,128)(2,1)S(1)} %collective-permute-done.10.rest_3_), channel_id=1, source_target_pairs={{0,1},{1,0},{2,3},{3,2},{4,5},{5,4},{6,7},{7,6},{8,9},{9,8},{10,11... | collective-permute-start | bytes 1572872 | tf_op jit(solution)/shard_map/ppermute | solution.py:65
  56.9 2.9 %collective-permute-start.17 = (bf16[4096,128]{1,0:T(8,128)(2,1)S(1)}, bf16[4096,128]{1,0:T(8,128)(2,1)S(1)}, u32[]{:S(2)}, u32[]{:S(2)}) collective-permute-start(bf16[4096,128]{1,0:T(8,128)(2,1)S(1)} %get-tuple-element.79), channel_id=1, source_target_pairs={{0,1},{1,0},{2,3},{3,2},{4,5},{5,4},{6,7},{7,6},{8,9},{9,8},{10,11... | collective-permute-start | bytes 3145736 | tf_op jit(solution)/shard_map/ppermute | solution.py:65
  57.4 2.5 %collective-permute-start.18 = (f32[264,128]{1,0:T(8,128)S(1)}, f32[264,128]{1,0:T(8,128)S(1)}, u32[]{:S(2)}, u32[]{:S(2)}) collective-permute-start(f32[264,128]{1,0:T(8,128)S(1)} %slice_bitcast_fusion.2), channel_id=1, source_target_pairs={{0,1},{1,0},{2,3},{3,2},{4,5},{5,4},{6,7},{7,6},{8,9},{9,8},{10,11... | collective-permute-start | bytes 405512 | tf_op jit(solution)/shard_map/ppermute | solution.py:65
  60.1 11.8 %collective-permute-start.19 = (bf16[2,4096,128]{2,1,0:T(8,128)(2,1)S(1)}, bf16[2,4096,128]{2,1,0:T(8,128)(2,1)S(1)}, u32[]{:S(2)}, u32[]{:S(2)}) collective-permute-start(bf16[2,4096,128]{2,1,0:T(8,128)(2,1)S(1)} %slice.14), channel_id=1, source_target_pairs={{0,1},{1,0},{2,3},{3,2},{4,5},{5,4},{6,7},{7,6},{8,9},{9,8},{10,11... | collective-permute-start | bytes 6291464 | tf_op jit(solution)/shard_map/ppermute | solution.py:65
  60.7 11.1 %collective-permute-start.20 = (bf16[2320,128]{1,0:T(8,128)(2,1)S(1)}, bf16[2320,128]{1,0:T(8,128)(2,1)S(1)}, u32[]{:S(2)}, u32[]{:S(2)}) collective-permute-start(bf16[2320,128]{1,0:T(8,128)(2,1)S(1)} %get-tuple-element.55), channel_id=1, source_target_pairs={{0,8},{1,3},{2,10},{3,5},{4,12},{5,7},{6,14},{7,1},{8,16},{9,11},{... | collective-permute-start | bytes 1781768 | tf_op jit(solution)/shard_map/ppermute | solution.py:53
  62.0 9.9 %collective-permute-start.21 = (bf16[2320,128]{1,0:T(8,128)(2,1)S(1)}, bf16[2320,128]{1,0:T(8,128)(2,1)S(1)}, u32[]{:S(2)}, u32[]{:S(2)}) collective-permute-start(bf16[2320,128]{1,0:T(8,128)(2,1)S(1)} %get-tuple-element.56), channel_id=1, source_target_pairs={{0,24},{1,7},{2,26},{3,1},{4,28},{5,3},{6,30},{7,5},{8,0},{9,15},{... | collective-permute-start | bytes 1781768 | tf_op jit(solution)/shard_map/ppermute | solution.py:53
  63.4 8.4 %collective-permute-start.22 = (bf16[272,128]{1,0:T(8,128)(2,1)S(1)}, bf16[272,128]{1,0:T(8,128)(2,1)S(1)}, u32[]{:S(2)}, u32[]{:S(2)}) collective-permute-start(bf16[272,128]{1,0:T(8,128)(2,1)S(1)} %get-tuple-element.57), channel_id=1, source_target_pairs={{0,16},{1,5},{2,18},{3,7},{4,20},{5,1},{6,22},{7,3},{8,24},{9,13},... | collective-permute-start | bytes 208904 | tf_op jit(solution)/shard_map/ppermute | solution.py:53
  72.6 17.9 %collective-permute-start.23 = (bf16[4096,128]{1,0:T(8,128)(2,1)S(1)}, bf16[4096,128]{1,0:T(8,128)(2,1)S(1)}, u32[]{:S(2)}, u32[]{:S(2)}) collective-permute-start(bf16[4096,128]{1,0:T(8,128)(2,1)S(1)} %get-tuple-element.62), channel_id=1, source_target_pairs={{0,1},{1,0},{2,3},{3,2},{4,5},{5,4},{6,7},{7,6},{8,9},{9,8},{10,11... | collective-permute-start | bytes 3145736 | tf_op jit(solution)/shard_map/ppermute | solution.py:65
  74.3 16.2 %collective-permute-start.24 = (bf16[4096,128]{1,0:T(8,128)(2,1)S(1)}, bf16[4096,128]{1,0:T(8,128)(2,1)S(1)}, u32[]{:S(2)}, u32[]{:S(2)}) collective-permute-start(bf16[4096,128]{1,0:T(8,128)(2,1)S(1)} %get-tuple-element.63), channel_id=1, source_target_pairs={{0,8},{1,3},{2,10},{3,5},{4,12},{5,7},{6,14},{7,1},{8,16},{9,11},{... | collective-permute-start | bytes 3145736 | tf_op jit(solution)/shard_map/ppermute | solution.py:53
  75.5 15.0 %collective-permute-start.25 = (bf16[4096,128]{1,0:T(8,128)(2,1)S(1)}, bf16[4096,128]{1,0:T(8,128)(2,1)S(1)}, u32[]{:S(2)}, u32[]{:S(2)}) collective-permute-start(bf16[4096,128]{1,0:T(8,128)(2,1)S(1)} %get-tuple-element.64), channel_id=1, source_target_pairs={{0,24},{1,7},{2,26},{3,1},{4,28},{5,3},{6,30},{7,5},{8,0},{9,15},{... | collective-permute-start | bytes 3145736 | tf_op jit(solution)/shard_map/ppermute | solution.py:53
  91.2 6.9 %collective-permute-start.26 = (bf16[1056,128]{1,0:T(8,128)(2,1)S(1)}, bf16[1056,128]{1,0:T(8,128)(2,1)S(1)}, u32[]{:S(2)}, u32[]{:S(2)}) collective-permute-start(bf16[1056,128]{1,0:T(8,128)(2,1)S(1)} %get-tuple-element.68), channel_id=1, source_target_pairs={{0,2},{1,33},{2,4},{3,35},{4,6},{5,37},{6,0},{7,39},{8,10},{9,41},... | collective-permute-start | bytes 811016 | tf_op jit(solution)/shard_map/ppermute | solution.py:53
  91.6 9.6 %collective-permute-start.27 = (bf16[1056,128]{1,0:T(8,128)(2,1)S(1)}, bf16[1056,128]{1,0:T(8,128)(2,1)S(1)}, u32[]{:S(2)}, u32[]{:S(2)}) collective-permute-start(bf16[1056,128]{1,0:T(8,128)(2,1)S(1)} %get-tuple-element.69), channel_id=1, source_target_pairs={{0,4},{1,65},{2,6},{3,67},{4,0},{5,69},{6,2},{7,71},{8,12},{9,73},... | collective-permute-start | bytes 811016 | tf_op jit(solution)/shard_map/ppermute | solution.py:53
  94.2 7.4 %collective-permute-start.28 = (bf16[1056,128]{1,0:T(8,128)(2,1)S(1)}, bf16[1056,128]{1,0:T(8,128)(2,1)S(1)}, u32[]{:S(2)}, u32[]{:S(2)}) collective-permute-start(bf16[1056,128]{1,0:T(8,128)(2,1)S(1)} %get-tuple-element.70), channel_id=1, source_target_pairs={{0,6},{1,97},{2,0},{3,99},{4,2},{5,101},{6,4},{7,103},{8,14},{9,10... | collective-permute-start | bytes 811016 | tf_op jit(solution)/shard_map/ppermute | solution.py:53
  101.7 4.7 %collective-permute-start.29 = (bf16[384,128]{1,0:T(8,128)(2,1)S(1)}, bf16[384,128]{1,0:T(8,128)(2,1)S(1)}, u32[]{:S(2)}, u32[]{:S(2)}) collective-permute-start(bf16[384,128]{1,0:T(8,128)(2,1)S(1)} %get-tuple-element.72), channel_id=1, source_target_pairs={{0,32},{1,9},{2,34},{3,11},{4,36},{5,13},{6,38},{7,15},{8,40},{9,1... | collective-permute-start | bytes 294920 | tf_op jit(solution)/shard_map/ppermute | solution.py:53
  102.7 5.5 %collective-permute-start.30 = (bf16[384,128]{1,0:T(8,128)(2,1)S(1)}, bf16[384,128]{1,0:T(8,128)(2,1)S(1)}, u32[]{:S(2)}, u32[]{:S(2)}) collective-permute-start(bf16[384,128]{1,0:T(8,128)(2,1)S(1)} %get-tuple-element.73), channel_id=1, source_target_pairs={{0,64},{1,17},{2,66},{3,19},{4,68},{5,21},{6,70},{7,23},{8,72},{9,... | collective-permute-start | bytes 294920 | tf_op jit(solution)/shard_map/ppermute | solution.py:53
  105.2 3.8 %collective-permute-start.31 = (bf16[384,128]{1,0:T(8,128)(2,1)S(1)}, bf16[384,128]{1,0:T(8,128)(2,1)S(1)}, u32[]{:S(2)}, u32[]{:S(2)}) collective-permute-start(bf16[384,128]{1,0:T(8,128)(2,1)S(1)} %get-tuple-element.74), channel_id=1, source_target_pairs={{0,96},{1,25},{2,98},{3,27},{4,100},{5,29},{6,102},{7,31},{8,104},... | collective-permute-start | bytes 294920 | tf_op jit(solution)/shard_map/ppermute | solution.py:53
  109.0 4.3 %collective-permute-start.32 = (f32[264,128]{1,0:T(8,128)S(1)}, f32[264,128]{1,0:T(8,128)S(1)}, u32[]{:S(2)}, u32[]{:S(2)}) collective-permute-start(f32[264,128]{1,0:T(8,128)S(1)} %extra_half.1.own), channel_id=1, source_target_pairs={{0,1},{1,0},{2,3},{3,2},{4,5},{5,4},{6,7},{7,6},{8,9},{9,8},{10,11... | collective-permute-start | bytes 405512 | tf_op jit(solution)/shard_map/ppermute | solution.py:65
  (6 other events, 174.8 us)

commit v4 on v3

--- a/solution.py
+++ b/solution.py
@@ -18,6 +18,7 @@
 F32 = jnp.float32
 GROUP = 8
 STARTS = ((0,), (16, 56), (24, 48), (32,), (40,))
+AROUND = (2, 3, 1)
 DB = 16
 
 
@@ -54,7 +55,7 @@
 
 
 def around(x, axes):
-    return [hop(x, axes, k) for k in (3, 2, 1)]
+    return [hop(x, axes, k) for k in AROUND]
 
 
 def swap(x):
@@ -94,7 +95,7 @@
 
 
 def kernel(
-    col_ref, count_ref, a_ref, w_ref, b_ref, cot_ref, *rest,
+    col_ref, count_ref, a_ref, w_ref, b_ref, cot_ref, _zeros, *rest,
 ):
     blocks, (act_ref, r_ref, e_ref, g_buf, x_buf, acc, g_t) = rest[:10], rest[10:]
     count = count_ref[0]
@@ -108,8 +109,11 @@
     def source(t, zlo, cc):
         at = there(t, zlo)
         away = [(at[i] - me[i]) & 3 for i in range(3)]
-        first, second = STEPS[cc]
-        return (-away[LINE[cc]] & 3) * 16 + away[second] * 4 + away[first]
+        first, second = [
+            sum(jnp.where(away[i] == 4 - k, place + 1, 0) for place, k in enumerate(AROUND))
+            for i in STEPS[cc]
+        ]
+        return (-away[LINE[cc]] & 3) * 16 + second * 4 + first
 
     def target(t, zlo, cc):
         at = there(t, zlo)
@@ -122,7 +126,6 @@
             length = ref.shape[0] // len(starts)
             for i, start in enumerate(starts):
                 g_buf[side, start : start + length] = ref[i * length : i * length + length]
-    r_ref[...] = jnp.zeros_like(r_ref)
     acc[...] = jnp.zeros_like(acc)
 
     def forward(g, carry):
@@ -174,7 +177,11 @@
     lax.fori_loop(0, 16 // GROUP, backward, 0)
 
 
-def local(cols, count, values, weight, bias, cotangent, blocks):
+def clear(_after, zeros):
+    zeros[...] = jnp.zeros_like(zeros)
+
+
+def local(cols, count, values, weight, bias, cotangent, zeros, blocks):
     vmem = pl.BlockSpec(memory_space=pltpu.VMEM)
     return pl.pallas_call(
         kernel,
@@ -183,8 +190,9 @@
             pltpu.VMEM((8, 4096, 128), BF16),
             pltpu.VMEM((2, 264, 128), F32),
         ),
-        in_specs=[pl.BlockSpec(memory_space=pltpu.SMEM)] * 2 + [vmem] * 14,
+        in_specs=[pl.BlockSpec(memory_space=pltpu.SMEM)] * 2 + [vmem] * 15,
         out_specs=(vmem,) * 3,
+        input_output_aliases={6: 1},
         scratch_shapes=[
             pltpu.VMEM((2, 64, 128, 256), BF16),
             pltpu.VMEM((GROUP * 512, 256), BF16),
@@ -196,7 +204,7 @@
             flops=2 * 2 * 16 * 512 * 512 * 256, bytes_accessed=8 * 2**20, transcendentals=512 * 256
         ),
         name="layer",
-    )(cols, count, values, weight, bias, cotangent, *blocks)
+    )(cols, count, values, weight, bias, cotangent, zeros, *blocks)
 
 
 def in_vmem(name, body, outs, *ins, last=False):
@@ -298,7 +306,7 @@
             message[1024:] = piece[...]
 
 
-def plane_sum(own, piece, g1, g2, g3, rest, pieces, n1, n2, n3):
+def plane_sum(own, piece, g2, g1, g3, rest, pieces, n1, n2, n3):
     for i, ref in enumerate((piece, g1, g2, g3)):
         pieces[i * 32 : i * 32 + 32] = ref[-32:]
     for k, message in enumerate((None, n1, n2, n3)):
@@ -311,7 +319,7 @@
             message[256:] = pieces[...]
 
 
-def extra_half(pieces, h1, h2, h3, o):
+def extra_half(pieces, h2, h1, h3, o):
     index = lax.axis_index(AXIS)
     at = (index >> 5, (index >> 3) & 3, (index >> 1) & 3)
 
@@ -338,7 +346,7 @@
     db[:, :128], db[:, 128:] = first[256:257], second[256:257]
 
 
-def finish(rest, h1, h2, h3, w, o):
+def finish(rest, h2, h1, h3, w, o):
     total = rest[...] + widened(h1[:256], h2[:256], h3[:256])
     o[...] = dot(total.T.astype(BF16), w[...], ((1,), (1,)))
 
@@ -367,7 +375,9 @@
     first, second = zip(*STEPS)
     held = join(held, *around(held, first))
     held, values = lax.optimization_barrier((held, values))
+    zeros = in_vmem("clear", clear, [like(8, 4096, 128)], held)[0]
     held = join(held, *around(held, second))
+    held, zeros = lax.optimization_barrier((held, zeros))
     h1, h2 = in_vmem("halves", halves, [like(8, 128, 256)] * 2, held)
     a1, b2, a2, b1 = hop(h1, LINE, 1), hop(h2, LINE, 3), hop(h2, LINE, 1), hop(h1, LINE, 3)
     a1, b2, other = lax.optimization_barrier((a1, b2, held))
@@ -375,7 +385,7 @@
     mine = [held, join(a1, b2), join(a2, b1), c1, c2]
     theirs = [swap(other)] + [swap(g) for g in mine[1:]]
     activation, r_all, e_all = local(
-        tile_col, tile_count, values, weight, bias[None], cotangent, mine + theirs
+        tile_col, tile_count, values, weight, bias[None], cotangent, zeros, mine + theirs
     )
 
     some, whole = like(2048 + 272, 128), like(4096, 128)
@@ -406,12 +416,12 @@
         "line_sum", line_sum, [like(1024, 128, dtype=F32), like(32, 128)] + [like(1056, 128)] * 3,
         r_all, swap(own), p1, p3, pieces,
     )
-    got = [hop(m, second, k) for k, m in zip((1, 2, 3), sent)]
+    got = [hop(sent[k - 1], second, k) for k in (2, 1, 3)]
     rest, pieces, *sent = in_vmem(
         "plane_sum", plane_sum, [like(256, 128, dtype=F32), like(128, 128)] + [like(384, 128)] * 3,
         own, piece, *got,
     )
-    got = [hop(m, first, k) for k, m in zip((1, 2, 3), sent)]
+    got = [hop(sent[k - 1], first, k) for k in (2, 1, 3)]
     own = in_vmem("extra_half", extra_half, [like(264, 128, dtype=F32)], pieces, *got)[0]
     other = swap(own)
     grad_features = in_vmem(

time: 114 us -> 112 us (0.982)
  waiting for transfers between devices: 33.8 us -> 31.3 us
    ppermute x23, waiting for transfers between devices: 30.2 us -> 27.8 us  [hop(): return lax.ppermute(x, AXIS, pairs(move))]
    pallas_call x12 -> x13, Pallas kernels: 2.95 us -> 3.98 us  [in_vmem(): pl.pallas_call(body, out_shape=tuple((o if last else pltpu.VMEM(o.shape,...]
  transfers between devices with their start and end apart: 33 -> 33, of which waited for: 15 -> 16; matrix products, arithmetic and copies ran while one was open for 0% -> 0% of each run, Pallas kernels for 5% -> 6%
where the time goes in v4:
time: 112 us
  starting transfers between devices  49.4 us (44%)
  waiting for transfers between devices  31.3 us (28%)
  Pallas kernels  16.1 us (14%)
  blocking collectives  13.1 us (12%)
  between operations  1.53 us (1%)
    ppermute x23, starting transfers between devices, hop(): return lax.ppermute(x, AXIS, pairs(move))  31.7 us
    ppermute x23, waiting for transfers between devices, hop(): return lax.ppermute(x, AXIS, pairs(move))  27.8 us
    ppermute x10, starting transfers between devices, swap(): return lax.ppermute(x, AXIS, pairs(move))  17.7 us
    all_to_all x1, blocking collectives, exchange(): lax.all_to_all(x, AXIS, split_axis=0, concat_axis=0, tiled=True, axis_ind...  13.1 us
    pallas_call x1, Pallas kernels, local(): pl.pallas_call(kernel, out_shape=(pltpu.VMEM((512, 256), BF16), pltpu.VME...  7.14 us
    pallas_call x13, Pallas kernels, in_vmem(): pl.pallas_call(body, out_shape=tuple((o if last else pltpu.VMEM(o.shape,...  3.98 us
    ppermute x10, waiting for transfers between devices, swap(): return lax.ppermute(x, AXIS, pairs(move))  3.58 us
    pallas_call x1, Pallas kernels, load(): pl.pallas_call(load_kernel, out_shape=pltpu.VMEM((512, 8192), BF16), in_s...  3.54 us
  transfers between devices with their start and end apart: 33, of which 16 were waited for; matrix products, arithmetic and copies ran while one was open for 0% of the time, Pallas kernels for 6%

profile of v4, /device:TPU:1, one launch (start us, length us, event | category | flops | bytes accessed | tf_op | source)
XLA Modules:
  0.0 111.8 jit_solution(10386928566839299608)
XLA Ops:
  0.6 2.1 %collective-permute-start.2 = (bf16[1,128,256]{2,1,0:T(8,128)(2,1)}, bf16[1,128,256]{2,1,0:T(8,128)(2,1)S(1)}, u32[]{:S(2)}, u32[]{:S(2)}) collective-permute-start(bf16[1,128,256]{2,1,0:T(8,128)(2,1)} %bitcast.10), channel_id=1, source_target_pairs={{0,32},{1,9},{2,34},{3,11},{4,36},{5,13},{6,38},{7,15},{8,40},{9,1... | collective-permute-start | bytes 196616 | tf_op jit(solution)/shard_map/ppermute | solution.py:54
  2.7 1.3 %collective-permute-start.1 = (bf16[1,128,256]{2,1,0:T(8,128)(2,1)}, bf16[1,128,256]{2,1,0:T(8,128)(2,1)S(1)}, u32[]{:S(2)}, u32[]{:S(2)}) collective-permute-start(bf16[1,128,256]{2,1,0:T(8,128)(2,1)} %bitcast.11), channel_id=1, source_target_pairs={{0,96},{1,25},{2,98},{3,27},{4,100},{5,29},{6,102},{7,31},{8,104},... | collective-permute-start | bytes 196616 | tf_op jit(solution)/shard_map/ppermute | solution.py:54
  4.1 1.6 %collective-permute-start = (bf16[1,128,256]{2,1,0:T(8,128)(2,1)}, bf16[1,128,256]{2,1,0:T(8,128)(2,1)S(1)}, u32[]{:S(2)}, u32[]{:S(2)}) collective-permute-start(bf16[1,128,256]{2,1,0:T(8,128)(2,1)} %bitcast.12), channel_id=1, source_target_pairs={{0,64},{1,17},{2,66},{3,19},{4,68},{5,21},{6,70},{7,23},{8,72},{9,... | collective-permute-start | bytes 196616 | tf_op jit(solution)/shard_map/ppermute | solution.py:54
  5.7 3.5 %load.1.a_ref = bf16[512,8192]{1,0:T(8,128)(2,1)S(1)} custom-call(bf16[16,512,512]{2,1,0:T(8,128)(2,1)} %bitcast.15), custom_call_target="tpu_custom_call" | custom-call | bytes 16777216 | tf_op jit(solution)/shard_map/load/pallas_call | solution.py:85
  9.4 1.4 %collective-permute-start.5 = (bf16[4,128,256]{2,1,0:T(8,128)(2,1)S(1)}, bf16[4,128,256]{2,1,0:T(8,128)(2,1)S(1)}, u32[]{:S(2)}, u32[]{:S(2)}) collective-permute-start(bf16[4,128,256]{2,1,0:T(8,128)(2,1)S(1)} %join.4.refs_0_._after), channel_id=1, source_target_pairs={{0,2},{1,33},{2,4},{3,35},{4,6},{5,37},{6,0},{7,39},{8,10},{9,41},... | collective-permute-start | bytes 786440 | tf_op jit(solution)/shard_map/ppermute | solution.py:54
  10.8 1.5 %collective-permute-start.4 = (bf16[4,128,256]{2,1,0:T(8,128)(2,1)S(1)}, bf16[4,128,256]{2,1,0:T(8,128)(2,1)S(1)}, u32[]{:S(2)}, u32[]{:S(2)}) collective-permute-start(bf16[4,128,256]{2,1,0:T(8,128)(2,1)S(1)} %join.4.refs_0_._after), channel_id=1, source_target_pairs={{0,6},{1,97},{2,0},{3,99},{4,2},{5,101},{6,4},{7,103},{8,14},{9,10... | collective-permute-start | bytes 786440 | tf_op jit(solution)/shard_map/ppermute | solution.py:54
  12.3 1.6 %collective-permute-start.3 = (bf16[4,128,256]{2,1,0:T(8,128)(2,1)S(1)}, bf16[4,128,256]{2,1,0:T(8,128)(2,1)S(1)}, u32[]{:S(2)}, u32[]{:S(2)}) collective-permute-start(bf16[4,128,256]{2,1,0:T(8,128)(2,1)S(1)} %join.4.refs_0_._after), channel_id=1, source_target_pairs={{0,4},{1,65},{2,6},{3,67},{4,0},{5,69},{6,2},{7,71},{8,12},{9,73},... | collective-permute-start | bytes 786440 | tf_op jit(solution)/shard_map/ppermute | solution.py:54
  16.0 2.4 %collective-permute-done.4.refs_2_ = bf16[4,128,256]{2,1,0:T(8,128)(2,1)S(1)} collective-permute-done((bf16[4,128,256]{2,1,0:T(8,128)(2,1)S(1)}, bf16[4,128,256]{2,1,0:T(8,128)(2,1)S(1)}, u32[]{:S(2)}, u32[]{:S(2)}) %collective-permute-start.4) | collective-permute-done | bytes 262176 | tf_op jit(solution)/shard_map/ppermute | solution.py:54
  18.4 1.5 %collective-permute-done.3.refs_1_ = bf16[4,128,256]{2,1,0:T(8,128)(2,1)S(1)} collective-permute-done((bf16[4,128,256]{2,1,0:T(8,128)(2,1)S(1)}, bf16[4,128,256]{2,1,0:T(8,128)(2,1)S(1)}, u32[]{:S(2)}, u32[]{:S(2)}) %collective-permute-start.3) | collective-permute-done | bytes 262176 | tf_op jit(solution)/shard_map/ppermute | solution.py:54
  20.1 1.7 %collective-permute-start.6 = (bf16[8,128,256]{2,1,0:T(8,128)(2,1)S(1)}, bf16[8,128,256]{2,1,0:T(8,128)(2,1)S(1)}, u32[]{:S(2)}, u32[]{:S(2)}) collective-permute-start(bf16[8,128,256]{2,1,0:T(8,128)(2,1)S(1)} %get-tuple-element.47), channel_id=1, source_target_pairs={{0,8},{1,3},{2,10},{3,5},{4,12},{5,7},{6,14},{7,1},{8,16},{9,11},{... | collective-permute-start | bytes 1572872 | tf_op jit(solution)/shard_map/ppermute | solution.py:54
  21.8 2.5 %collective-permute-start.7 = (bf16[8,128,256]{2,1,0:T(8,128)(2,1)S(1)}, bf16[8,128,256]{2,1,0:T(8,128)(2,1)S(1)}, u32[]{:S(2)}, u32[]{:S(2)}) collective-permute-start(bf16[8,128,256]{2,1,0:T(8,128)(2,1)S(1)} %get-tuple-element.48), channel_id=1, source_target_pairs={{0,24},{1,7},{2,26},{3,1},{4,28},{5,3},{6,30},{7,5},{8,0},{9,15},{... | collective-permute-start | bytes 1572872 | tf_op jit(solution)/shard_map/ppermute | solution.py:54
  24.3 1.4 %collective-permute-start.9 = (bf16[8,128,256]{2,1,0:T(8,128)(2,1)S(1)}, bf16[8,128,256]{2,1,0:T(8,128)(2,1)S(1)}, u32[]{:S(2)}, u32[]{:S(2)}) collective-permute-start(bf16[8,128,256]{2,1,0:T(8,128)(2,1)S(1)} %get-tuple-element.47), channel_id=1, source_target_pairs={{0,24},{1,7},{2,26},{3,1},{4,28},{5,3},{6,30},{7,5},{8,0},{9,15},{... | collective-permute-start | bytes 1572872 | tf_op jit(solution)/shard_map/ppermute | solution.py:54
  25.8 5.3 %collective-permute-done.6.refs_0_ = bf16[8,128,256]{2,1,0:T(8,128)(2,1)S(1)} collective-permute-done((bf16[8,128,256]{2,1,0:T(8,128)(2,1)S(1)}, bf16[8,128,256]{2,1,0:T(8,128)(2,1)S(1)}, u32[]{:S(2)}, u32[]{:S(2)}) %collective-permute-start.6) | collective-permute-done | bytes 524320 | tf_op jit(solution)/shard_map/ppermute | solution.py:54
  32.0 1.9 %collective-permute-start.11 = (bf16[8,128,256]{2,1,0:T(8,128)(2,1)S(1)}, bf16[8,128,256]{2,1,0:T(8,128)(2,1)S(1)}, u32[]{:S(2)}, u32[]{:S(2)}) collective-permute-start(bf16[8,128,256]{2,1,0:T(8,128)(2,1)S(1)} %collective-permute-done.7.refs_1_), channel_id=1, source_target_pairs={{0,24},{1,7},{2,26},{3,1},{4,28},{5,3},{6,30},{7,5},{8,0},{9,15},{... | collective-permute-start | bytes 1572872 | tf_op jit(solution)/shard_map/ppermute | solution.py:54
  33.9 4.5 %collective-permute-start.13 = (bf16[16,128,256]{2,1,0:T(8,128)(2,1)S(1)}, bf16[16,128,256]{2,1,0:T(8,128)(2,1)S(1)}, u32[]{:S(2)}, u32[]{:S(2)}) collective-permute-start(bf16[16,128,256]{2,1,0:T(8,128)(2,1)S(1)} %join.6.rest_1_), channel_id=1, source_target_pairs={{0,1},{1,0},{2,3},{3,2},{4,5},{5,4},{6,7},{7,6},{8,9},{9,8},{10,11... | collective-permute-start | bytes 3145736 | tf_op jit(solution)/shard_map/ppermute | solution.py:66
  38.5 2.2 %collective-permute-start.12 = (bf16[16,128,256]{2,1,0:T(8,128)(2,1)S(1)}, bf16[16,128,256]{2,1,0:T(8,128)(2,1)S(1)}, u32[]{:S(2)}, u32[]{:S(2)}) collective-permute-start(bf16[16,128,256]{2,1,0:T(8,128)(2,1)S(1)} %join.5.x.rest_0_), channel_id=1, source_target_pairs={{0,1},{1,0},{2,3},{3,2},{4,5},{5,4},{6,7},{7,6},{8,9},{9,8},{10,11... | collective-permute-start | bytes 3145736 | tf_op jit(solution)/shard_map/ppermute | solution.py:66
  40.9 1.5 %collective-permute-done.10.rest_3_ = bf16[8,128,256]{2,1,0:T(8,128)(2,1)S(1)} collective-permute-done((bf16[8,128,256]{2,1,0:T(8,128)(2,1)S(1)}, bf16[8,128,256]{2,1,0:T(8,128)(2,1)S(1)}, u32[]{:S(2)}, u32[]{:S(2)}) %collective-permute-start.10) | collective-permute-done | bytes 524320 | tf_op jit(solution)/shard_map/ppermute | solution.py:54
  42.3 3.7 %collective-permute-start.15 = (bf16[8,128,256]{2,1,0:T(8,128)(2,1)S(1)}, bf16[8,128,256]{2,1,0:T(8,128)(2,1)S(1)}, u32[]{:S(2)}, u32[]{:S(2)}) collective-permute-start(bf16[8,128,256]{2,1,0:T(8,128)(2,1)S(1)} %collective-permute-done.10.rest_3_), channel_id=1, source_target_pairs={{0,1},{1,0},{2,3},{3,2},{4,5},{5,4},{6,7},{7,6},{8,9},{9,8},{10,11... | collective-permute-start | bytes 1572872 | tf_op jit(solution)/shard_map/ppermute | solution.py:66
  48.4 7.1 %layer.1 = (bf16[512,256]{1,0:T(8,128)(2,1)S(1)}, bf16[8,4096,128]{2,1,0:T(8,128)(2,1)S(1)}, f32[2,264,128]{2,1,0:T(8,128)S(1)}) custom-call(s32[1,16]{1,0:T(1,128)S(1)} %copy-done.4, s32[1]{0:T(128)S(6)} %copy.13.count_ref, bf16[512,8192]{1,0:T(8,128)(2,1)S(1)} %load.1.a_ref, bf16[256,256]{1,0:T(8,128)(2,1)S(1)} %copy-done, ...), custom_call_target="tpu_custom_call", output_to_operand_aliasing={{1}: (6, {})} | custom-call | flops 4294967296 | bytes 8388608 | tf_op jit(solution)/shard_map/layer/pallas_call | solution.py:186
  56.5 2.1 %collective-permute-done.18.te = f32[264,128]{1,0:T(8,128)S(1)} collective-permute-done((f32[264,128]{1,0:T(8,128)S(1)}, f32[264,128]{1,0:T(8,128)S(1)}, u32[]{:S(2)}, u32[]{:S(2)}) %collective-permute-start.18) | collective-permute-done | bytes 135200 | tf_op jit(solution)/shard_map/ppermute | solution.py:66
  60.6 1.5 %collective-permute-start.21 = (bf16[2320,128]{1,0:T(8,128)(2,1)S(1)}, bf16[2320,128]{1,0:T(8,128)(2,1)S(1)}, u32[]{:S(2)}, u32[]{:S(2)}) collective-permute-start(bf16[2320,128]{1,0:T(8,128)(2,1)S(1)} %get-tuple-element.60), channel_id=1, source_target_pairs={{0,24},{1,7},{2,26},{3,1},{4,28},{5,3},{6,30},{7,5},{8,0},{9,15},{... | collective-permute-start | bytes 1781768 | tf_op jit(solution)/shard_map/ppermute | solution.py:54
  63.1 7.2 %collective-permute-done.22.far = bf16[272,128]{1,0:T(8,128)(2,1)S(1)} collective-permute-done((bf16[272,128]{1,0:T(8,128)(2,1)S(1)}, bf16[272,128]{1,0:T(8,128)(2,1)S(1)}, u32[]{:S(2)}, u32[]{:S(2)}) %collective-permute-start.22) | collective-permute-done | bytes 69664 | tf_op jit(solution)/shard_map/ppermute | solution.py:54
  71.0 2.0 %collective-permute-start.23 = (bf16[4096,128]{1,0:T(8,128)(2,1)S(1)}, bf16[4096,128]{1,0:T(8,128)(2,1)S(1)}, u32[]{:S(2)}, u32[]{:S(2)}) collective-permute-start(bf16[4096,128]{1,0:T(8,128)(2,1)S(1)} %get-tuple-element.66), channel_id=1, source_target_pairs={{0,1},{1,0},{2,3},{3,2},{4,5},{5,4},{6,7},{7,6},{8,9},{9,8},{10,11... | collective-permute-start | bytes 3145736 | tf_op jit(solution)/shard_map/ppermute | solution.py:66
  74.1 1.6 %collective-permute-start.25 = (bf16[4096,128]{1,0:T(8,128)(2,1)S(1)}, bf16[4096,128]{1,0:T(8,128)(2,1)S(1)}, u32[]{:S(2)}, u32[]{:S(2)}) collective-permute-start(bf16[4096,128]{1,0:T(8,128)(2,1)S(1)} %get-tuple-element.68), channel_id=1, source_target_pairs={{0,24},{1,7},{2,26},{3,1},{4,28},{5,3},{6,30},{7,5},{8,0},{9,15},{... | collective-permute-start | bytes 3145736 | tf_op jit(solution)/shard_map/ppermute | solution.py:54
  75.7 13.1 %all_to_all.5.got = f32[16,24,128]{2,1,0:T(8,128)S(1)} all-to-all(f32[16,24,128]{2,1,0:T(8,128)S(1)} %extra_pieces.1._pieces), channel_id=1, replica_groups={{1,9,17,25,33,41,49,57,65,73,81,89,97,105,113,121},{3,11,19,27,35,43,51..., dimensions={0} | all-to-all | bytes 393216 | tf_op jit(solution)/shard_map/all_to_all | solution.py:40
  89.9 1.8 %collective-permute-start.26 = (bf16[1056,128]{1,0:T(8,128)(2,1)S(1)}, bf16[1056,128]{1,0:T(8,128)(2,1)S(1)}, u32[]{:S(2)}, u32[]{:S(2)}) collective-permute-start(bf16[1056,128]{1,0:T(8,128)(2,1)S(1)} %get-tuple-element.72), channel_id=1, source_target_pairs={{0,4},{1,65},{2,6},{3,67},{4,0},{5,69},{6,2},{7,71},{8,12},{9,73},... | collective-permute-start | bytes 811016 | tf_op jit(solution)/shard_map/ppermute | solution.py:54
  92.0 2.3 %collective-permute-start.28 = (bf16[1056,128]{1,0:T(8,128)(2,1)S(1)}, bf16[1056,128]{1,0:T(8,128)(2,1)S(1)}, u32[]{:S(2)}, u32[]{:S(2)}) collective-permute-start(bf16[1056,128]{1,0:T(8,128)(2,1)S(1)} %get-tuple-element.74), channel_id=1, source_target_pairs={{0,6},{1,97},{2,0},{3,99},{4,2},{5,101},{6,4},{7,103},{8,14},{9,10... | collective-permute-start | bytes 811016 | tf_op jit(solution)/shard_map/ppermute | solution.py:54
  94.3 2.7 %collective-permute-done.26.g2 = bf16[1056,128]{1,0:T(8,128)(2,1)S(1)} collective-permute-done((bf16[1056,128]{1,0:T(8,128)(2,1)S(1)}, bf16[1056,128]{1,0:T(8,128)(2,1)S(1)}, u32[]{:S(2)}, u32[]{:S(2)}) %collective-permute-start.26) | collective-permute-done | bytes 270368 | tf_op jit(solution)/shard_map/ppermute | solution.py:54
  97.0 2.9 %collective-permute-done.27.g1 = bf16[1056,128]{1,0:T(8,128)(2,1)S(1)} collective-permute-done((bf16[1056,128]{1,0:T(8,128)(2,1)S(1)}, bf16[1056,128]{1,0:T(8,128)(2,1)S(1)}, u32[]{:S(2)}, u32[]{:S(2)}) %collective-permute-start.27) | collective-permute-done | bytes 270368 | tf_op jit(solution)/shard_map/ppermute | solution.py:54
  101.1 1.9 %collective-permute-start.30 = (bf16[384,128]{1,0:T(8,128)(2,1)S(1)}, bf16[384,128]{1,0:T(8,128)(2,1)S(1)}, u32[]{:S(2)}, u32[]{:S(2)}) collective-permute-start(bf16[384,128]{1,0:T(8,128)(2,1)S(1)} %get-tuple-element.77), channel_id=1, source_target_pairs={{0,32},{1,9},{2,34},{3,11},{4,36},{5,13},{6,38},{7,15},{8,40},{9,1... | collective-permute-start | bytes 294920 | tf_op jit(solution)/shard_map/ppermute | solution.py:54
  103.7 1.4 %collective-permute-done.29.h2 = bf16[384,128]{1,0:T(8,128)(2,1)S(1)} collective-permute-done((bf16[384,128]{1,0:T(8,128)(2,1)S(1)}, bf16[384,128]{1,0:T(8,128)(2,1)S(1)}, u32[]{:S(2)}, u32[]{:S(2)}) %collective-permute-start.29) | collective-permute-done | bytes 98336 | tf_op jit(solution)/shard_map/ppermute | solution.py:54
  106.5 3.6 %collective-permute-start.32 = (f32[264,128]{1,0:T(8,128)S(1)}, f32[264,128]{1,0:T(8,128)S(1)}, u32[]{:S(2)}, u32[]{:S(2)}) collective-permute-start(f32[264,128]{1,0:T(8,128)S(1)} %extra_half.1.own), channel_id=1, source_target_pairs={{0,1},{1,0},{2,3},{3,2},{4,5},{5,4},{6,7},{7,6},{8,9},{9,8},{10,11... | collective-permute-start | bytes 405512 | tf_op jit(solution)/shard_map/ppermute | solution.py:66
  (65 shorter events, 17.2 us)
Async XLA Ops:
  0.6 8.7 %collective-permute-start.2 = (bf16[1,128,256]{2,1,0:T(8,128)(2,1)}, bf16[1,128,256]{2,1,0:T(8,128)(2,1)S(1)}, u32[]{:S(2)}, u32[]{:S(2)}) collective-permute-start(bf16[1,128,256]{2,1,0:T(8,128)(2,1)} %bitcast.10), channel_id=1, source_target_pairs={{0,32},{1,9},{2,34},{3,11},{4,36},{5,13},{6,38},{7,15},{8,40},{9,1... | collective-permute-start | bytes 196616 | tf_op jit(solution)/shard_map/ppermute | solution.py:54
  2.7 6.6 %collective-permute-start.1 = (bf16[1,128,256]{2,1,0:T(8,128)(2,1)}, bf16[1,128,256]{2,1,0:T(8,128)(2,1)S(1)}, u32[]{:S(2)}, u32[]{:S(2)}) collective-permute-start(bf16[1,128,256]{2,1,0:T(8,128)(2,1)} %bitcast.11), channel_id=1, source_target_pairs={{0,96},{1,25},{2,98},{3,27},{4,100},{5,29},{6,102},{7,31},{8,104},... | collective-permute-start | bytes 196616 | tf_op jit(solution)/shard_map/ppermute | solution.py:54
  4.1 5.3 %collective-permute-start = (bf16[1,128,256]{2,1,0:T(8,128)(2,1)}, bf16[1,128,256]{2,1,0:T(8,128)(2,1)S(1)}, u32[]{:S(2)}, u32[]{:S(2)}) collective-permute-start(bf16[1,128,256]{2,1,0:T(8,128)(2,1)} %bitcast.12), channel_id=1, source_target_pairs={{0,64},{1,17},{2,66},{3,19},{4,68},{5,21},{6,70},{7,23},{8,72},{9,... | collective-permute-start | bytes 196616 | tf_op jit(solution)/shard_map/ppermute | solution.py:54
  9.4 6.6 %collective-permute-start.5 = (bf16[4,128,256]{2,1,0:T(8,128)(2,1)S(1)}, bf16[4,128,256]{2,1,0:T(8,128)(2,1)S(1)}, u32[]{:S(2)}, u32[]{:S(2)}) collective-permute-start(bf16[4,128,256]{2,1,0:T(8,128)(2,1)S(1)} %join.4.refs_0_._after), channel_id=1, source_target_pairs={{0,2},{1,33},{2,4},{3,35},{4,6},{5,37},{6,0},{7,39},{8,10},{9,41},... | collective-permute-start | bytes 786440 | tf_op jit(solution)/shard_map/ppermute | solution.py:54
  10.8 7.6 %collective-permute-start.4 = (bf16[4,128,256]{2,1,0:T(8,128)(2,1)S(1)}, bf16[4,128,256]{2,1,0:T(8,128)(2,1)S(1)}, u32[]{:S(2)}, u32[]{:S(2)}) collective-permute-start(bf16[4,128,256]{2,1,0:T(8,128)(2,1)S(1)} %join.4.refs_0_._after), channel_id=1, source_target_pairs={{0,6},{1,97},{2,0},{3,99},{4,2},{5,101},{6,4},{7,103},{8,14},{9,10... | collective-permute-start | bytes 786440 | tf_op jit(solution)/shard_map/ppermute | solution.py:54
  12.3 7.7 %collective-permute-start.3 = (bf16[4,128,256]{2,1,0:T(8,128)(2,1)S(1)}, bf16[4,128,256]{2,1,0:T(8,128)(2,1)S(1)}, u32[]{:S(2)}, u32[]{:S(2)}) collective-permute-start(bf16[4,128,256]{2,1,0:T(8,128)(2,1)S(1)} %join.4.refs_0_._after), channel_id=1, source_target_pairs={{0,4},{1,65},{2,6},{3,67},{4,0},{5,69},{6,2},{7,71},{8,12},{9,73},... | collective-permute-start | bytes 786440 | tf_op jit(solution)/shard_map/ppermute | solution.py:54
  20.1 11.0 %collective-permute-start.6 = (bf16[8,128,256]{2,1,0:T(8,128)(2,1)S(1)}, bf16[8,128,256]{2,1,0:T(8,128)(2,1)S(1)}, u32[]{:S(2)}, u32[]{:S(2)}) collective-permute-start(bf16[8,128,256]{2,1,0:T(8,128)(2,1)S(1)} %get-tuple-element.47), channel_id=1, source_target_pairs={{0,8},{1,3},{2,10},{3,5},{4,12},{5,7},{6,14},{7,1},{8,16},{9,11},{... | collective-permute-start | bytes 1572872 | tf_op jit(solution)/shard_map/ppermute | solution.py:54
  21.8 9.3 %collective-permute-start.7 = (bf16[8,128,256]{2,1,0:T(8,128)(2,1)S(1)}, bf16[8,128,256]{2,1,0:T(8,128)(2,1)S(1)}, u32[]{:S(2)}, u32[]{:S(2)}) collective-permute-start(bf16[8,128,256]{2,1,0:T(8,128)(2,1)S(1)} %get-tuple-element.48), channel_id=1, source_target_pairs={{0,24},{1,7},{2,26},{3,1},{4,28},{5,3},{6,30},{7,5},{8,0},{9,15},{... | collective-permute-start | bytes 1572872 | tf_op jit(solution)/shard_map/ppermute | solution.py:54
  24.3 14.1 %collective-permute-start.9 = (bf16[8,128,256]{2,1,0:T(8,128)(2,1)S(1)}, bf16[8,128,256]{2,1,0:T(8,128)(2,1)S(1)}, u32[]{:S(2)}, u32[]{:S(2)}) collective-permute-start(bf16[8,128,256]{2,1,0:T(8,128)(2,1)S(1)} %get-tuple-element.47), channel_id=1, source_target_pairs={{0,24},{1,7},{2,26},{3,1},{4,28},{5,3},{6,30},{7,5},{8,0},{9,15},{... | collective-permute-start | bytes 1572872 | tf_op jit(solution)/shard_map/ppermute | solution.py:54
  25.7 15.0 %collective-permute-start.8 = (bf16[8,128,256]{2,1,0:T(8,128)(2,1)S(1)}, bf16[8,128,256]{2,1,0:T(8,128)(2,1)S(1)}, u32[]{:S(2)}, u32[]{:S(2)}) collective-permute-start(bf16[8,128,256]{2,1,0:T(8,128)(2,1)S(1)} %get-tuple-element.48), channel_id=1, source_target_pairs={{0,8},{1,3},{2,10},{3,5},{4,12},{5,7},{6,14},{7,1},{8,16},{9,11},{... | collective-permute-start | bytes 1572872 | tf_op jit(solution)/shard_map/ppermute | solution.py:54
  31.1 11.2 %collective-permute-start.10 = (bf16[8,128,256]{2,1,0:T(8,128)(2,1)S(1)}, bf16[8,128,256]{2,1,0:T(8,128)(2,1)S(1)}, u32[]{:S(2)}, u32[]{:S(2)}) collective-permute-start(bf16[8,128,256]{2,1,0:T(8,128)(2,1)S(1)} %collective-permute-done.6.refs_0_), channel_id=1, source_target_pairs={{0,8},{1,3},{2,10},{3,5},{4,12},{5,7},{6,14},{7,1},{8,16},{9,11},{... | collective-permute-start | bytes 1572872 | tf_op jit(solution)/shard_map/ppermute | solution.py:54
  32.0 14.1 %collective-permute-start.11 = (bf16[8,128,256]{2,1,0:T(8,128)(2,1)S(1)}, bf16[8,128,256]{2,1,0:T(8,128)(2,1)S(1)}, u32[]{:S(2)}, u32[]{:S(2)}) collective-permute-start(bf16[8,128,256]{2,1,0:T(8,128)(2,1)S(1)} %collective-permute-done.7.refs_1_), channel_id=1, source_target_pairs={{0,24},{1,7},{2,26},{3,1},{4,28},{5,3},{6,30},{7,5},{8,0},{9,15},{... | collective-permute-start | bytes 1572872 | tf_op jit(solution)/shard_map/ppermute | solution.py:54
  33.9 14.4 %collective-permute-start.13 = (bf16[16,128,256]{2,1,0:T(8,128)(2,1)S(1)}, bf16[16,128,256]{2,1,0:T(8,128)(2,1)S(1)}, u32[]{:S(2)}, u32[]{:S(2)}) collective-permute-start(bf16[16,128,256]{2,1,0:T(8,128)(2,1)S(1)} %join.6.rest_1_), channel_id=1, source_target_pairs={{0,1},{1,0},{2,3},{3,2},{4,5},{5,4},{6,7},{7,6},{8,9},{9,8},{10,11... | collective-permute-start | bytes 3145736 | tf_op jit(solution)/shard_map/ppermute | solution.py:66
  38.5 9.9 %collective-permute-start.12 = (bf16[16,128,256]{2,1,0:T(8,128)(2,1)S(1)}, bf16[16,128,256]{2,1,0:T(8,128)(2,1)S(1)}, u32[]{:S(2)}, u32[]{:S(2)}) collective-permute-start(bf16[16,128,256]{2,1,0:T(8,128)(2,1)S(1)} %join.5.x.rest_0_), channel_id=1, source_target_pairs={{0,1},{1,0},{2,3},{3,2},{4,5},{5,4},{6,7},{7,6},{8,9},{9,8},{10,11... | collective-permute-start | bytes 3145736 | tf_op jit(solution)/shard_map/ppermute | solution.py:66
  40.8 7.6 %collective-permute-start.14 = (bf16[16,128,256]{2,1,0:T(8,128)(2,1)S(1)}, bf16[16,128,256]{2,1,0:T(8,128)(2,1)S(1)}, u32[]{:S(2)}, u32[]{:S(2)}) collective-permute-start(bf16[16,128,256]{2,1,0:T(8,128)(2,1)S(1)} %join.7.rest_2_), channel_id=1, source_target_pairs={{0,1},{1,0},{2,3},{3,2},{4,5},{5,4},{6,7},{7,6},{8,9},{9,8},{10,11... | collective-permute-start | bytes 3145736 | tf_op jit(solution)/shard_map/ppermute | solution.py:66
  42.3 5.2 %collective-permute-start.15 = (bf16[8,128,256]{2,1,0:T(8,128)(2,1)S(1)}, bf16[8,128,256]{2,1,0:T(8,128)(2,1)S(1)}, u32[]{:S(2)}, u32[]{:S(2)}) collective-permute-start(bf16[8,128,256]{2,1,0:T(8,128)(2,1)S(1)} %collective-permute-done.10.rest_3_), channel_id=1, source_target_pairs={{0,1},{1,0},{2,3},{3,2},{4,5},{5,4},{6,7},{7,6},{8,9},{9,8},{10,11... | collective-permute-start | bytes 1572872 | tf_op jit(solution)/shard_map/ppermute | solution.py:66
  55.7 2.9 %collective-permute-start.17 = (bf16[4096,128]{1,0:T(8,128)(2,1)S(1)}, bf16[4096,128]{1,0:T(8,128)(2,1)S(1)}, u32[]{:S(2)}, u32[]{:S(2)}) collective-permute-start(bf16[4096,128]{1,0:T(8,128)(2,1)S(1)} %get-tuple-element.83), channel_id=1, source_target_pairs={{0,1},{1,0},{2,3},{3,2},{4,5},{5,4},{6,7},{7,6},{8,9},{9,8},{10,11... | collective-permute-start | bytes 3145736 | tf_op jit(solution)/shard_map/ppermute | solution.py:66
  56.1 2.5 %collective-permute-start.18 = (f32[264,128]{1,0:T(8,128)S(1)}, f32[264,128]{1,0:T(8,128)S(1)}, u32[]{:S(2)}, u32[]{:S(2)}) collective-permute-start(f32[264,128]{1,0:T(8,128)S(1)} %slice_bitcast_fusion.2), channel_id=1, source_target_pairs={{0,1},{1,0},{2,3},{3,2},{4,5},{5,4},{6,7},{7,6},{8,9},{9,8},{10,11... | collective-permute-start | bytes 405512 | tf_op jit(solution)/shard_map/ppermute | solution.py:66
  58.9 11.5 %collective-permute-start.19 = (bf16[2,4096,128]{2,1,0:T(8,128)(2,1)S(1)}, bf16[2,4096,128]{2,1,0:T(8,128)(2,1)S(1)}, u32[]{:S(2)}, u32[]{:S(2)}) collective-permute-start(bf16[2,4096,128]{2,1,0:T(8,128)(2,1)S(1)} %slice.14), channel_id=1, source_target_pairs={{0,1},{1,0},{2,3},{3,2},{4,5},{5,4},{6,7},{7,6},{8,9},{9,8},{10,11... | collective-permute-start | bytes 6291464 | tf_op jit(solution)/shard_map/ppermute | solution.py:66
  59.5 10.8 %collective-permute-start.20 = (bf16[2320,128]{1,0:T(8,128)(2,1)S(1)}, bf16[2320,128]{1,0:T(8,128)(2,1)S(1)}, u32[]{:S(2)}, u32[]{:S(2)}) collective-permute-start(bf16[2320,128]{1,0:T(8,128)(2,1)S(1)} %get-tuple-element.59), channel_id=1, source_target_pairs={{0,8},{1,3},{2,10},{3,5},{4,12},{5,7},{6,14},{7,1},{8,16},{9,11},{... | collective-permute-start | bytes 1781768 | tf_op jit(solution)/shard_map/ppermute | solution.py:54
  60.6 9.7 %collective-permute-start.21 = (bf16[2320,128]{1,0:T(8,128)(2,1)S(1)}, bf16[2320,128]{1,0:T(8,128)(2,1)S(1)}, u32[]{:S(2)}, u32[]{:S(2)}) collective-permute-start(bf16[2320,128]{1,0:T(8,128)(2,1)S(1)} %get-tuple-element.60), channel_id=1, source_target_pairs={{0,24},{1,7},{2,26},{3,1},{4,28},{5,3},{6,30},{7,5},{8,0},{9,15},{... | collective-permute-start | bytes 1781768 | tf_op jit(solution)/shard_map/ppermute | solution.py:54
  62.2 8.1 %collective-permute-start.22 = (bf16[272,128]{1,0:T(8,128)(2,1)S(1)}, bf16[272,128]{1,0:T(8,128)(2,1)S(1)}, u32[]{:S(2)}, u32[]{:S(2)}) collective-permute-start(bf16[272,128]{1,0:T(8,128)(2,1)S(1)} %get-tuple-element.61), channel_id=1, source_target_pairs={{0,16},{1,5},{2,18},{3,7},{4,20},{5,1},{6,22},{7,3},{8,24},{9,13},... | collective-permute-start | bytes 208904 | tf_op jit(solution)/shard_map/ppermute | solution.py:54
  71.0 17.8 %collective-permute-start.23 = (bf16[4096,128]{1,0:T(8,128)(2,1)S(1)}, bf16[4096,128]{1,0:T(8,128)(2,1)S(1)}, u32[]{:S(2)}, u32[]{:S(2)}) collective-permute-start(bf16[4096,128]{1,0:T(8,128)(2,1)S(1)} %get-tuple-element.66), channel_id=1, source_target_pairs={{0,1},{1,0},{2,3},{3,2},{4,5},{5,4},{6,7},{7,6},{8,9},{9,8},{10,11... | collective-permute-start | bytes 3145736 | tf_op jit(solution)/shard_map/ppermute | solution.py:66
  73.0 16.2 %collective-permute-start.24 = (bf16[4096,128]{1,0:T(8,128)(2,1)S(1)}, bf16[4096,128]{1,0:T(8,128)(2,1)S(1)}, u32[]{:S(2)}, u32[]{:S(2)}) collective-permute-start(bf16[4096,128]{1,0:T(8,128)(2,1)S(1)} %get-tuple-element.67), channel_id=1, source_target_pairs={{0,8},{1,3},{2,10},{3,5},{4,12},{5,7},{6,14},{7,1},{8,16},{9,11},{... | collective-permute-start | bytes 3145736 | tf_op jit(solution)/shard_map/ppermute | solution.py:54
  74.1 15.1 %collective-permute-start.25 = (bf16[4096,128]{1,0:T(8,128)(2,1)S(1)}, bf16[4096,128]{1,0:T(8,128)(2,1)S(1)}, u32[]{:S(2)}, u32[]{:S(2)}) collective-permute-start(bf16[4096,128]{1,0:T(8,128)(2,1)S(1)} %get-tuple-element.68), channel_id=1, source_target_pairs={{0,24},{1,7},{2,26},{3,1},{4,28},{5,3},{6,30},{7,5},{8,0},{9,15},{... | collective-permute-start | bytes 3145736 | tf_op jit(solution)/shard_map/ppermute | solution.py:54
  89.9 7.2 %collective-permute-start.26 = (bf16[1056,128]{1,0:T(8,128)(2,1)S(1)}, bf16[1056,128]{1,0:T(8,128)(2,1)S(1)}, u32[]{:S(2)}, u32[]{:S(2)}) collective-permute-start(bf16[1056,128]{1,0:T(8,128)(2,1)S(1)} %get-tuple-element.72), channel_id=1, source_target_pairs={{0,4},{1,65},{2,6},{3,67},{4,0},{5,69},{6,2},{7,71},{8,12},{9,73},... | collective-permute-start | bytes 811016 | tf_op jit(solution)/shard_map/ppermute | solution.py:54
  91.6 8.3 %collective-permute-start.27 = (bf16[1056,128]{1,0:T(8,128)(2,1)S(1)}, bf16[1056,128]{1,0:T(8,128)(2,1)S(1)}, u32[]{:S(2)}, u32[]{:S(2)}) collective-permute-start(bf16[1056,128]{1,0:T(8,128)(2,1)S(1)} %get-tuple-element.73), channel_id=1, source_target_pairs={{0,2},{1,33},{2,4},{3,35},{4,6},{5,37},{6,0},{7,39},{8,10},{9,41},... | collective-permute-start | bytes 811016 | tf_op jit(solution)/shard_map/ppermute | solution.py:54
  92.0 7.9 %collective-permute-start.28 = (bf16[1056,128]{1,0:T(8,128)(2,1)S(1)}, bf16[1056,128]{1,0:T(8,128)(2,1)S(1)}, u32[]{:S(2)}, u32[]{:S(2)}) collective-permute-start(bf16[1056,128]{1,0:T(8,128)(2,1)S(1)} %get-tuple-element.74), channel_id=1, source_target_pairs={{0,6},{1,97},{2,0},{3,99},{4,2},{5,101},{6,4},{7,103},{8,14},{9,10... | collective-permute-start | bytes 811016 | tf_op jit(solution)/shard_map/ppermute | solution.py:54
  100.1 5.1 %collective-permute-start.29 = (bf16[384,128]{1,0:T(8,128)(2,1)S(1)}, bf16[384,128]{1,0:T(8,128)(2,1)S(1)}, u32[]{:S(2)}, u32[]{:S(2)}) collective-permute-start(bf16[384,128]{1,0:T(8,128)(2,1)S(1)} %get-tuple-element.76), channel_id=1, source_target_pairs={{0,64},{1,17},{2,66},{3,19},{4,68},{5,21},{6,70},{7,23},{8,72},{9,... | collective-permute-start | bytes 294920 | tf_op jit(solution)/shard_map/ppermute | solution.py:54
  101.1 5.1 %collective-permute-start.30 = (bf16[384,128]{1,0:T(8,128)(2,1)S(1)}, bf16[384,128]{1,0:T(8,128)(2,1)S(1)}, u32[]{:S(2)}, u32[]{:S(2)}) collective-permute-start(bf16[384,128]{1,0:T(8,128)(2,1)S(1)} %get-tuple-element.77), channel_id=1, source_target_pairs={{0,32},{1,9},{2,34},{3,11},{4,36},{5,13},{6,38},{7,15},{8,40},{9,1... | collective-permute-start | bytes 294920 | tf_op jit(solution)/shard_map/ppermute | solution.py:54
  103.0 3.5 %collective-permute-start.31 = (bf16[384,128]{1,0:T(8,128)(2,1)S(1)}, bf16[384,128]{1,0:T(8,128)(2,1)S(1)}, u32[]{:S(2)}, u32[]{:S(2)}) collective-permute-start(bf16[384,128]{1,0:T(8,128)(2,1)S(1)} %get-tuple-element.78), channel_id=1, source_target_pairs={{0,96},{1,25},{2,98},{3,27},{4,100},{5,29},{6,102},{7,31},{8,104},... | collective-permute-start | bytes 294920 | tf_op jit(solution)/shard_map/ppermute | solution.py:54
  106.5 4.6 %collective-permute-start.32 = (f32[264,128]{1,0:T(8,128)S(1)}, f32[264,128]{1,0:T(8,128)S(1)}, u32[]{:S(2)}, u32[]{:S(2)}) collective-permute-start(f32[264,128]{1,0:T(8,128)S(1)} %extra_half.1.own), channel_id=1, source_target_pairs={{0,1},{1,0},{2,3},{3,2},{4,5},{5,4},{6,7},{7,6},{8,9},{9,8},{10,11... | collective-permute-start | bytes 405512 | tf_op jit(solution)/shard_map/ppermute | solution.py:66
  (6 other events, 162.0 us)

commit v5 on v4

--- a/solution.py
+++ b/solution.py
@@ -126,9 +126,7 @@
             length = ref.shape[0] // len(starts)
             for i, start in enumerate(starts):
                 g_buf[side, start : start + length] = ref[i * length : i * length + length]
-    acc[...] = jnp.zeros_like(acc)
-
-    def forward(g, carry):
+    def forward(g):
         for q in range(GROUP):
             s = g * GROUP + q
             t = col_ref[0, s]
@@ -139,11 +137,11 @@
                 piece = g_buf[jnp.where(core == cc, 0, 1), at]
                 rows = slice(q * 512 + j * 128, q * 512 + j * 128 + 128)
                 x_buf[rows] = jnp.where(live, piece, jnp.zeros_like(piece))
-        columns = pl.ds(pl.multiple_of(g * (GROUP * 512), GROUP * 512), GROUP * 512)
-        acc[...] += dot(a_ref[:, columns], x_buf[...], ((1,), (0,)))
-        return carry
-
-    lax.fori_loop(0, 16 // GROUP, forward, 0)
+        columns = slice(g * GROUP * 512, (g + 1) * GROUP * 512)
+        return dot(a_ref[:, columns], x_buf[...], ((1,), (0,)))
+
+    acc[...] = forward(0)
+    acc[...] += forward(1)
 
     agg = acc[...].astype(BF16)
     pre = dot(agg, w_ref[...], ((1,), (0,))) + b_ref[...]

time: 112 us -> 111 us (level)
  no operation moved by 1% of the time
where the time goes in v5:
time: 111 us
  starting transfers between devices  49.5 us (45%)
  waiting for transfers between devices  31.1 us (28%)
  Pallas kernels  15.8 us (14%)
  blocking collectives  13.1 us (12%)
  between operations  1.53 us (1%)
    ppermute x23, starting transfers between devices, hop(): return lax.ppermute(x, AXIS, pairs(move))  31.7 us
    ppermute x23, waiting for transfers between devices, hop(): return lax.ppermute(x, AXIS, pairs(move))  27.7 us
    ppermute x10, starting transfers between devices, swap(): return lax.ppermute(x, AXIS, pairs(move))  17.7 us
    all_to_all x1, blocking collectives, exchange(): lax.all_to_all(x, AXIS, split_axis=0, concat_axis=0, tiled=True, axis_ind...  13.1 us
    pallas_call x1, Pallas kernels, local(): pl.pallas_call(kernel, out_shape=(pltpu.VMEM((512, 256), BF16), pltpu.VME...  6.83 us
    pallas_call x13, Pallas kernels, in_vmem(): pl.pallas_call(body, out_shape=tuple((o if last else pltpu.VMEM(o.shape,...  3.98 us
    pallas_call x1, Pallas kernels, load(): pl.pallas_call(load_kernel, out_shape=pltpu.VMEM((512, 8192), BF16), in_s...  3.54 us
    ppermute x10, waiting for transfers between devices, swap(): return lax.ppermute(x, AXIS, pairs(move))  3.4 us
  transfers between devices with their start and end apart: 33, of which 16 were waited for; matrix products, arithmetic and copies ran while one was open for 0% of the time, Pallas kernels for 6%

profile of v5, /device:TPU:1, one launch (start us, length us, event | category | flops | bytes accessed | tf_op | source)
XLA Modules:
  0.0 111.3 jit_solution(14066975493371766101)
XLA Ops:
  0.6 2.1 %collective-permute-start.2 = (bf16[1,128,256]{2,1,0:T(8,128)(2,1)}, bf16[1,128,256]{2,1,0:T(8,128)(2,1)S(1)}, u32[]{:S(2)}, u32[]{:S(2)}) collective-permute-start(bf16[1,128,256]{2,1,0:T(8,128)(2,1)} %bitcast.10), channel_id=1, source_target_pairs={{0,32},{1,9},{2,34},{3,11},{4,36},{5,13},{6,38},{7,15},{8,40},{9,1... | collective-permute-start | bytes 196616 | tf_op jit(solution)/shard_map/ppermute | solution.py:54
  2.7 1.3 %collective-permute-start.1 = (bf16[1,128,256]{2,1,0:T(8,128)(2,1)}, bf16[1,128,256]{2,1,0:T(8,128)(2,1)S(1)}, u32[]{:S(2)}, u32[]{:S(2)}) collective-permute-start(bf16[1,128,256]{2,1,0:T(8,128)(2,1)} %bitcast.11), channel_id=1, source_target_pairs={{0,96},{1,25},{2,98},{3,27},{4,100},{5,29},{6,102},{7,31},{8,104},... | collective-permute-start | bytes 196616 | tf_op jit(solution)/shard_map/ppermute | solution.py:54
  4.1 1.6 %collective-permute-start = (bf16[1,128,256]{2,1,0:T(8,128)(2,1)}, bf16[1,128,256]{2,1,0:T(8,128)(2,1)S(1)}, u32[]{:S(2)}, u32[]{:S(2)}) collective-permute-start(bf16[1,128,256]{2,1,0:T(8,128)(2,1)} %bitcast.12), channel_id=1, source_target_pairs={{0,64},{1,17},{2,66},{3,19},{4,68},{5,21},{6,70},{7,23},{8,72},{9,... | collective-permute-start | bytes 196616 | tf_op jit(solution)/shard_map/ppermute | solution.py:54
  5.7 3.5 %load.1.a_ref = bf16[512,8192]{1,0:T(8,128)(2,1)S(1)} custom-call(bf16[16,512,512]{2,1,0:T(8,128)(2,1)} %bitcast.15), custom_call_target="tpu_custom_call" | custom-call | bytes 16777216 | tf_op jit(solution)/shard_map/load/pallas_call | solution.py:85
  9.4 1.4 %collective-permute-start.5 = (bf16[4,128,256]{2,1,0:T(8,128)(2,1)S(1)}, bf16[4,128,256]{2,1,0:T(8,128)(2,1)S(1)}, u32[]{:S(2)}, u32[]{:S(2)}) collective-permute-start(bf16[4,128,256]{2,1,0:T(8,128)(2,1)S(1)} %join.4.refs_0_._after), channel_id=1, source_target_pairs={{0,2},{1,33},{2,4},{3,35},{4,6},{5,37},{6,0},{7,39},{8,10},{9,41},... | collective-permute-start | bytes 786440 | tf_op jit(solution)/shard_map/ppermute | solution.py:54
  10.8 1.5 %collective-permute-start.4 = (bf16[4,128,256]{2,1,0:T(8,128)(2,1)S(1)}, bf16[4,128,256]{2,1,0:T(8,128)(2,1)S(1)}, u32[]{:S(2)}, u32[]{:S(2)}) collective-permute-start(bf16[4,128,256]{2,1,0:T(8,128)(2,1)S(1)} %join.4.refs_0_._after), channel_id=1, source_target_pairs={{0,6},{1,97},{2,0},{3,99},{4,2},{5,101},{6,4},{7,103},{8,14},{9,10... | collective-permute-start | bytes 786440 | tf_op jit(solution)/shard_map/ppermute | solution.py:54
  12.3 1.6 %collective-permute-start.3 = (bf16[4,128,256]{2,1,0:T(8,128)(2,1)S(1)}, bf16[4,128,256]{2,1,0:T(8,128)(2,1)S(1)}, u32[]{:S(2)}, u32[]{:S(2)}) collective-permute-start(bf16[4,128,256]{2,1,0:T(8,128)(2,1)S(1)} %join.4.refs_0_._after), channel_id=1, source_target_pairs={{0,4},{1,65},{2,6},{3,67},{4,0},{5,69},{6,2},{7,71},{8,12},{9,73},... | collective-permute-start | bytes 786440 | tf_op jit(solution)/shard_map/ppermute | solution.py:54
  16.0 2.4 %collective-permute-done.4.refs_2_ = bf16[4,128,256]{2,1,0:T(8,128)(2,1)S(1)} collective-permute-done((bf16[4,128,256]{2,1,0:T(8,128)(2,1)S(1)}, bf16[4,128,256]{2,1,0:T(8,128)(2,1)S(1)}, u32[]{:S(2)}, u32[]{:S(2)}) %collective-permute-start.4) | collective-permute-done | bytes 262176 | tf_op jit(solution)/shard_map/ppermute | solution.py:54
  18.4 1.5 %collective-permute-done.3.refs_1_ = bf16[4,128,256]{2,1,0:T(8,128)(2,1)S(1)} collective-permute-done((bf16[4,128,256]{2,1,0:T(8,128)(2,1)S(1)}, bf16[4,128,256]{2,1,0:T(8,128)(2,1)S(1)}, u32[]{:S(2)}, u32[]{:S(2)}) %collective-permute-start.3) | collective-permute-done | bytes 262176 | tf_op jit(solution)/shard_map/ppermute | solution.py:54
  20.1 1.7 %collective-permute-start.6 = (bf16[8,128,256]{2,1,0:T(8,128)(2,1)S(1)}, bf16[8,128,256]{2,1,0:T(8,128)(2,1)S(1)}, u32[]{:S(2)}, u32[]{:S(2)}) collective-permute-start(bf16[8,128,256]{2,1,0:T(8,128)(2,1)S(1)} %get-tuple-element.47), channel_id=1, source_target_pairs={{0,8},{1,3},{2,10},{3,5},{4,12},{5,7},{6,14},{7,1},{8,16},{9,11},{... | collective-permute-start | bytes 1572872 | tf_op jit(solution)/shard_map/ppermute | solution.py:54
  21.8 2.5 %collective-permute-start.7 = (bf16[8,128,256]{2,1,0:T(8,128)(2,1)S(1)}, bf16[8,128,256]{2,1,0:T(8,128)(2,1)S(1)}, u32[]{:S(2)}, u32[]{:S(2)}) collective-permute-start(bf16[8,128,256]{2,1,0:T(8,128)(2,1)S(1)} %get-tuple-element.48), channel_id=1, source_target_pairs={{0,24},{1,7},{2,26},{3,1},{4,28},{5,3},{6,30},{7,5},{8,0},{9,15},{... | collective-permute-start | bytes 1572872 | tf_op jit(solution)/shard_map/ppermute | solution.py:54
  24.3 1.4 %collective-permute-start.9 = (bf16[8,128,256]{2,1,0:T(8,128)(2,1)S(1)}, bf16[8,128,256]{2,1,0:T(8,128)(2,1)S(1)}, u32[]{:S(2)}, u32[]{:S(2)}) collective-permute-start(bf16[8,128,256]{2,1,0:T(8,128)(2,1)S(1)} %get-tuple-element.47), channel_id=1, source_target_pairs={{0,24},{1,7},{2,26},{3,1},{4,28},{5,3},{6,30},{7,5},{8,0},{9,15},{... | collective-permute-start | bytes 1572872 | tf_op jit(solution)/shard_map/ppermute | solution.py:54
  25.8 5.3 %collective-permute-done.6.refs_0_ = bf16[8,128,256]{2,1,0:T(8,128)(2,1)S(1)} collective-permute-done((bf16[8,128,256]{2,1,0:T(8,128)(2,1)S(1)}, bf16[8,128,256]{2,1,0:T(8,128)(2,1)S(1)}, u32[]{:S(2)}, u32[]{:S(2)}) %collective-permute-start.6) | collective-permute-done | bytes 524320 | tf_op jit(solution)/shard_map/ppermute | solution.py:54
  32.0 1.9 %collective-permute-start.11 = (bf16[8,128,256]{2,1,0:T(8,128)(2,1)S(1)}, bf16[8,128,256]{2,1,0:T(8,128)(2,1)S(1)}, u32[]{:S(2)}, u32[]{:S(2)}) collective-permute-start(bf16[8,128,256]{2,1,0:T(8,128)(2,1)S(1)} %collective-permute-done.7.refs_1_), channel_id=1, source_target_pairs={{0,24},{1,7},{2,26},{3,1},{4,28},{5,3},{6,30},{7,5},{8,0},{9,15},{... | collective-permute-start | bytes 1572872 | tf_op jit(solution)/shard_map/ppermute | solution.py:54
  33.9 4.5 %collective-permute-start.13 = (bf16[16,128,256]{2,1,0:T(8,128)(2,1)S(1)}, bf16[16,128,256]{2,1,0:T(8,128)(2,1)S(1)}, u32[]{:S(2)}, u32[]{:S(2)}) collective-permute-start(bf16[16,128,256]{2,1,0:T(8,128)(2,1)S(1)} %join.6.rest_1_), channel_id=1, source_target_pairs={{0,1},{1,0},{2,3},{3,2},{4,5},{5,4},{6,7},{7,6},{8,9},{9,8},{10,11... | collective-permute-start | bytes 3145736 | tf_op jit(solution)/shard_map/ppermute | solution.py:66
  38.5 2.2 %collective-permute-start.12 = (bf16[16,128,256]{2,1,0:T(8,128)(2,1)S(1)}, bf16[16,128,256]{2,1,0:T(8,128)(2,1)S(1)}, u32[]{:S(2)}, u32[]{:S(2)}) collective-permute-start(bf16[16,128,256]{2,1,0:T(8,128)(2,1)S(1)} %join.5.x.rest_0_), channel_id=1, source_target_pairs={{0,1},{1,0},{2,3},{3,2},{4,5},{5,4},{6,7},{7,6},{8,9},{9,8},{10,11... | collective-permute-start | bytes 3145736 | tf_op jit(solution)/shard_map/ppermute | solution.py:66
  40.9 1.5 %collective-permute-done.10.rest_3_ = bf16[8,128,256]{2,1,0:T(8,128)(2,1)S(1)} collective-permute-done((bf16[8,128,256]{2,1,0:T(8,128)(2,1)S(1)}, bf16[8,128,256]{2,1,0:T(8,128)(2,1)S(1)}, u32[]{:S(2)}, u32[]{:S(2)}) %collective-permute-start.10) | collective-permute-done | bytes 524320 | tf_op jit(solution)/shard_map/ppermute | solution.py:54
  42.3 3.7 %collective-permute-start.15 = (bf16[8,128,256]{2,1,0:T(8,128)(2,1)S(1)}, bf16[8,128,256]{2,1,0:T(8,128)(2,1)S(1)}, u32[]{:S(2)}, u32[]{:S(2)}) collective-permute-start(bf16[8,128,256]{2,1,0:T(8,128)(2,1)S(1)} %collective-permute-done.10.rest_3_), channel_id=1, source_target_pairs={{0,1},{1,0},{2,3},{3,2},{4,5},{5,4},{6,7},{7,6},{8,9},{9,8},{10,11... | collective-permute-start | bytes 1572872 | tf_op jit(solution)/shard_map/ppermute | solution.py:66
  48.4 6.8 %layer.1 = (bf16[512,256]{1,0:T(8,128)(2,1)S(1)}, bf16[8,4096,128]{2,1,0:T(8,128)(2,1)S(1)}, f32[2,264,128]{2,1,0:T(8,128)S(1)}) custom-call(s32[1,16]{1,0:T(1,128)S(1)} %copy-done.4, s32[1]{0:T(128)S(6)} %copy.13.count_ref, bf16[512,8192]{1,0:T(8,128)(2,1)S(1)} %load.1.a_ref, bf16[256,256]{1,0:T(8,128)(2,1)S(1)} %copy-done, ...), custom_call_target="tpu_custom_call", output_to_operand_aliasing={{1}: (6, {})} | custom-call | flops 4294967296 | bytes 8388608 | tf_op jit(solution)/shard_map/layer/pallas_call | solution.py:184
  56.3 1.9 %collective-permute-done.18.te = f32[264,128]{1,0:T(8,128)S(1)} collective-permute-done((f32[264,128]{1,0:T(8,128)S(1)}, f32[264,128]{1,0:T(8,128)S(1)}, u32[]{:S(2)}, u32[]{:S(2)}) %collective-permute-start.18) | collective-permute-done | bytes 135200 | tf_op jit(solution)/shard_map/ppermute | solution.py:66
  60.2 1.5 %collective-permute-start.21 = (bf16[2320,128]{1,0:T(8,128)(2,1)S(1)}, bf16[2320,128]{1,0:T(8,128)(2,1)S(1)}, u32[]{:S(2)}, u32[]{:S(2)}) collective-permute-start(bf16[2320,128]{1,0:T(8,128)(2,1)S(1)} %get-tuple-element.60), channel_id=1, source_target_pairs={{0,24},{1,7},{2,26},{3,1},{4,28},{5,3},{6,30},{7,5},{8,0},{9,15},{... | collective-permute-start | bytes 1781768 | tf_op jit(solution)/shard_map/ppermute | solution.py:54
  62.7 7.2 %collective-permute-done.22.far = bf16[272,128]{1,0:T(8,128)(2,1)S(1)} collective-permute-done((bf16[272,128]{1,0:T(8,128)(2,1)S(1)}, bf16[272,128]{1,0:T(8,128)(2,1)S(1)}, u32[]{:S(2)}, u32[]{:S(2)}) %collective-permute-start.22) | collective-permute-done | bytes 69664 | tf_op jit(solution)/shard_map/ppermute | solution.py:54
  70.5 2.0 %collective-permute-start.23 = (bf16[4096,128]{1,0:T(8,128)(2,1)S(1)}, bf16[4096,128]{1,0:T(8,128)(2,1)S(1)}, u32[]{:S(2)}, u32[]{:S(2)}) collective-permute-start(bf16[4096,128]{1,0:T(8,128)(2,1)S(1)} %get-tuple-element.66), channel_id=1, source_target_pairs={{0,1},{1,0},{2,3},{3,2},{4,5},{5,4},{6,7},{7,6},{8,9},{9,8},{10,11... | collective-permute-start | bytes 3145736 | tf_op jit(solution)/shard_map/ppermute | solution.py:66
  73.7 1.5 %collective-permute-start.25 = (bf16[4096,128]{1,0:T(8,128)(2,1)S(1)}, bf16[4096,128]{1,0:T(8,128)(2,1)S(1)}, u32[]{:S(2)}, u32[]{:S(2)}) collective-permute-start(bf16[4096,128]{1,0:T(8,128)(2,1)S(1)} %get-tuple-element.68), channel_id=1, source_target_pairs={{0,24},{1,7},{2,26},{3,1},{4,28},{5,3},{6,30},{7,5},{8,0},{9,15},{... | collective-permute-start | bytes 3145736 | tf_op jit(solution)/shard_map/ppermute | solution.py:54
  75.2 13.1 %all_to_all.5.got = f32[16,24,128]{2,1,0:T(8,128)S(1)} all-to-all(f32[16,24,128]{2,1,0:T(8,128)S(1)} %extra_pieces.1._pieces), channel_id=1, replica_groups={{1,9,17,25,33,41,49,57,65,73,81,89,97,105,113,121},{3,11,19,27,35,43,51..., dimensions={0} | all-to-all | bytes 393216 | tf_op jit(solution)/shard_map/all_to_all | solution.py:40
  89.4 1.8 %collective-permute-start.26 = (bf16[1056,128]{1,0:T(8,128)(2,1)S(1)}, bf16[1056,128]{1,0:T(8,128)(2,1)S(1)}, u32[]{:S(2)}, u32[]{:S(2)}) collective-permute-start(bf16[1056,128]{1,0:T(8,128)(2,1)S(1)} %get-tuple-element.72), channel_id=1, source_target_pairs={{0,4},{1,65},{2,6},{3,67},{4,0},{5,69},{6,2},{7,71},{8,12},{9,73},... | collective-permute-start | bytes 811016 | tf_op jit(solution)/shard_map/ppermute | solution.py:54
  91.5 2.3 %collective-permute-start.28 = (bf16[1056,128]{1,0:T(8,128)(2,1)S(1)}, bf16[1056,128]{1,0:T(8,128)(2,1)S(1)}, u32[]{:S(2)}, u32[]{:S(2)}) collective-permute-start(bf16[1056,128]{1,0:T(8,128)(2,1)S(1)} %get-tuple-element.74), channel_id=1, source_target_pairs={{0,6},{1,97},{2,0},{3,99},{4,2},{5,101},{6,4},{7,103},{8,14},{9,10... | collective-permute-start | bytes 811016 | tf_op jit(solution)/shard_map/ppermute | solution.py:54
  93.8 2.7 %collective-permute-done.26.g2 = bf16[1056,128]{1,0:T(8,128)(2,1)S(1)} collective-permute-done((bf16[1056,128]{1,0:T(8,128)(2,1)S(1)}, bf16[1056,128]{1,0:T(8,128)(2,1)S(1)}, u32[]{:S(2)}, u32[]{:S(2)}) %collective-permute-start.26) | collective-permute-done | bytes 270368 | tf_op jit(solution)/shard_map/ppermute | solution.py:54
  96.6 2.9 %collective-permute-done.27.g1 = bf16[1056,128]{1,0:T(8,128)(2,1)S(1)} collective-permute-done((bf16[1056,128]{1,0:T(8,128)(2,1)S(1)}, bf16[1056,128]{1,0:T(8,128)(2,1)S(1)}, u32[]{:S(2)}, u32[]{:S(2)}) %collective-permute-start.27) | collective-permute-done | bytes 270368 | tf_op jit(solution)/shard_map/ppermute | solution.py:54
  100.6 1.9 %collective-permute-start.30 = (bf16[384,128]{1,0:T(8,128)(2,1)S(1)}, bf16[384,128]{1,0:T(8,128)(2,1)S(1)}, u32[]{:S(2)}, u32[]{:S(2)}) collective-permute-start(bf16[384,128]{1,0:T(8,128)(2,1)S(1)} %get-tuple-element.77), channel_id=1, source_target_pairs={{0,32},{1,9},{2,34},{3,11},{4,36},{5,13},{6,38},{7,15},{8,40},{9,1... | collective-permute-start | bytes 294920 | tf_op jit(solution)/shard_map/ppermute | solution.py:54
  103.3 1.4 %collective-permute-done.29.h2 = bf16[384,128]{1,0:T(8,128)(2,1)S(1)} collective-permute-done((bf16[384,128]{1,0:T(8,128)(2,1)S(1)}, bf16[384,128]{1,0:T(8,128)(2,1)S(1)}, u32[]{:S(2)}, u32[]{:S(2)}) %collective-permute-start.29) | collective-permute-done | bytes 98336 | tf_op jit(solution)/shard_map/ppermute | solution.py:54
  106.0 3.6 %collective-permute-start.32 = (f32[264,128]{1,0:T(8,128)S(1)}, f32[264,128]{1,0:T(8,128)S(1)}, u32[]{:S(2)}, u32[]{:S(2)}) collective-permute-start(f32[264,128]{1,0:T(8,128)S(1)} %extra_half.1.own), channel_id=1, source_target_pairs={{0,1},{1,0},{2,3},{3,2},{4,5},{5,4},{6,7},{7,6},{8,9},{9,8},{10,11... | collective-permute-start | bytes 405512 | tf_op jit(solution)/shard_map/ppermute | solution.py:66
  (65 shorter events, 17.3 us)
Async XLA Ops:
  0.6 8.7 %collective-permute-start.2 = (bf16[1,128,256]{2,1,0:T(8,128)(2,1)}, bf16[1,128,256]{2,1,0:T(8,128)(2,1)S(1)}, u32[]{:S(2)}, u32[]{:S(2)}) collective-permute-start(bf16[1,128,256]{2,1,0:T(8,128)(2,1)} %bitcast.10), channel_id=1, source_target_pairs={{0,32},{1,9},{2,34},{3,11},{4,36},{5,13},{6,38},{7,15},{8,40},{9,1... | collective-permute-start | bytes 196616 | tf_op jit(solution)/shard_map/ppermute | solution.py:54
  2.7 6.6 %collective-permute-start.1 = (bf16[1,128,256]{2,1,0:T(8,128)(2,1)}, bf16[1,128,256]{2,1,0:T(8,128)(2,1)S(1)}, u32[]{:S(2)}, u32[]{:S(2)}) collective-permute-start(bf16[1,128,256]{2,1,0:T(8,128)(2,1)} %bitcast.11), channel_id=1, source_target_pairs={{0,96},{1,25},{2,98},{3,27},{4,100},{5,29},{6,102},{7,31},{8,104},... | collective-permute-start | bytes 196616 | tf_op jit(solution)/shard_map/ppermute | solution.py:54
  4.1 5.3 %collective-permute-start = (bf16[1,128,256]{2,1,0:T(8,128)(2,1)}, bf16[1,128,256]{2,1,0:T(8,128)(2,1)S(1)}, u32[]{:S(2)}, u32[]{:S(2)}) collective-permute-start(bf16[1,128,256]{2,1,0:T(8,128)(2,1)} %bitcast.12), channel_id=1, source_target_pairs={{0,64},{1,17},{2,66},{3,19},{4,68},{5,21},{6,70},{7,23},{8,72},{9,... | collective-permute-start | bytes 196616 | tf_op jit(solution)/shard_map/ppermute | solution.py:54
  9.4 6.6 %collective-permute-start.5 = (bf16[4,128,256]{2,1,0:T(8,128)(2,1)S(1)}, bf16[4,128,256]{2,1,0:T(8,128)(2,1)S(1)}, u32[]{:S(2)}, u32[]{:S(2)}) collective-permute-start(bf16[4,128,256]{2,1,0:T(8,128)(2,1)S(1)} %join.4.refs_0_._after), channel_id=1, source_target_pairs={{0,2},{1,33},{2,4},{3,35},{4,6},{5,37},{6,0},{7,39},{8,10},{9,41},... | collective-permute-start | bytes 786440 | tf_op jit(solution)/shard_map/ppermute | solution.py:54
  10.8 7.6 %collective-permute-start.4 = (bf16[4,128,256]{2,1,0:T(8,128)(2,1)S(1)}, bf16[4,128,256]{2,1,0:T(8,128)(2,1)S(1)}, u32[]{:S(2)}, u32[]{:S(2)}) collective-permute-start(bf16[4,128,256]{2,1,0:T(8,128)(2,1)S(1)} %join.4.refs_0_._after), channel_id=1, source_target_pairs={{0,6},{1,97},{2,0},{3,99},{4,2},{5,101},{6,4},{7,103},{8,14},{9,10... | collective-permute-start | bytes 786440 | tf_op jit(solution)/shard_map/ppermute | solution.py:54
  12.3 7.7 %collective-permute-start.3 = (bf16[4,128,256]{2,1,0:T(8,128)(2,1)S(1)}, bf16[4,128,256]{2,1,0:T(8,128)(2,1)S(1)}, u32[]{:S(2)}, u32[]{:S(2)}) collective-permute-start(bf16[4,128,256]{2,1,0:T(8,128)(2,1)S(1)} %join.4.refs_0_._after), channel_id=1, source_target_pairs={{0,4},{1,65},{2,6},{3,67},{4,0},{5,69},{6,2},{7,71},{8,12},{9,73},... | collective-permute-start | bytes 786440 | tf_op jit(solution)/shard_map/ppermute | solution.py:54
  20.1 11.0 %collective-permute-start.6 = (bf16[8,128,256]{2,1,0:T(8,128)(2,1)S(1)}, bf16[8,128,256]{2,1,0:T(8,128)(2,1)S(1)}, u32[]{:S(2)}, u32[]{:S(2)}) collective-permute-start(bf16[8,128,256]{2,1,0:T(8,128)(2,1)S(1)} %get-tuple-element.47), channel_id=1, source_target_pairs={{0,8},{1,3},{2,10},{3,5},{4,12},{5,7},{6,14},{7,1},{8,16},{9,11},{... | collective-permute-start | bytes 1572872 | tf_op jit(solution)/shard_map/ppermute | solution.py:54
  21.8 9.3 %collective-permute-start.7 = (bf16[8,128,256]{2,1,0:T(8,128)(2,1)S(1)}, bf16[8,128,256]{2,1,0:T(8,128)(2,1)S(1)}, u32[]{:S(2)}, u32[]{:S(2)}) collective-permute-start(bf16[8,128,256]{2,1,0:T(8,128)(2,1)S(1)} %get-tuple-element.48), channel_id=1, source_target_pairs={{0,24},{1,7},{2,26},{3,1},{4,28},{5,3},{6,30},{7,5},{8,0},{9,15},{... | collective-permute-start | bytes 1572872 | tf_op jit(solution)/shard_map/ppermute | solution.py:54
  24.3 14.1 %collective-permute-start.9 = (bf16[8,128,256]{2,1,0:T(8,128)(2,1)S(1)}, bf16[8,128,256]{2,1,0:T(8,128)(2,1)S(1)}, u32[]{:S(2)}, u32[]{:S(2)}) collective-permute-start(bf16[8,128,256]{2,1,0:T(8,128)(2,1)S(1)} %get-tuple-element.47), channel_id=1, source_target_pairs={{0,24},{1,7},{2,26},{3,1},{4,28},{5,3},{6,30},{7,5},{8,0},{9,15},{... | collective-permute-start | bytes 1572872 | tf_op jit(solution)/shard_map/ppermute | solution.py:54
  25.7 15.0 %collective-permute-start.8 = (bf16[8,128,256]{2,1,0:T(8,128)(2,1)S(1)}, bf16[8,128,256]{2,1,0:T(8,128)(2,1)S(1)}, u32[]{:S(2)}, u32[]{:S(2)}) collective-permute-start(bf16[8,128,256]{2,1,0:T(8,128)(2,1)S(1)} %get-tuple-element.48), channel_id=1, source_target_pairs={{0,8},{1,3},{2,10},{3,5},{4,12},{5,7},{6,14},{7,1},{8,16},{9,11},{... | collective-permute-start | bytes 1572872 | tf_op jit(solution)/shard_map/ppermute | solution.py:54
  31.1 11.2 %collective-permute-start.10 = (bf16[8,128,256]{2,1,0:T(8,128)(2,1)S(1)}, bf16[8,128,256]{2,1,0:T(8,128)(2,1)S(1)}, u32[]{:S(2)}, u32[]{:S(2)}) collective-permute-start(bf16[8,128,256]{2,1,0:T(8,128)(2,1)S(1)} %collective-permute-done.6.refs_0_), channel_id=1, source_target_pairs={{0,8},{1,3},{2,10},{3,5},{4,12},{5,7},{6,14},{7,1},{8,16},{9,11},{... | collective-permute-start | bytes 1572872 | tf_op jit(solution)/shard_map/ppermute | solution.py:54
  32.0 14.1 %collective-permute-start.11 = (bf16[8,128,256]{2,1,0:T(8,128)(2,1)S(1)}, bf16[8,128,256]{2,1,0:T(8,128)(2,1)S(1)}, u32[]{:S(2)}, u32[]{:S(2)}) collective-permute-start(bf16[8,128,256]{2,1,0:T(8,128)(2,1)S(1)} %collective-permute-done.7.refs_1_), channel_id=1, source_target_pairs={{0,24},{1,7},{2,26},{3,1},{4,28},{5,3},{6,30},{7,5},{8,0},{9,15},{... | collective-permute-start | bytes 1572872 | tf_op jit(solution)/shard_map/ppermute | solution.py:54
  33.9 14.4 %collective-permute-start.13 = (bf16[16,128,256]{2,1,0:T(8,128)(2,1)S(1)}, bf16[16,128,256]{2,1,0:T(8,128)(2,1)S(1)}, u32[]{:S(2)}, u32[]{:S(2)}) collective-permute-start(bf16[16,128,256]{2,1,0:T(8,128)(2,1)S(1)} %join.6.rest_1_), channel_id=1, source_target_pairs={{0,1},{1,0},{2,3},{3,2},{4,5},{5,4},{6,7},{7,6},{8,9},{9,8},{10,11... | collective-permute-start | bytes 3145736 | tf_op jit(solution)/shard_map/ppermute | solution.py:66
  38.5 9.9 %collective-permute-start.12 = (bf16[16,128,256]{2,1,0:T(8,128)(2,1)S(1)}, bf16[16,128,256]{2,1,0:T(8,128)(2,1)S(1)}, u32[]{:S(2)}, u32[]{:S(2)}) collective-permute-start(bf16[16,128,256]{2,1,0:T(8,128)(2,1)S(1)} %join.5.x.rest_0_), channel_id=1, source_target_pairs={{0,1},{1,0},{2,3},{3,2},{4,5},{5,4},{6,7},{7,6},{8,9},{9,8},{10,11... | collective-permute-start | bytes 3145736 | tf_op jit(solution)/shard_map/ppermute | solution.py:66
  40.8 7.6 %collective-permute-start.14 = (bf16[16,128,256]{2,1,0:T(8,128)(2,1)S(1)}, bf16[16,128,256]{2,1,0:T(8,128)(2,1)S(1)}, u32[]{:S(2)}, u32[]{:S(2)}) collective-permute-start(bf16[16,128,256]{2,1,0:T(8,128)(2,1)S(1)} %join.7.rest_2_), channel_id=1, source_target_pairs={{0,1},{1,0},{2,3},{3,2},{4,5},{5,4},{6,7},{7,6},{8,9},{9,8},{10,11... | collective-permute-start | bytes 3145736 | tf_op jit(solution)/shard_map/ppermute | solution.py:66
  42.3 5.2 %collective-permute-start.15 = (bf16[8,128,256]{2,1,0:T(8,128)(2,1)S(1)}, bf16[8,128,256]{2,1,0:T(8,128)(2,1)S(1)}, u32[]{:S(2)}, u32[]{:S(2)}) collective-permute-start(bf16[8,128,256]{2,1,0:T(8,128)(2,1)S(1)} %collective-permute-done.10.rest_3_), channel_id=1, source_target_pairs={{0,1},{1,0},{2,3},{3,2},{4,5},{5,4},{6,7},{7,6},{8,9},{9,8},{10,11... | collective-permute-start | bytes 1572872 | tf_op jit(solution)/shard_map/ppermute | solution.py:66
  55.3 2.9 %collective-permute-start.17 = (bf16[4096,128]{1,0:T(8,128)(2,1)S(1)}, bf16[4096,128]{1,0:T(8,128)(2,1)S(1)}, u32[]{:S(2)}, u32[]{:S(2)}) collective-permute-start(bf16[4096,128]{1,0:T(8,128)(2,1)S(1)} %get-tuple-element.83), channel_id=1, source_target_pairs={{0,1},{1,0},{2,3},{3,2},{4,5},{5,4},{6,7},{7,6},{8,9},{9,8},{10,11... | collective-permute-start | bytes 3145736 | tf_op jit(solution)/shard_map/ppermute | solution.py:66
  55.8 2.5 %collective-permute-start.18 = (f32[264,128]{1,0:T(8,128)S(1)}, f32[264,128]{1,0:T(8,128)S(1)}, u32[]{:S(2)}, u32[]{:S(2)}) collective-permute-start(f32[264,128]{1,0:T(8,128)S(1)} %slice_bitcast_fusion.2), channel_id=1, source_target_pairs={{0,1},{1,0},{2,3},{3,2},{4,5},{5,4},{6,7},{7,6},{8,9},{9,8},{10,11... | collective-permute-start | bytes 405512 | tf_op jit(solution)/shard_map/ppermute | solution.py:66
  58.6 11.3 %collective-permute-start.19 = (bf16[2,4096,128]{2,1,0:T(8,128)(2,1)S(1)}, bf16[2,4096,128]{2,1,0:T(8,128)(2,1)S(1)}, u32[]{:S(2)}, u32[]{:S(2)}) collective-permute-start(bf16[2,4096,128]{2,1,0:T(8,128)(2,1)S(1)} %slice.14), channel_id=1, source_target_pairs={{0,1},{1,0},{2,3},{3,2},{4,5},{5,4},{6,7},{7,6},{8,9},{9,8},{10,11... | collective-permute-start | bytes 6291464 | tf_op jit(solution)/shard_map/ppermute | solution.py:66
  59.0 10.8 %collective-permute-start.20 = (bf16[2320,128]{1,0:T(8,128)(2,1)S(1)}, bf16[2320,128]{1,0:T(8,128)(2,1)S(1)}, u32[]{:S(2)}, u32[]{:S(2)}) collective-permute-start(bf16[2320,128]{1,0:T(8,128)(2,1)S(1)} %get-tuple-element.59), channel_id=1, source_target_pairs={{0,8},{1,3},{2,10},{3,5},{4,12},{5,7},{6,14},{7,1},{8,16},{9,11},{... | collective-permute-start | bytes 1781768 | tf_op jit(solution)/shard_map/ppermute | solution.py:54
  60.2 9.7 %collective-permute-start.21 = (bf16[2320,128]{1,0:T(8,128)(2,1)S(1)}, bf16[2320,128]{1,0:T(8,128)(2,1)S(1)}, u32[]{:S(2)}, u32[]{:S(2)}) collective-permute-start(bf16[2320,128]{1,0:T(8,128)(2,1)S(1)} %get-tuple-element.60), channel_id=1, source_target_pairs={{0,24},{1,7},{2,26},{3,1},{4,28},{5,3},{6,30},{7,5},{8,0},{9,15},{... | collective-permute-start | bytes 1781768 | tf_op jit(solution)/shard_map/ppermute | solution.py:54
  61.7 8.1 %collective-permute-start.22 = (bf16[272,128]{1,0:T(8,128)(2,1)S(1)}, bf16[272,128]{1,0:T(8,128)(2,1)S(1)}, u32[]{:S(2)}, u32[]{:S(2)}) collective-permute-start(bf16[272,128]{1,0:T(8,128)(2,1)S(1)} %get-tuple-element.61), channel_id=1, source_target_pairs={{0,16},{1,5},{2,18},{3,7},{4,20},{5,1},{6,22},{7,3},{8,24},{9,13},... | collective-permute-start | bytes 208904 | tf_op jit(solution)/shard_map/ppermute | solution.py:54
  70.5 17.8 %collective-permute-start.23 = (bf16[4096,128]{1,0:T(8,128)(2,1)S(1)}, bf16[4096,128]{1,0:T(8,128)(2,1)S(1)}, u32[]{:S(2)}, u32[]{:S(2)}) collective-permute-start(bf16[4096,128]{1,0:T(8,128)(2,1)S(1)} %get-tuple-element.66), channel_id=1, source_target_pairs={{0,1},{1,0},{2,3},{3,2},{4,5},{5,4},{6,7},{7,6},{8,9},{9,8},{10,11... | collective-permute-start | bytes 3145736 | tf_op jit(solution)/shard_map/ppermute | solution.py:66
  72.5 16.2 %collective-permute-start.24 = (bf16[4096,128]{1,0:T(8,128)(2,1)S(1)}, bf16[4096,128]{1,0:T(8,128)(2,1)S(1)}, u32[]{:S(2)}, u32[]{:S(2)}) collective-permute-start(bf16[4096,128]{1,0:T(8,128)(2,1)S(1)} %get-tuple-element.67), channel_id=1, source_target_pairs={{0,8},{1,3},{2,10},{3,5},{4,12},{5,7},{6,14},{7,1},{8,16},{9,11},{... | collective-permute-start | bytes 3145736 | tf_op jit(solution)/shard_map/ppermute | solution.py:54
  73.7 15.1 %collective-permute-start.25 = (bf16[4096,128]{1,0:T(8,128)(2,1)S(1)}, bf16[4096,128]{1,0:T(8,128)(2,1)S(1)}, u32[]{:S(2)}, u32[]{:S(2)}) collective-permute-start(bf16[4096,128]{1,0:T(8,128)(2,1)S(1)} %get-tuple-element.68), channel_id=1, source_target_pairs={{0,24},{1,7},{2,26},{3,1},{4,28},{5,3},{6,30},{7,5},{8,0},{9,15},{... | collective-permute-start | bytes 3145736 | tf_op jit(solution)/shard_map/ppermute | solution.py:54
  89.4 7.2 %collective-permute-start.26 = (bf16[1056,128]{1,0:T(8,128)(2,1)S(1)}, bf16[1056,128]{1,0:T(8,128)(2,1)S(1)}, u32[]{:S(2)}, u32[]{:S(2)}) collective-permute-start(bf16[1056,128]{1,0:T(8,128)(2,1)S(1)} %get-tuple-element.72), channel_id=1, source_target_pairs={{0,4},{1,65},{2,6},{3,67},{4,0},{5,69},{6,2},{7,71},{8,12},{9,73},... | collective-permute-start | bytes 811016 | tf_op jit(solution)/shard_map/ppermute | solution.py:54
  91.1 8.3 %collective-permute-start.27 = (bf16[1056,128]{1,0:T(8,128)(2,1)S(1)}, bf16[1056,128]{1,0:T(8,128)(2,1)S(1)}, u32[]{:S(2)}, u32[]{:S(2)}) collective-permute-start(bf16[1056,128]{1,0:T(8,128)(2,1)S(1)} %get-tuple-element.73), channel_id=1, source_target_pairs={{0,2},{1,33},{2,4},{3,35},{4,6},{5,37},{6,0},{7,39},{8,10},{9,41},... | collective-permute-start | bytes 811016 | tf_op jit(solution)/shard_map/ppermute | solution.py:54
  91.5 7.9 %collective-permute-start.28 = (bf16[1056,128]{1,0:T(8,128)(2,1)S(1)}, bf16[1056,128]{1,0:T(8,128)(2,1)S(1)}, u32[]{:S(2)}, u32[]{:S(2)}) collective-permute-start(bf16[1056,128]{1,0:T(8,128)(2,1)S(1)} %get-tuple-element.74), channel_id=1, source_target_pairs={{0,6},{1,97},{2,0},{3,99},{4,2},{5,101},{6,4},{7,103},{8,14},{9,10... | collective-permute-start | bytes 811016 | tf_op jit(solution)/shard_map/ppermute | solution.py:54
  99.6 5.1 %collective-permute-start.29 = (bf16[384,128]{1,0:T(8,128)(2,1)S(1)}, bf16[384,128]{1,0:T(8,128)(2,1)S(1)}, u32[]{:S(2)}, u32[]{:S(2)}) collective-permute-start(bf16[384,128]{1,0:T(8,128)(2,1)S(1)} %get-tuple-element.76), channel_id=1, source_target_pairs={{0,64},{1,17},{2,66},{3,19},{4,68},{5,21},{6,70},{7,23},{8,72},{9,... | collective-permute-start | bytes 294920 | tf_op jit(solution)/shard_map/ppermute | solution.py:54
  100.6 5.1 %collective-permute-start.30 = (bf16[384,128]{1,0:T(8,128)(2,1)S(1)}, bf16[384,128]{1,0:T(8,128)(2,1)S(1)}, u32[]{:S(2)}, u32[]{:S(2)}) collective-permute-start(bf16[384,128]{1,0:T(8,128)(2,1)S(1)} %get-tuple-element.77), channel_id=1, source_target_pairs={{0,32},{1,9},{2,34},{3,11},{4,36},{5,13},{6,38},{7,15},{8,40},{9,1... | collective-permute-start | bytes 294920 | tf_op jit(solution)/shard_map/ppermute | solution.py:54
  102.5 3.5 %collective-permute-start.31 = (bf16[384,128]{1,0:T(8,128)(2,1)S(1)}, bf16[384,128]{1,0:T(8,128)(2,1)S(1)}, u32[]{:S(2)}, u32[]{:S(2)}) collective-permute-start(bf16[384,128]{1,0:T(8,128)(2,1)S(1)} %get-tuple-element.78), channel_id=1, source_target_pairs={{0,96},{1,25},{2,98},{3,27},{4,100},{5,29},{6,102},{7,31},{8,104},... | collective-permute-start | bytes 294920 | tf_op jit(solution)/shard_map/ppermute | solution.py:54
  106.0 4.6 %collective-permute-start.32 = (f32[264,128]{1,0:T(8,128)S(1)}, f32[264,128]{1,0:T(8,128)S(1)}, u32[]{:S(2)}, u32[]{:S(2)}) collective-permute-start(f32[264,128]{1,0:T(8,128)S(1)} %extra_half.1.own), channel_id=1, source_target_pairs={{0,1},{1,0},{2,3},{3,2},{4,5},{5,4},{6,7},{7,6},{8,9},{9,8},{10,11... | collective-permute-start | bytes 405512 | tf_op jit(solution)/shard_map/ppermute | solution.py:66
  (6 other events, 162.0 us)

commit v6 on v5

--- a/solution.py
+++ b/solution.py
@@ -270,7 +270,8 @@
 def extra_pieces(e, te, via1, via3, far, o):
     total = e[0] + te[...]
     dw = total[:256] + widened(via1[2048:2304], via3[2048:2304], far[:256])
-    db = total[256:] + widened(via1[2304:2312], via1[2312:], via3[2304:2312], via3[2312:], far[256:264], far[264:])
+    tail = widened(via1[2304:], via3[2304:], far[256:])
+    db = total[256:] + tail[:8] + tail[8:]
     for i in range(16):
         o[i, :DB] = dw[i * 16 : i * 16 + 16]
         o[i, DB:] = db
@@ -333,7 +334,8 @@
             place = jnp.where(flip, j * 4 + i, i * 4 + j)
             start = base + k2 * 32
             o[pl.ds(pl.multiple_of(place * 16, 16), 16)] = ref[start : start + DB].astype(F32)
-    o[256:] = widened(pieces[DB : DB + 8], pieces[DB + 8 : DB + 16])
+    tail = pieces[DB : DB + 16].astype(F32)
+    o[256:] = tail[:8] + tail[8:]
 
 
 def extra_both(core, own, other, dw, db):

time: 111 us -> 111 us (level)
  no operation moved by 1% of the time
where the time goes in v6:
time: 111 us
  starting transfers between devices  49.5 us (45%)
  waiting for transfers between devices  31.1 us (28%)
  Pallas kernels  15.8 us (14%)
  blocking collectives  13.1 us (12%)
  between operations  1.53 us (1%)
    ppermute x23, starting transfers between devices, hop(): return lax.ppermute(x, AXIS, pairs(move))  31.7 us
    ppermute x23, waiting for transfers between devices, hop(): return lax.ppermute(x, AXIS, pairs(move))  27.7 us
    ppermute x10, starting transfers between devices, swap(): return lax.ppermute(x, AXIS, pairs(move))  17.7 us
    all_to_all x1, blocking collectives, exchange(): lax.all_to_all(x, AXIS, split_axis=0, concat_axis=0, tiled=True, axis_ind...  13.1 us
    pallas_call x1, Pallas kernels, local(): pl.pallas_call(kernel, out_shape=(pltpu.VMEM((512, 256), BF16), pltpu.VME...  6.83 us
    pallas_call x13, Pallas kernels, in_vmem(): pl.pallas_call(body, out_shape=tuple((o if last else pltpu.VMEM(o.shape,...  3.98 us
    pallas_call x1, Pallas kernels, load(): pl.pallas_call(load_kernel, out_shape=pltpu.VMEM((512, 8192), BF16), in_s...  3.54 us
    ppermute x10, waiting for transfers between devices, swap(): return lax.ppermute(x, AXIS, pairs(move))  3.4 us
  transfers between devices with their start and end apart: 33, of which 16 were waited for; matrix products, arithmetic and copies ran while one was open for 0% of the time, Pallas kernels for 6%

profile of v6, /device:TPU:1, one launch (start us, length us, event | category | flops | bytes accessed | tf_op | source)
XLA Modules:
  0.0 111.3 jit_solution(5535017960428141860)
XLA Ops:
  0.6 2.1 %collective-permute-start.2 = (bf16[1,128,256]{2,1,0:T(8,128)(2,1)}, bf16[1,128,256]{2,1,0:T(8,128)(2,1)S(1)}, u32[]{:S(2)}, u32[]{:S(2)}) collective-permute-start(bf16[1,128,256]{2,1,0:T(8,128)(2,1)} %bitcast.10), channel_id=1, source_target_pairs={{0,32},{1,9},{2,34},{3,11},{4,36},{5,13},{6,38},{7,15},{8,40},{9,1... | collective-permute-start | bytes 196616 | tf_op jit(solution)/shard_map/ppermute | solution.py:54
  2.7 1.3 %collective-permute-start.1 = (bf16[1,128,256]{2,1,0:T(8,128)(2,1)}, bf16[1,128,256]{2,1,0:T(8,128)(2,1)S(1)}, u32[]{:S(2)}, u32[]{:S(2)}) collective-permute-start(bf16[1,128,256]{2,1,0:T(8,128)(2,1)} %bitcast.11), channel_id=1, source_target_pairs={{0,96},{1,25},{2,98},{3,27},{4,100},{5,29},{6,102},{7,31},{8,104},... | collective-permute-start | bytes 196616 | tf_op jit(solution)/shard_map/ppermute | solution.py:54
  4.1 1.6 %collective-permute-start = (bf16[1,128,256]{2,1,0:T(8,128)(2,1)}, bf16[1,128,256]{2,1,0:T(8,128)(2,1)S(1)}, u32[]{:S(2)}, u32[]{:S(2)}) collective-permute-start(bf16[1,128,256]{2,1,0:T(8,128)(2,1)} %bitcast.12), channel_id=1, source_target_pairs={{0,64},{1,17},{2,66},{3,19},{4,68},{5,21},{6,70},{7,23},{8,72},{9,... | collective-permute-start | bytes 196616 | tf_op jit(solution)/shard_map/ppermute | solution.py:54
  5.7 3.5 %load.1.a_ref = bf16[512,8192]{1,0:T(8,128)(2,1)S(1)} custom-call(bf16[16,512,512]{2,1,0:T(8,128)(2,1)} %bitcast.15), custom_call_target="tpu_custom_call" | custom-call | bytes 16777216 | tf_op jit(solution)/shard_map/load/pallas_call | solution.py:85
  9.4 1.4 %collective-permute-start.5 = (bf16[4,128,256]{2,1,0:T(8,128)(2,1)S(1)}, bf16[4,128,256]{2,1,0:T(8,128)(2,1)S(1)}, u32[]{:S(2)}, u32[]{:S(2)}) collective-permute-start(bf16[4,128,256]{2,1,0:T(8,128)(2,1)S(1)} %join.4.refs_0_._after), channel_id=1, source_target_pairs={{0,2},{1,33},{2,4},{3,35},{4,6},{5,37},{6,0},{7,39},{8,10},{9,41},... | collective-permute-start | bytes 786440 | tf_op jit(solution)/shard_map/ppermute | solution.py:54
  10.8 1.5 %collective-permute-start.4 = (bf16[4,128,256]{2,1,0:T(8,128)(2,1)S(1)}, bf16[4,128,256]{2,1,0:T(8,128)(2,1)S(1)}, u32[]{:S(2)}, u32[]{:S(2)}) collective-permute-start(bf16[4,128,256]{2,1,0:T(8,128)(2,1)S(1)} %join.4.refs_0_._after), channel_id=1, source_target_pairs={{0,6},{1,97},{2,0},{3,99},{4,2},{5,101},{6,4},{7,103},{8,14},{9,10... | collective-permute-start | bytes 786440 | tf_op jit(solution)/shard_map/ppermute | solution.py:54
  12.3 1.6 %collective-permute-start.3 = (bf16[4,128,256]{2,1,0:T(8,128)(2,1)S(1)}, bf16[4,128,256]{2,1,0:T(8,128)(2,1)S(1)}, u32[]{:S(2)}, u32[]{:S(2)}) collective-permute-start(bf16[4,128,256]{2,1,0:T(8,128)(2,1)S(1)} %join.4.refs_0_._after), channel_id=1, source_target_pairs={{0,4},{1,65},{2,6},{3,67},{4,0},{5,69},{6,2},{7,71},{8,12},{9,73},... | collective-permute-start | bytes 786440 | tf_op jit(solution)/shard_map/ppermute | solution.py:54
  16.0 2.4 %collective-permute-done.4.refs_2_ = bf16[4,128,256]{2,1,0:T(8,128)(2,1)S(1)} collective-permute-done((bf16[4,128,256]{2,1,0:T(8,128)(2,1)S(1)}, bf16[4,128,256]{2,1,0:T(8,128)(2,1)S(1)}, u32[]{:S(2)}, u32[]{:S(2)}) %collective-permute-start.4) | collective-permute-done | bytes 262176 | tf_op jit(solution)/shard_map/ppermute | solution.py:54
  18.4 1.5 %collective-permute-done.3.refs_1_ = bf16[4,128,256]{2,1,0:T(8,128)(2,1)S(1)} collective-permute-done((bf16[4,128,256]{2,1,0:T(8,128)(2,1)S(1)}, bf16[4,128,256]{2,1,0:T(8,128)(2,1)S(1)}, u32[]{:S(2)}, u32[]{:S(2)}) %collective-permute-start.3) | collective-permute-done | bytes 262176 | tf_op jit(solution)/shard_map/ppermute | solution.py:54
  20.1 1.7 %collective-permute-start.6 = (bf16[8,128,256]{2,1,0:T(8,128)(2,1)S(1)}, bf16[8,128,256]{2,1,0:T(8,128)(2,1)S(1)}, u32[]{:S(2)}, u32[]{:S(2)}) collective-permute-start(bf16[8,128,256]{2,1,0:T(8,128)(2,1)S(1)} %get-tuple-element.47), channel_id=1, source_target_pairs={{0,8},{1,3},{2,10},{3,5},{4,12},{5,7},{6,14},{7,1},{8,16},{9,11},{... | collective-permute-start | bytes 1572872 | tf_op jit(solution)/shard_map/ppermute | solution.py:54
  21.8 2.5 %collective-permute-start.7 = (bf16[8,128,256]{2,1,0:T(8,128)(2,1)S(1)}, bf16[8,128,256]{2,1,0:T(8,128)(2,1)S(1)}, u32[]{:S(2)}, u32[]{:S(2)}) collective-permute-start(bf16[8,128,256]{2,1,0:T(8,128)(2,1)S(1)} %get-tuple-element.48), channel_id=1, source_target_pairs={{0,24},{1,7},{2,26},{3,1},{4,28},{5,3},{6,30},{7,5},{8,0},{9,15},{... | collective-permute-start | bytes 1572872 | tf_op jit(solution)/shard_map/ppermute | solution.py:54
  24.3 1.4 %collective-permute-start.9 = (bf16[8,128,256]{2,1,0:T(8,128)(2,1)S(1)}, bf16[8,128,256]{2,1,0:T(8,128)(2,1)S(1)}, u32[]{:S(2)}, u32[]{:S(2)}) collective-permute-start(bf16[8,128,256]{2,1,0:T(8,128)(2,1)S(1)} %get-tuple-element.47), channel_id=1, source_target_pairs={{0,24},{1,7},{2,26},{3,1},{4,28},{5,3},{6,30},{7,5},{8,0},{9,15},{... | collective-permute-start | bytes 1572872 | tf_op jit(solution)/shard_map/ppermute | solution.py:54
  25.8 5.3 %collective-permute-done.6.refs_0_ = bf16[8,128,256]{2,1,0:T(8,128)(2,1)S(1)} collective-permute-done((bf16[8,128,256]{2,1,0:T(8,128)(2,1)S(1)}, bf16[8,128,256]{2,1,0:T(8,128)(2,1)S(1)}, u32[]{:S(2)}, u32[]{:S(2)}) %collective-permute-start.6) | collective-permute-done | bytes 524320 | tf_op jit(solution)/shard_map/ppermute | solution.py:54
  32.0 1.9 %collective-permute-start.11 = (bf16[8,128,256]{2,1,0:T(8,128)(2,1)S(1)}, bf16[8,128,256]{2,1,0:T(8,128)(2,1)S(1)}, u32[]{:S(2)}, u32[]{:S(2)}) collective-permute-start(bf16[8,128,256]{2,1,0:T(8,128)(2,1)S(1)} %collective-permute-done.7.refs_1_), channel_id=1, source_target_pairs={{0,24},{1,7},{2,26},{3,1},{4,28},{5,3},{6,30},{7,5},{8,0},{9,15},{... | collective-permute-start | bytes 1572872 | tf_op jit(solution)/shard_map/ppermute | solution.py:54
  33.9 4.5 %collective-permute-start.13 = (bf16[16,128,256]{2,1,0:T(8,128)(2,1)S(1)}, bf16[16,128,256]{2,1,0:T(8,128)(2,1)S(1)}, u32[]{:S(2)}, u32[]{:S(2)}) collective-permute-start(bf16[16,128,256]{2,1,0:T(8,128)(2,1)S(1)} %join.6.rest_1_), channel_id=1, source_target_pairs={{0,1},{1,0},{2,3},{3,2},{4,5},{5,4},{6,7},{7,6},{8,9},{9,8},{10,11... | collective-permute-start | bytes 3145736 | tf_op jit(solution)/shard_map/ppermute | solution.py:66
  38.5 2.2 %collective-permute-start.12 = (bf16[16,128,256]{2,1,0:T(8,128)(2,1)S(1)}, bf16[16,128,256]{2,1,0:T(8,128)(2,1)S(1)}, u32[]{:S(2)}, u32[]{:S(2)}) collective-permute-start(bf16[16,128,256]{2,1,0:T(8,128)(2,1)S(1)} %join.5.x.rest_0_), channel_id=1, source_target_pairs={{0,1},{1,0},{2,3},{3,2},{4,5},{5,4},{6,7},{7,6},{8,9},{9,8},{10,11... | collective-permute-start | bytes 3145736 | tf_op jit(solution)/shard_map/ppermute | solution.py:66
  40.9 1.5 %collective-permute-done.10.rest_3_ = bf16[8,128,256]{2,1,0:T(8,128)(2,1)S(1)} collective-permute-done((bf16[8,128,256]{2,1,0:T(8,128)(2,1)S(1)}, bf16[8,128,256]{2,1,0:T(8,128)(2,1)S(1)}, u32[]{:S(2)}, u32[]{:S(2)}) %collective-permute-start.10) | collective-permute-done | bytes 524320 | tf_op jit(solution)/shard_map/ppermute | solution.py:54
  42.3 3.7 %collective-permute-start.15 = (bf16[8,128,256]{2,1,0:T(8,128)(2,1)S(1)}, bf16[8,128,256]{2,1,0:T(8,128)(2,1)S(1)}, u32[]{:S(2)}, u32[]{:S(2)}) collective-permute-start(bf16[8,128,256]{2,1,0:T(8,128)(2,1)S(1)} %collective-permute-done.10.rest_3_), channel_id=1, source_target_pairs={{0,1},{1,0},{2,3},{3,2},{4,5},{5,4},{6,7},{7,6},{8,9},{9,8},{10,11... | collective-permute-start | bytes 1572872 | tf_op jit(solution)/shard_map/ppermute | solution.py:66
  48.4 6.8 %layer.1 = (bf16[512,256]{1,0:T(8,128)(2,1)S(1)}, bf16[8,4096,128]{2,1,0:T(8,128)(2,1)S(1)}, f32[2,264,128]{2,1,0:T(8,128)S(1)}) custom-call(s32[1,16]{1,0:T(1,128)S(1)} %copy-done.4, s32[1]{0:T(128)S(6)} %copy.13.count_ref, bf16[512,8192]{1,0:T(8,128)(2,1)S(1)} %load.1.a_ref, bf16[256,256]{1,0:T(8,128)(2,1)S(1)} %copy-done, ...), custom_call_target="tpu_custom_call", output_to_operand_aliasing={{1}: (6, {})} | custom-call | flops 4294967296 | bytes 8388608 | tf_op jit(solution)/shard_map/layer/pallas_call | solution.py:184
  56.3 1.9 %collective-permute-done.18.te = f32[264,128]{1,0:T(8,128)S(1)} collective-permute-done((f32[264,128]{1,0:T(8,128)S(1)}, f32[264,128]{1,0:T(8,128)S(1)}, u32[]{:S(2)}, u32[]{:S(2)}) %collective-permute-start.18) | collective-permute-done | bytes 135200 | tf_op jit(solution)/shard_map/ppermute | solution.py:66
  60.2 1.5 %collective-permute-start.21 = (bf16[2320,128]{1,0:T(8,128)(2,1)S(1)}, bf16[2320,128]{1,0:T(8,128)(2,1)S(1)}, u32[]{:S(2)}, u32[]{:S(2)}) collective-permute-start(bf16[2320,128]{1,0:T(8,128)(2,1)S(1)} %get-tuple-element.60), channel_id=1, source_target_pairs={{0,24},{1,7},{2,26},{3,1},{4,28},{5,3},{6,30},{7,5},{8,0},{9,15},{... | collective-permute-start | bytes 1781768 | tf_op jit(solution)/shard_map/ppermute | solution.py:54
  62.7 7.2 %collective-permute-done.22.far = bf16[272,128]{1,0:T(8,128)(2,1)S(1)} collective-permute-done((bf16[272,128]{1,0:T(8,128)(2,1)S(1)}, bf16[272,128]{1,0:T(8,128)(2,1)S(1)}, u32[]{:S(2)}, u32[]{:S(2)}) %collective-permute-start.22) | collective-permute-done | bytes 69664 | tf_op jit(solution)/shard_map/ppermute | solution.py:54
  70.5 2.0 %collective-permute-start.23 = (bf16[4096,128]{1,0:T(8,128)(2,1)S(1)}, bf16[4096,128]{1,0:T(8,128)(2,1)S(1)}, u32[]{:S(2)}, u32[]{:S(2)}) collective-permute-start(bf16[4096,128]{1,0:T(8,128)(2,1)S(1)} %get-tuple-element.66), channel_id=1, source_target_pairs={{0,1},{1,0},{2,3},{3,2},{4,5},{5,4},{6,7},{7,6},{8,9},{9,8},{10,11... | collective-permute-start | bytes 3145736 | tf_op jit(solution)/shard_map/ppermute | solution.py:66
  73.7 1.5 %collective-permute-start.25 = (bf16[4096,128]{1,0:T(8,128)(2,1)S(1)}, bf16[4096,128]{1,0:T(8,128)(2,1)S(1)}, u32[]{:S(2)}, u32[]{:S(2)}) collective-permute-start(bf16[4096,128]{1,0:T(8,128)(2,1)S(1)} %get-tuple-element.68), channel_id=1, source_target_pairs={{0,24},{1,7},{2,26},{3,1},{4,28},{5,3},{6,30},{7,5},{8,0},{9,15},{... | collective-permute-start | bytes 3145736 | tf_op jit(solution)/shard_map/ppermute | solution.py:54
  75.2 13.1 %all_to_all.5.got = f32[16,24,128]{2,1,0:T(8,128)S(1)} all-to-all(f32[16,24,128]{2,1,0:T(8,128)S(1)} %extra_pieces.1._pieces), channel_id=1, replica_groups={{1,9,17,25,33,41,49,57,65,73,81,89,97,105,113,121},{3,11,19,27,35,43,51..., dimensions={0} | all-to-all | bytes 393216 | tf_op jit(solution)/shard_map/all_to_all | solution.py:40
  89.4 1.8 %collective-permute-start.26 = (bf16[1056,128]{1,0:T(8,128)(2,1)S(1)}, bf16[1056,128]{1,0:T(8,128)(2,1)S(1)}, u32[]{:S(2)}, u32[]{:S(2)}) collective-permute-start(bf16[1056,128]{1,0:T(8,128)(2,1)S(1)} %get-tuple-element.72), channel_id=1, source_target_pairs={{0,4},{1,65},{2,6},{3,67},{4,0},{5,69},{6,2},{7,71},{8,12},{9,73},... | collective-permute-start | bytes 811016 | tf_op jit(solution)/shard_map/ppermute | solution.py:54
  91.5 2.3 %collective-permute-start.28 = (bf16[1056,128]{1,0:T(8,128)(2,1)S(1)}, bf16[1056,128]{1,0:T(8,128)(2,1)S(1)}, u32[]{:S(2)}, u32[]{:S(2)}) collective-permute-start(bf16[1056,128]{1,0:T(8,128)(2,1)S(1)} %get-tuple-element.74), channel_id=1, source_target_pairs={{0,6},{1,97},{2,0},{3,99},{4,2},{5,101},{6,4},{7,103},{8,14},{9,10... | collective-permute-start | bytes 811016 | tf_op jit(solution)/shard_map/ppermute | solution.py:54
  93.8 2.7 %collective-permute-done.26.g2 = bf16[1056,128]{1,0:T(8,128)(2,1)S(1)} collective-permute-done((bf16[1056,128]{1,0:T(8,128)(2,1)S(1)}, bf16[1056,128]{1,0:T(8,128)(2,1)S(1)}, u32[]{:S(2)}, u32[]{:S(2)}) %collective-permute-start.26) | collective-permute-done | bytes 270368 | tf_op jit(solution)/shard_map/ppermute | solution.py:54
  96.6 2.9 %collective-permute-done.27.g1 = bf16[1056,128]{1,0:T(8,128)(2,1)S(1)} collective-permute-done((bf16[1056,128]{1,0:T(8,128)(2,1)S(1)}, bf16[1056,128]{1,0:T(8,128)(2,1)S(1)}, u32[]{:S(2)}, u32[]{:S(2)}) %collective-permute-start.27) | collective-permute-done | bytes 270368 | tf_op jit(solution)/shard_map/ppermute | solution.py:54
  100.6 1.9 %collective-permute-start.30 = (bf16[384,128]{1,0:T(8,128)(2,1)S(1)}, bf16[384,128]{1,0:T(8,128)(2,1)S(1)}, u32[]{:S(2)}, u32[]{:S(2)}) collective-permute-start(bf16[384,128]{1,0:T(8,128)(2,1)S(1)} %get-tuple-element.77), channel_id=1, source_target_pairs={{0,32},{1,9},{2,34},{3,11},{4,36},{5,13},{6,38},{7,15},{8,40},{9,1... | collective-permute-start | bytes 294920 | tf_op jit(solution)/shard_map/ppermute | solution.py:54
  103.3 1.4 %collective-permute-done.29.h2 = bf16[384,128]{1,0:T(8,128)(2,1)S(1)} collective-permute-done((bf16[384,128]{1,0:T(8,128)(2,1)S(1)}, bf16[384,128]{1,0:T(8,128)(2,1)S(1)}, u32[]{:S(2)}, u32[]{:S(2)}) %collective-permute-start.29) | collective-permute-done | bytes 98336 | tf_op jit(solution)/shard_map/ppermute | solution.py:54
  106.0 3.6 %collective-permute-start.32 = (f32[264,128]{1,0:T(8,128)S(1)}, f32[264,128]{1,0:T(8,128)S(1)}, u32[]{:S(2)}, u32[]{:S(2)}) collective-permute-start(f32[264,128]{1,0:T(8,128)S(1)} %extra_half.1.own), channel_id=1, source_target_pairs={{0,1},{1,0},{2,3},{3,2},{4,5},{5,4},{6,7},{7,6},{8,9},{9,8},{10,11... | collective-permute-start | bytes 405512 | tf_op jit(solution)/shard_map/ppermute | solution.py:66
  (65 shorter events, 17.3 us)
Async XLA Ops:
  0.6 8.7 %collective-permute-start.2 = (bf16[1,128,256]{2,1,0:T(8,128)(2,1)}, bf16[1,128,256]{2,1,0:T(8,128)(2,1)S(1)}, u32[]{:S(2)}, u32[]{:S(2)}) collective-permute-start(bf16[1,128,256]{2,1,0:T(8,128)(2,1)} %bitcast.10), channel_id=1, source_target_pairs={{0,32},{1,9},{2,34},{3,11},{4,36},{5,13},{6,38},{7,15},{8,40},{9,1... | collective-permute-start | bytes 196616 | tf_op jit(solution)/shard_map/ppermute | solution.py:54
  2.7 6.6 %collective-permute-start.1 = (bf16[1,128,256]{2,1,0:T(8,128)(2,1)}, bf16[1,128,256]{2,1,0:T(8,128)(2,1)S(1)}, u32[]{:S(2)}, u32[]{:S(2)}) collective-permute-start(bf16[1,128,256]{2,1,0:T(8,128)(2,1)} %bitcast.11), channel_id=1, source_target_pairs={{0,96},{1,25},{2,98},{3,27},{4,100},{5,29},{6,102},{7,31},{8,104},... | collective-permute-start | bytes 196616 | tf_op jit(solution)/shard_map/ppermute | solution.py:54
  4.1 5.3 %collective-permute-start = (bf16[1,128,256]{2,1,0:T(8,128)(2,1)}, bf16[1,128,256]{2,1,0:T(8,128)(2,1)S(1)}, u32[]{:S(2)}, u32[]{:S(2)}) collective-permute-start(bf16[1,128,256]{2,1,0:T(8,128)(2,1)} %bitcast.12), channel_id=1, source_target_pairs={{0,64},{1,17},{2,66},{3,19},{4,68},{5,21},{6,70},{7,23},{8,72},{9,... | collective-permute-start | bytes 196616 | tf_op jit(solution)/shard_map/ppermute | solution.py:54
  9.4 6.6 %collective-permute-start.5 = (bf16[4,128,256]{2,1,0:T(8,128)(2,1)S(1)}, bf16[4,128,256]{2,1,0:T(8,128)(2,1)S(1)}, u32[]{:S(2)}, u32[]{:S(2)}) collective-permute-start(bf16[4,128,256]{2,1,0:T(8,128)(2,1)S(1)} %join.4.refs_0_._after), channel_id=1, source_target_pairs={{0,2},{1,33},{2,4},{3,35},{4,6},{5,37},{6,0},{7,39},{8,10},{9,41},... | collective-permute-start | bytes 786440 | tf_op jit(solution)/shard_map/ppermute | solution.py:54
  10.8 7.6 %collective-permute-start.4 = (bf16[4,128,256]{2,1,0:T(8,128)(2,1)S(1)}, bf16[4,128,256]{2,1,0:T(8,128)(2,1)S(1)}, u32[]{:S(2)}, u32[]{:S(2)}) collective-permute-start(bf16[4,128,256]{2,1,0:T(8,128)(2,1)S(1)} %join.4.refs_0_._after), channel_id=1, source_target_pairs={{0,6},{1,97},{2,0},{3,99},{4,2},{5,101},{6,4},{7,103},{8,14},{9,10... | collective-permute-start | bytes 786440 | tf_op jit(solution)/shard_map/ppermute | solution.py:54
  12.3 7.7 %collective-permute-start.3 = (bf16[4,128,256]{2,1,0:T(8,128)(2,1)S(1)}, bf16[4,128,256]{2,1,0:T(8,128)(2,1)S(1)}, u32[]{:S(2)}, u32[]{:S(2)}) collective-permute-start(bf16[4,128,256]{2,1,0:T(8,128)(2,1)S(1)} %join.4.refs_0_._after), channel_id=1, source_target_pairs={{0,4},{1,65},{2,6},{3,67},{4,0},{5,69},{6,2},{7,71},{8,12},{9,73},... | collective-permute-start | bytes 786440 | tf_op jit(solution)/shard_map/ppermute | solution.py:54
  20.1 11.0 %collective-permute-start.6 = (bf16[8,128,256]{2,1,0:T(8,128)(2,1)S(1)}, bf16[8,128,256]{2,1,0:T(8,128)(2,1)S(1)}, u32[]{:S(2)}, u32[]{:S(2)}) collective-permute-start(bf16[8,128,256]{2,1,0:T(8,128)(2,1)S(1)} %get-tuple-element.47), channel_id=1, source_target_pairs={{0,8},{1,3},{2,10},{3,5},{4,12},{5,7},{6,14},{7,1},{8,16},{9,11},{... | collective-permute-start | bytes 1572872 | tf_op jit(solution)/shard_map/ppermute | solution.py:54
  21.8 9.3 %collective-permute-start.7 = (bf16[8,128,256]{2,1,0:T(8,128)(2,1)S(1)}, bf16[8,128,256]{2,1,0:T(8,128)(2,1)S(1)}, u32[]{:S(2)}, u32[]{:S(2)}) collective-permute-start(bf16[8,128,256]{2,1,0:T(8,128)(2,1)S(1)} %get-tuple-element.48), channel_id=1, source_target_pairs={{0,24},{1,7},{2,26},{3,1},{4,28},{5,3},{6,30},{7,5},{8,0},{9,15},{... | collective-permute-start | bytes 1572872 | tf_op jit(solution)/shard_map/ppermute | solution.py:54
  24.3 14.1 %collective-permute-start.9 = (bf16[8,128,256]{2,1,0:T(8,128)(2,1)S(1)}, bf16[8,128,256]{2,1,0:T(8,128)(2,1)S(1)}, u32[]{:S(2)}, u32[]{:S(2)}) collective-permute-start(bf16[8,128,256]{2,1,0:T(8,128)(2,1)S(1)} %get-tuple-element.47), channel_id=1, source_target_pairs={{0,24},{1,7},{2,26},{3,1},{4,28},{5,3},{6,30},{7,5},{8,0},{9,15},{... | collective-permute-start | bytes 1572872 | tf_op jit(solution)/shard_map/ppermute | solution.py:54
  25.7 15.0 %collective-permute-start.8 = (bf16[8,128,256]{2,1,0:T(8,128)(2,1)S(1)}, bf16[8,128,256]{2,1,0:T(8,128)(2,1)S(1)}, u32[]{:S(2)}, u32[]{:S(2)}) collective-permute-start(bf16[8,128,256]{2,1,0:T(8,128)(2,1)S(1)} %get-tuple-element.48), channel_id=1, source_target_pairs={{0,8},{1,3},{2,10},{3,5},{4,12},{5,7},{6,14},{7,1},{8,16},{9,11},{... | collective-permute-start | bytes 1572872 | tf_op jit(solution)/shard_map/ppermute | solution.py:54
  31.1 11.2 %collective-permute-start.10 = (bf16[8,128,256]{2,1,0:T(8,128)(2,1)S(1)}, bf16[8,128,256]{2,1,0:T(8,128)(2,1)S(1)}, u32[]{:S(2)}, u32[]{:S(2)}) collective-permute-start(bf16[8,128,256]{2,1,0:T(8,128)(2,1)S(1)} %collective-permute-done.6.refs_0_), channel_id=1, source_target_pairs={{0,8},{1,3},{2,10},{3,5},{4,12},{5,7},{6,14},{7,1},{8,16},{9,11},{... | collective-permute-start | bytes 1572872 | tf_op jit(solution)/shard_map/ppermute | solution.py:54
  32.0 14.1 %collective-permute-start.11 = (bf16[8,128,256]{2,1,0:T(8,128)(2,1)S(1)}, bf16[8,128,256]{2,1,0:T(8,128)(2,1)S(1)}, u32[]{:S(2)}, u32[]{:S(2)}) collective-permute-start(bf16[8,128,256]{2,1,0:T(8,128)(2,1)S(1)} %collective-permute-done.7.refs_1_), channel_id=1, source_target_pairs={{0,24},{1,7},{2,26},{3,1},{4,28},{5,3},{6,30},{7,5},{8,0},{9,15},{... | collective-permute-start | bytes 1572872 | tf_op jit(solution)/shard_map/ppermute | solution.py:54
  33.9 14.4 %collective-permute-start.13 = (bf16[16,128,256]{2,1,0:T(8,128)(2,1)S(1)}, bf16[16,128,256]{2,1,0:T(8,128)(2,1)S(1)}, u32[]{:S(2)}, u32[]{:S(2)}) collective-permute-start(bf16[16,128,256]{2,1,0:T(8,128)(2,1)S(1)} %join.6.rest_1_), channel_id=1, source_target_pairs={{0,1},{1,0},{2,3},{3,2},{4,5},{5,4},{6,7},{7,6},{8,9},{9,8},{10,11... | collective-permute-start | bytes 3145736 | tf_op jit(solution)/shard_map/ppermute | solution.py:66
  38.5 9.9 %collective-permute-start.12 = (bf16[16,128,256]{2,1,0:T(8,128)(2,1)S(1)}, bf16[16,128,256]{2,1,0:T(8,128)(2,1)S(1)}, u32[]{:S(2)}, u32[]{:S(2)}) collective-permute-start(bf16[16,128,256]{2,1,0:T(8,128)(2,1)S(1)} %join.5.x.rest_0_), channel_id=1, source_target_pairs={{0,1},{1,0},{2,3},{3,2},{4,5},{5,4},{6,7},{7,6},{8,9},{9,8},{10,11... | collective-permute-start | bytes 3145736 | tf_op jit(solution)/shard_map/ppermute | solution.py:66
  40.8 7.6 %collective-permute-start.14 = (bf16[16,128,256]{2,1,0:T(8,128)(2,1)S(1)}, bf16[16,128,256]{2,1,0:T(8,128)(2,1)S(1)}, u32[]{:S(2)}, u32[]{:S(2)}) collective-permute-start(bf16[16,128,256]{2,1,0:T(8,128)(2,1)S(1)} %join.7.rest_2_), channel_id=1, source_target_pairs={{0,1},{1,0},{2,3},{3,2},{4,5},{5,4},{6,7},{7,6},{8,9},{9,8},{10,11... | collective-permute-start | bytes 3145736 | tf_op jit(solution)/shard_map/ppermute | solution.py:66
  42.3 5.2 %collective-permute-start.15 = (bf16[8,128,256]{2,1,0:T(8,128)(2,1)S(1)}, bf16[8,128,256]{2,1,0:T(8,128)(2,1)S(1)}, u32[]{:S(2)}, u32[]{:S(2)}) collective-permute-start(bf16[8,128,256]{2,1,0:T(8,128)(2,1)S(1)} %collective-permute-done.10.rest_3_), channel_id=1, source_target_pairs={{0,1},{1,0},{2,3},{3,2},{4,5},{5,4},{6,7},{7,6},{8,9},{9,8},{10,11... | collective-permute-start | bytes 1572872 | tf_op jit(solution)/shard_map/ppermute | solution.py:66
  55.3 2.9 %collective-permute-start.17 = (bf16[4096,128]{1,0:T(8,128)(2,1)S(1)}, bf16[4096,128]{1,0:T(8,128)(2,1)S(1)}, u32[]{:S(2)}, u32[]{:S(2)}) collective-permute-start(bf16[4096,128]{1,0:T(8,128)(2,1)S(1)} %get-tuple-element.83), channel_id=1, source_target_pairs={{0,1},{1,0},{2,3},{3,2},{4,5},{5,4},{6,7},{7,6},{8,9},{9,8},{10,11... | collective-permute-start | bytes 3145736 | tf_op jit(solution)/shard_map/ppermute | solution.py:66
  55.8 2.5 %collective-permute-start.18 = (f32[264,128]{1,0:T(8,128)S(1)}, f32[264,128]{1,0:T(8,128)S(1)}, u32[]{:S(2)}, u32[]{:S(2)}) collective-permute-start(f32[264,128]{1,0:T(8,128)S(1)} %slice_bitcast_fusion.2), channel_id=1, source_target_pairs={{0,1},{1,0},{2,3},{3,2},{4,5},{5,4},{6,7},{7,6},{8,9},{9,8},{10,11... | collective-permute-start | bytes 405512 | tf_op jit(solution)/shard_map/ppermute | solution.py:66
  58.6 11.3 %collective-permute-start.19 = (bf16[2,4096,128]{2,1,0:T(8,128)(2,1)S(1)}, bf16[2,4096,128]{2,1,0:T(8,128)(2,1)S(1)}, u32[]{:S(2)}, u32[]{:S(2)}) collective-permute-start(bf16[2,4096,128]{2,1,0:T(8,128)(2,1)S(1)} %slice.14), channel_id=1, source_target_pairs={{0,1},{1,0},{2,3},{3,2},{4,5},{5,4},{6,7},{7,6},{8,9},{9,8},{10,11... | collective-permute-start | bytes 6291464 | tf_op jit(solution)/shard_map/ppermute | solution.py:66
  59.0 10.8 %collective-permute-start.20 = (bf16[2320,128]{1,0:T(8,128)(2,1)S(1)}, bf16[2320,128]{1,0:T(8,128)(2,1)S(1)}, u32[]{:S(2)}, u32[]{:S(2)}) collective-permute-start(bf16[2320,128]{1,0:T(8,128)(2,1)S(1)} %get-tuple-element.59), channel_id=1, source_target_pairs={{0,8},{1,3},{2,10},{3,5},{4,12},{5,7},{6,14},{7,1},{8,16},{9,11},{... | collective-permute-start | bytes 1781768 | tf_op jit(solution)/shard_map/ppermute | solution.py:54
  60.2 9.7 %collective-permute-start.21 = (bf16[2320,128]{1,0:T(8,128)(2,1)S(1)}, bf16[2320,128]{1,0:T(8,128)(2,1)S(1)}, u32[]{:S(2)}, u32[]{:S(2)}) collective-permute-start(bf16[2320,128]{1,0:T(8,128)(2,1)S(1)} %get-tuple-element.60), channel_id=1, source_target_pairs={{0,24},{1,7},{2,26},{3,1},{4,28},{5,3},{6,30},{7,5},{8,0},{9,15},{... | collective-permute-start | bytes 1781768 | tf_op jit(solution)/shard_map/ppermute | solution.py:54
  61.7 8.1 %collective-permute-start.22 = (bf16[272,128]{1,0:T(8,128)(2,1)S(1)}, bf16[272,128]{1,0:T(8,128)(2,1)S(1)}, u32[]{:S(2)}, u32[]{:S(2)}) collective-permute-start(bf16[272,128]{1,0:T(8,128)(2,1)S(1)} %get-tuple-element.61), channel_id=1, source_target_pairs={{0,16},{1,5},{2,18},{3,7},{4,20},{5,1},{6,22},{7,3},{8,24},{9,13},... | collective-permute-start | bytes 208904 | tf_op jit(solution)/shard_map/ppermute | solution.py:54
  70.5 17.8 %collective-permute-start.23 = (bf16[4096,128]{1,0:T(8,128)(2,1)S(1)}, bf16[4096,128]{1,0:T(8,128)(2,1)S(1)}, u32[]{:S(2)}, u32[]{:S(2)}) collective-permute-start(bf16[4096,128]{1,0:T(8,128)(2,1)S(1)} %get-tuple-element.66), channel_id=1, source_target_pairs={{0,1},{1,0},{2,3},{3,2},{4,5},{5,4},{6,7},{7,6},{8,9},{9,8},{10,11... | collective-permute-start | bytes 3145736 | tf_op jit(solution)/shard_map/ppermute | solution.py:66
  72.5 16.2 %collective-permute-start.24 = (bf16[4096,128]{1,0:T(8,128)(2,1)S(1)}, bf16[4096,128]{1,0:T(8,128)(2,1)S(1)}, u32[]{:S(2)}, u32[]{:S(2)}) collective-permute-start(bf16[4096,128]{1,0:T(8,128)(2,1)S(1)} %get-tuple-element.67), channel_id=1, source_target_pairs={{0,8},{1,3},{2,10},{3,5},{4,12},{5,7},{6,14},{7,1},{8,16},{9,11},{... | collective-permute-start | bytes 3145736 | tf_op jit(solution)/shard_map/ppermute | solution.py:54
  73.7 15.1 %collective-permute-start.25 = (bf16[4096,128]{1,0:T(8,128)(2,1)S(1)}, bf16[4096,128]{1,0:T(8,128)(2,1)S(1)}, u32[]{:S(2)}, u32[]{:S(2)}) collective-permute-start(bf16[4096,128]{1,0:T(8,128)(2,1)S(1)} %get-tuple-element.68), channel_id=1, source_target_pairs={{0,24},{1,7},{2,26},{3,1},{4,28},{5,3},{6,30},{7,5},{8,0},{9,15},{... | collective-permute-start | bytes 3145736 | tf_op jit(solution)/shard_map/ppermute | solution.py:54
  89.4 7.2 %collective-permute-start.26 = (bf16[1056,128]{1,0:T(8,128)(2,1)S(1)}, bf16[1056,128]{1,0:T(8,128)(2,1)S(1)}, u32[]{:S(2)}, u32[]{:S(2)}) collective-permute-start(bf16[1056,128]{1,0:T(8,128)(2,1)S(1)} %get-tuple-element.72), channel_id=1, source_target_pairs={{0,4},{1,65},{2,6},{3,67},{4,0},{5,69},{6,2},{7,71},{8,12},{9,73},... | collective-permute-start | bytes 811016 | tf_op jit(solution)/shard_map/ppermute | solution.py:54
  91.1 8.3 %collective-permute-start.27 = (bf16[1056,128]{1,0:T(8,128)(2,1)S(1)}, bf16[1056,128]{1,0:T(8,128)(2,1)S(1)}, u32[]{:S(2)}, u32[]{:S(2)}) collective-permute-start(bf16[1056,128]{1,0:T(8,128)(2,1)S(1)} %get-tuple-element.73), channel_id=1, source_target_pairs={{0,2},{1,33},{2,4},{3,35},{4,6},{5,37},{6,0},{7,39},{8,10},{9,41},... | collective-permute-start | bytes 811016 | tf_op jit(solution)/shard_map/ppermute | solution.py:54
  91.5 7.9 %collective-permute-start.28 = (bf16[1056,128]{1,0:T(8,128)(2,1)S(1)}, bf16[1056,128]{1,0:T(8,128)(2,1)S(1)}, u32[]{:S(2)}, u32[]{:S(2)}) collective-permute-start(bf16[1056,128]{1,0:T(8,128)(2,1)S(1)} %get-tuple-element.74), channel_id=1, source_target_pairs={{0,6},{1,97},{2,0},{3,99},{4,2},{5,101},{6,4},{7,103},{8,14},{9,10... | collective-permute-start | bytes 811016 | tf_op jit(solution)/shard_map/ppermute | solution.py:54
  99.6 5.1 %collective-permute-start.29 = (bf16[384,128]{1,0:T(8,128)(2,1)S(1)}, bf16[384,128]{1,0:T(8,128)(2,1)S(1)}, u32[]{:S(2)}, u32[]{:S(2)}) collective-permute-start(bf16[384,128]{1,0:T(8,128)(2,1)S(1)} %get-tuple-element.76), channel_id=1, source_target_pairs={{0,64},{1,17},{2,66},{3,19},{4,68},{5,21},{6,70},{7,23},{8,72},{9,... | collective-permute-start | bytes 294920 | tf_op jit(solution)/shard_map/ppermute | solution.py:54
  100.6 5.1 %collective-permute-start.30 = (bf16[384,128]{1,0:T(8,128)(2,1)S(1)}, bf16[384,128]{1,0:T(8,128)(2,1)S(1)}, u32[]{:S(2)}, u32[]{:S(2)}) collective-permute-start(bf16[384,128]{1,0:T(8,128)(2,1)S(1)} %get-tuple-element.77), channel_id=1, source_target_pairs={{0,32},{1,9},{2,34},{3,11},{4,36},{5,13},{6,38},{7,15},{8,40},{9,1... | collective-permute-start | bytes 294920 | tf_op jit(solution)/shard_map/ppermute | solution.py:54
  102.5 3.5 %collective-permute-start.31 = (bf16[384,128]{1,0:T(8,128)(2,1)S(1)}, bf16[384,128]{1,0:T(8,128)(2,1)S(1)}, u32[]{:S(2)}, u32[]{:S(2)}) collective-permute-start(bf16[384,128]{1,0:T(8,128)(2,1)S(1)} %get-tuple-element.78), channel_id=1, source_target_pairs={{0,96},{1,25},{2,98},{3,27},{4,100},{5,29},{6,102},{7,31},{8,104},... | collective-permute-start | bytes 294920 | tf_op jit(solution)/shard_map/ppermute | solution.py:54
  106.0 4.6 %collective-permute-start.32 = (f32[264,128]{1,0:T(8,128)S(1)}, f32[264,128]{1,0:T(8,128)S(1)}, u32[]{:S(2)}, u32[]{:S(2)}) collective-permute-start(f32[264,128]{1,0:T(8,128)S(1)} %extra_half.1.own), channel_id=1, source_target_pairs={{0,1},{1,0},{2,3},{3,2},{4,5},{5,4},{6,7},{7,6},{8,9},{9,8},{10,11... | collective-permute-start | bytes 405512 | tf_op jit(solution)/shard_map/ppermute | solution.py:66
  (6 other events, 162.0 us)
